TPU v7x, 32 devices: a whole 2x2x4 slice. The times are simulated.
32 devices in a mesh: fsdp: 8 (over y, x, core), tp: 4 (over z).
Axes of the slice: x: 2, y: 2, z: 4, core: 2. Of those that a mesh axis runs over, the one named last changes fastest.
Arguments:
- tokens: bfloat16 [8, 1024, 2048], P('fsdp', 'tp'), may hold values from -6 to 6
- layer_norm_gain: float32 [2048], replicated, may hold values from 0.25 to 1.75
- layer_norm_bias: float32 [2048], replicated, may hold values from -3 to 3
- w_qkv: bfloat16 [2048, 3, 2048], P('fsdp', None, 'tp'), may hold values from -0.125 to 0.125
- w_out: bfloat16 [2048, 2048], P('tp', 'fsdp'), may hold values from -0.75 to 0.75
- w_up: bfloat16 [2048, 8192], P('fsdp', 'tp'), may hold values from -0.125 to 0.125
- w_down: bfloat16 [8192, 2048], P('tp', 'fsdp'), may hold values from -0.0625 to 0.0625
- cotangent: bfloat16 [8, 1024, 2048], P('fsdp', 'tp'), may hold values from -6 to 6
Outputs:
- output: bfloat16 [8, 1024, 2048], P('fsdp', 'tp')
- in_grad: float32 [8, 1024, 2048], P('fsdp', 'tp')
- gain_grad: float32 [2048], P('fsdp')
- bias_grad: float32 [2048], P('fsdp')
- qkv_grad: float32 [2048, 3, 2048], P('fsdp', None, 'tp')
- out_grad: float32 [2048, 2048], P('tp', 'fsdp')
- up_grad: float32 [2048, 8192], P('fsdp', 'tp')
- down_grad: float32 [8192, 2048], P('tp', 'fsdp')
All inputs are finite; a program needn't handle non-finite values.
Results may differ from a plain program's by a relative error of at most 0.012.
Values may be sent and summed in bfloat16 or wider, within the bound.
No kernel may reach another device: no remote copies, remote signals or barrier semaphores. Data moves between devices by JAX's collectives and lax.ppermute only.
A program may use at most 256 MiB of HBM per device.

v0:
```python
import functools

import jax
import jax.numpy as jnp
from jax import lax
from jax.experimental import pallas as pl
from jax.experimental.pallas import tpu as pltpu
from jax.sharding import PartitionSpec as P

HEADS = 32
HEAD_DIM = 64
ROT = 32
PAIR = 2 * HEAD_DIM
BF = jnp.bfloat16
F32 = jnp.float32

NN = (((1,), (0,)), ((), ()))
NT = (((1,), (1,)), ((), ()))
TN = (((0,), (0,)), ((), ()))


def dot(a, b, dims):
    return lax.dot_general(a, b, dims, preferred_element_type=F32)


def params(mebibytes=14):
    return pltpu.CompilerParams(vmem_limit_bytes=mebibytes * 1024 * 1024)


def cost(flops, arrays, shapes, transcendentals=0):
    moved = sum(a.size * a.dtype.itemsize for a in list(arrays) + list(shapes))
    return pl.CostEstimate(flops=flops // 8, bytes_accessed=moved // 8, transcendentals=transcendentals // 8)


def angle_tables(length):
    half_rot = ROT // 2
    position = jnp.arange(length, dtype=jnp.int32).astype(F32)[:, None]
    channel = jnp.arange(PAIR, dtype=jnp.int32) % HEAD_DIM
    exponent = (2 * (channel % half_rot)).astype(F32) / ROT
    angles = position * (10000.0 ** (-exponent))[None, :]
    low = (channel < half_rot)[None, :]
    inside = (channel < ROT)[None, :]
    cosine = jnp.where(inside, jnp.cos(angles), 1.0)
    sine = jnp.sin(angles)
    return (
        cosine,
        jnp.where(inside & ~low, sine, 0.0),
        jnp.where(low, -sine, 0.0),
    )


def turn(z, c, a, b):
    return z * c + pltpu.roll(z, ROT // 2, 1) * a + pltpu.roll(z, PAIR - ROT // 2, 1) * b


def turn_back(z, c, a, b):
    return z * c - pltpu.roll(z, ROT // 2, 1) * a - pltpu.roll(z, PAIR - ROT // 2, 1) * b


def after(value, *earlier):
    return lax.optimization_barrier((value, *earlier))[0]


def fence(*values):
    return lax.optimization_barrier(values)


def place_order(count):
    return list(range(0, count, 2)) + list(range(1, count, 2))


def enter_kernel(count, me_ref, x_ref, cot_ref, gain_ref, bias_ref, normed_ref, cot_out_ref, row_ref):
    x = x_ref[...].astype(F32)
    centered = x - jnp.mean(x, axis=-1, keepdims=True)
    inverse = lax.rsqrt(jnp.mean(centered * centered, axis=-1, keepdims=True) + 1e-05)
    row_ref[...] = (centered * inverse * gain_ref[...] + bias_ref[...]).astype(BF)
    size = x.shape[1] // count
    for place, r in enumerate(place_order(count)):
        at = pl.ds(pl.multiple_of((me_ref[0] ^ r) * size, size), size)
        to = slice(place * size, (place + 1) * size)
        normed_ref[:, to] = row_ref[:, at]
        cot_out_ref[:, to] = cot_ref[:, at]


def enter(x, cot, gain, bias, me, count):
    shape = jax.ShapeDtypeStruct(x.shape, BF)
    whole = pl.BlockSpec(x.shape, lambda j, me: (0, 0))
    line = pl.BlockSpec((1, x.shape[1]), lambda j, me: (0, 0))
    return pl.pallas_call(
        functools.partial(enter_kernel, count),
        grid_spec=pltpu.PrefetchScalarGridSpec(
            num_scalar_prefetch=1,
            grid=(1,),
            in_specs=[whole, whole, line, line],
            out_specs=[whole, whole],
            scratch_shapes=[pltpu.VMEM(x.shape, BF)],
        ),
        out_shape=[shape, shape],
        compiler_params=params(),
        cost_estimate=cost(12 * x.size, [x, cot], [shape, shape]),
        name="enter",
    )(me, x, cot, gain[None], bias[None])


def leave_output_kernel(count, me_ref, x_ref, own_ref, in_ref, out_ref):
    size = x_ref.shape[1] // count
    for place, r in enumerate(place_order(count)):
        at = pl.ds(pl.multiple_of((me_ref[0] ^ r) * size, size), size)
        here = slice(place * size, (place + 1) * size)
        total = own_ref[:, here].astype(F32) + in_ref[:, here].astype(F32)
        out_ref[:, at] = (x_ref[:, at].astype(F32) + total).astype(BF)


def leave_output(x, part, arrived, me, count):
    whole = pl.BlockSpec(x.shape, lambda j, me: (0, 0))
    shape = jax.ShapeDtypeStruct(x.shape, BF)
    return pl.pallas_call(
        functools.partial(leave_output_kernel, count),
        grid_spec=pltpu.PrefetchScalarGridSpec(
            num_scalar_prefetch=1, grid=(1,), in_specs=[whole] * 3, out_specs=whole
        ),
        out_shape=shape,
        compiler_params=params(),
        cost_estimate=cost(3 * x.size, [x, x, arrived], [shape]),
        name="leave_output",
    )(me, x, part, arrived)


def leave_grad_kernel(count, me_ref, x_ref, cot_ref, own_ref, in_ref, gain_ref, out_ref, stats_ref, d_ref, xhat_ref):
    size = x_ref.shape[1] // count
    for place, r in enumerate(place_order(count)):
        at = pl.ds(pl.multiple_of((me_ref[0] ^ r) * size, size), size)
        here = slice(place * size, (place + 1) * size)
        d_ref[:, at] = own_ref[:, here].astype(F32) + in_ref[:, here].astype(F32)
    x = x_ref[...].astype(F32)
    centered = x - jnp.mean(x, axis=-1, keepdims=True)
    inverse = lax.rsqrt(jnp.mean(centered * centered, axis=-1, keepdims=True) + 1e-05)
    xhat = centered * inverse
    d = d_ref[...]
    xhat_ref[...] = xhat
    for place, r in enumerate(place_order(count)):
        at = pl.ds(pl.multiple_of((me_ref[0] ^ r) * size, size), size)
        here = slice(place * size, (place + 1) * size)
        stats_ref[0:1, here] = jnp.sum(d_ref[:, at] * xhat_ref[:, at], axis=0, keepdims=True)
        stats_ref[1:2, here] = jnp.sum(d_ref[:, at], axis=0, keepdims=True)
    d_hat = d * gain_ref[...]
    out_ref[...] = cot_ref[...].astype(F32) + inverse * (
        d_hat
        - jnp.mean(d_hat, axis=-1, keepdims=True)
        - xhat * jnp.mean(d_hat * xhat, axis=-1, keepdims=True)
    )


def leave_grad(x, cot, part, arrived, gain, me, count):
    whole = pl.BlockSpec(x.shape, lambda j, me: (0, 0))
    line = pl.BlockSpec((1, x.shape[1]), lambda j, me: (0, 0))
    two = pl.BlockSpec((2, x.shape[1]), lambda j, me: (0, 0))
    shapes = [jax.ShapeDtypeStruct(x.shape, F32), jax.ShapeDtypeStruct((2, x.shape[1]), F32)]
    return pl.pallas_call(
        functools.partial(leave_grad_kernel, count),
        grid_spec=pltpu.PrefetchScalarGridSpec(
            num_scalar_prefetch=1,
            grid=(1,),
            in_specs=[whole] * 4 + [line],
            out_specs=[whole, two],
            scratch_shapes=[pltpu.VMEM(x.shape, F32)] * 2,
        ),
        out_shape=shapes,
        compiler_params=params(),
        cost_estimate=cost(20 * x.size, [x, cot, x, arrived], shapes),
        name="leave_grad",
    )(me, x, cot, part, arrived, gain[None])


def ring_rows(me_ref, a, count, rows):
    place = lax.rem(me_ref[0] - a + count, count)
    return pl.ds(pl.multiple_of(place * rows, rows), rows)


def attend_forward_kernel(block, count, me_ref, q_in, k_in, v_in, c_ref, a_ref, b_ref, q_ref, k_ref, v_ref, o_ref, lse_ref, o_acc):
    length = q_in.shape[0]
    rows_each = length // count
    for n in range(count):
        src = ring_rows(me_ref, n, count, rows_each)
        dst = slice(n * rows_each, (n + 1) * rows_each)
        c, a, b = c_ref[dst, :], a_ref[dst, :], b_ref[dst, :]
        q_ref[dst, :] = (turn(q_in[src, :], c, a, b) * HEAD_DIM**-0.5).astype(BF)
        k_ref[dst, :] = turn(k_in[src, :], c, a, b).astype(BF)
        v_ref[dst, :] = v_in[src, :].astype(BF)
    k = k_ref[...]
    q_t = q_ref[...].T
    v_t = v_ref[...].T
    head_row = lax.broadcasted_iota(jnp.int32, (PAIR, 1), 0) // HEAD_DIM
    key_at = lax.broadcasted_iota(jnp.int32, (block, block), 0)
    query_at = lax.broadcasted_iota(jnp.int32, (block, block), 1)
    allowed = key_at <= query_at

    def scores(j, h):
        cols, done = slice(j * block, (j + 1) * block), j * block
        q_h = jnp.where(head_row == h, q_t[:, cols], jnp.zeros((), BF))
        return dot(k[cols], q_h, NN), dot(k[:done], q_h, NN) if j else None

    def soften(j, h, s_diag, s_past):
        cols = slice(j * block, (j + 1) * block)
        s_diag = jnp.where(allowed, s_diag, -1e30)
        largest = jnp.max(s_diag, axis=0, keepdims=True)
        if j:
            largest = jnp.maximum(largest, jnp.max(s_past, axis=0, keepdims=True))
        p_diag = jnp.exp(s_diag - largest)
        total = jnp.sum(p_diag, axis=0, keepdims=True)
        p_past = None
        if j:
            p_past = jnp.exp(s_past - largest)
            total = total + jnp.sum(p_past, axis=0, keepdims=True)
            p_past = p_past.astype(BF)
        lse_ref[0, h : h + 1, cols] = largest + jnp.log(total)
        return p_diag.astype(BF), p_past, total

    def weigh(j, h, p_diag, p_past, total):
        rows = slice(h * HEAD_DIM, (h + 1) * HEAD_DIM)
        out = dot(v_t[rows, j * block : (j + 1) * block], p_diag, NN)
        if j:
            out = out + dot(v_t[rows, : j * block], p_past, NN)
        return out / total

    items = [(j, h) for j in range(length // block) for h in range(2)]
    held, outs = {}, []
    for n in range(len(items) + 2):
        if n < len(items):
            held[n] = scores(*items[n])
        if 0 <= n - 1 < len(items):
            held[n - 1] = soften(*items[n - 1], *held[n - 1])
        if 0 <= n - 2:
            j, h = items[n - 2]
            outs.append(weigh(j, h, *held.pop(n - 2)))
            if h == 1:
                o_acc[j * block : (j + 1) * block, :] = jnp.concatenate(outs, axis=0).T.astype(BF)
                outs = []
    for n in range(count):
        o_ref[ring_rows(me_ref, n, count, rows_each), :] = o_acc[n * rows_each : (n + 1) * rows_each, :]


def attend_forward(qkv, tables, heads_here, me, count):
    length = qkv.shape[0]
    pairs = heads_here // 2
    width = heads_here * HEAD_DIM
    block = min(256, length)

    def part(n):
        return pl.BlockSpec((length, PAIR), lambda p, me: (0, n * pairs + p))

    head = pl.BlockSpec((length, PAIR), lambda p, me: (0, p))
    table = pl.BlockSpec((length, PAIR), lambda p, me: (0, 0))
    shapes = [jax.ShapeDtypeStruct((length, width), BF)] * 4 + [
        jax.ShapeDtypeStruct((pairs, 8, length), F32)
    ]
    return pl.pallas_call(
        functools.partial(attend_forward_kernel, block, count),
        grid_spec=pltpu.PrefetchScalarGridSpec(
            num_scalar_prefetch=1,
            grid=(pairs,),
            in_specs=[part(0), part(1), part(2), table, table, table],
            out_specs=[head] * 4 + [pl.BlockSpec((1, 8, length), lambda p, me: (p, 0, 0))],
            scratch_shapes=[pltpu.VMEM((length, PAIR), BF)],
        ),
        out_shape=shapes,
        compiler_params=params(),
        cost_estimate=cost(16 * length * length * width, [qkv, *tables], shapes, length * length * heads_here // 2),
        name="attend_forward",
    )(me, qkv, qkv, qkv, *tables)


def attend_backward_kernel(block, count, me_ref, q_ref, k_ref, v_ref, g_in, lse_ref, c_ref, a_ref, b_ref, dq_ref, dk_ref, dv_ref, g_ref, dq_acc, dk_acc, dv_acc):
    length = q_ref.shape[0]
    rows_each = length // count
    for n in range(count):
        g_ref[n * rows_each : (n + 1) * rows_each, :] = g_in[ring_rows(me_ref, n, count, rows_each), :]
    q, k, v, g = q_ref[...], k_ref[...], v_ref[...], g_ref[...]
    q_t, g_t, k_t = q.T, g.T, k.T
    head_row = lax.broadcasted_iota(jnp.int32, (PAIR, 1), 0) // HEAD_DIM
    head_col = lax.broadcasted_iota(jnp.int32, (1, PAIR), 1) // HEAD_DIM
    key_at = lax.broadcasted_iota(jnp.int32, (block, block), 0)
    query_at = lax.broadcasted_iota(jnp.int32, (block, block), 1)
    allowed = key_at <= query_at
    zero = jnp.zeros((), BF)

    def products(j, h):
        cols, done = slice(j * block, (j + 1) * block), j * block
        q_th = jnp.where(head_row == h, q_t[:, cols], zero)
        g_th = jnp.where(head_row == h, g_t[:, cols], zero)
        past = (dot(k[:done], q_th, NN), dot(v[:done], g_th, NN)) if j else (None, None)
        return dot(k[cols], q_th, NN), dot(v[cols], g_th, NN), *past

    def d_scores(j, h, s_diag, dp_diag, s_past, dp_past):
        lse = lse_ref[0, h : h + 1, j * block : (j + 1) * block]
        p_diag = jnp.where(allowed, jnp.exp(s_diag - lse), 0.0)
        pd_diag = p_diag * dp_diag
        delta = jnp.sum(pd_diag, axis=0, keepdims=True)
        p_past = ds_past = None
        if j:
            p_past = jnp.exp(s_past - lse)
            pd_past = p_past * dp_past
            delta = delta + jnp.sum(pd_past, axis=0, keepdims=True)
            ds_past = (pd_past - p_past * delta).astype(BF)
            p_past = p_past.astype(BF)
        return p_diag.astype(BF), (pd_diag - p_diag * delta).astype(BF), p_past, ds_past

    def sums(j, h, p_diag, ds_diag, p_past, ds_past):
        cols, done = slice(j * block, (j + 1) * block), j * block
        rows = slice(h * HEAD_DIM, (h + 1) * HEAD_DIM)
        q_h = jnp.where(head_col == h, q[cols], zero)
        g_h = jnp.where(head_col == h, g[cols], zero)
        dq = dot(k_t[rows, cols], ds_diag, NN)
        dk, dv = dot(ds_diag, q_h, NN), dot(p_diag, g_h, NN)
        dk_acc[cols, :] = dk_acc[cols, :] + dk if h else dk
        dv_acc[cols, :] = dv_acc[cols, :] + dv if h else dv
        if j:
            dq = dq + dot(k_t[rows, :done], ds_past, NN)
            dk_acc[:done, :] += dot(ds_past, q_h, NN)
            dv_acc[:done, :] += dot(p_past, g_h, NN)
        return dq

    items = [(j, h) for j in range(length // block) for h in range(2)]
    held, dqs = {}, []
    for n in range(len(items) + 2):
        if n < len(items):
            held[n] = products(*items[n])
        if 0 <= n - 1 < len(items):
            held[n - 1] = d_scores(*items[n - 1], *held[n - 1])
        if 0 <= n - 2:
            j, h = items[n - 2]
            dqs.append(sums(j, h, *held.pop(n - 2)))
            if h == 1:
                dq_acc[j * block : (j + 1) * block, :] = jnp.concatenate(dqs, axis=0).T * HEAD_DIM**-0.5
                dqs = []
    for n in range(count):
        src = slice(n * rows_each, (n + 1) * rows_each)
        dst = ring_rows(me_ref, n, count, rows_each)
        c, a, b = c_ref[src, :], a_ref[src, :], b_ref[src, :]
        dq_ref[dst, :] = turn_back(dq_acc[src, :], c, a, b).astype(BF)
        dk_ref[dst, :] = turn_back(dk_acc[src, :], c, a, b).astype(BF)
        dv_ref[dst, :] = dv_acc[src, :].astype(BF)


def attend_backward(q, k, v, g, g_at, lse, tables, me, count):
    length, width = q.shape
    pairs = width // PAIR
    block = min(256, length)
    head = pl.BlockSpec((length, PAIR), lambda p, me: (0, p))
    grad = pl.BlockSpec((length, PAIR), lambda p, me: (0, g_at // PAIR + p))
    table = pl.BlockSpec((length, PAIR), lambda p, me: (0, 0))
    shapes = [jax.ShapeDtypeStruct((length, width), BF)] * 3
    return pl.pallas_call(
        functools.partial(attend_backward_kernel, block, count),
        grid_spec=pltpu.PrefetchScalarGridSpec(
            num_scalar_prefetch=1,
            grid=(pairs,),
            in_specs=[head] * 3 + [grad, pl.BlockSpec((1, 8, length), lambda p, me: (p, 0, 0)), table, table, table],
            out_specs=[head] * 3,
            scratch_shapes=[pltpu.VMEM((length, PAIR), BF)] + [pltpu.VMEM((length, PAIR), F32)] * 3,
        ),
        out_shape=shapes,
        compiler_params=params(),
        cost_estimate=cost(40 * length * length * width, [q, k, v, q, *tables], shapes, length * length * pairs),
        name="attend_backward",
    )(me, q, k, v, g, lse, *tables)


GELU_C = 0.7978845608028654
GELU_A = 0.044715


def tile_of(*sizes):
    tile = 512
    while any(size % tile for size in sizes):
        tile //= 2
    return tile


def resident(shape):
    return pl.BlockSpec(shape, lambda j: (0, 0), pipeline_mode=pl.Buffered(1))


def product(body, operands, specs, out_specs, shapes, steps, flops, name, transcendentals=0, aliases=None, scratch=(), mebibytes=14):
    return pl.pallas_call(
        body,
        grid=(steps,),
        in_specs=specs,
        out_specs=out_specs,
        out_shape=shapes,
        scratch_shapes=list(scratch),
        input_output_aliases=aliases or {},
        compiler_params=params(mebibytes),
        cost_estimate=cost(flops, operands, shapes if isinstance(shapes, list) else [shapes], transcendentals),
        name=name,
    )(*operands)


def join_rows(parts, whole_ref):
    @pl.when(pl.program_id(0) == 0)
    def _():
        rows = parts[0].shape[0]
        for n, part in enumerate(parts):
            whole_ref[n * rows : (n + 1) * rows, :] = part[...]


def pair_dot(x_ref, mine_ref, other_ref):
    half = mine_ref.shape[0]
    return dot(x_ref[:, :half], mine_ref[...], NN) + dot(x_ref[:, half:], other_ref[...], NN)


def qkv_kernel(count, *refs):
    mine_ref, other_ref, out_ref, x_ref = refs[count:]
    join_rows(refs[:count], x_ref)
    out_ref[...] = pair_dot(x_ref, mine_ref.at[0], other_ref.at[0])


def up_kernel(count, *refs):
    mine_ref, other_ref, hidden_ref, slope_ref, x_ref = refs[count:]
    join_rows(refs[:count], x_ref)
    u = pair_dot(x_ref, mine_ref, other_ref)
    square = u * u
    t = jnp.tanh(u * (GELU_C + (GELU_C * GELU_A) * square))
    half = 0.5 + 0.5 * t
    hidden_ref[...] = (u * half).astype(BF)
    slope_ref[...] = (half + u * (0.5 - 0.5 * (t * t)) * (GELU_C + (3.0 * GELU_C * GELU_A) * square)).astype(BF)


def forward_product(body, xs, w, specs, columns, tile, out_types, name, transcendentals=0):
    rows, depth = xs[0].shape[0] * len(xs), xs[0].shape[1]
    outs = [jax.ShapeDtypeStruct((rows, columns), t) for t in out_types]
    return product(
        functools.partial(body, len(xs)),
        [*xs, *w],
        [resident(x.shape) for x in xs] + specs,
        [pl.BlockSpec((rows, tile), lambda j: (0, j)) for _ in outs],
        outs,
        columns // tile,
        2 * rows * depth * columns,
        name,
        transcendentals,
        scratch=[pltpu.VMEM((rows, depth), BF)],
        mebibytes=26,
    )


def qkv_project(xs, w):
    parts, half, part = w[0].shape
    spec = pl.BlockSpec((1, half, part), lambda j: (j, 0, 0))
    return forward_product(qkv_kernel, xs, w, [spec] * 2, parts * part, part, [F32], "qkv")[0]


def up_project(xs, w):
    half, columns = w[0].shape
    tile = tile_of(columns)
    spec = pl.BlockSpec((half, tile), lambda j: (0, j))
    return forward_product(up_kernel, xs, w, [spec] * 2, columns, tile, [BF, BF], "up", columns)


def first_or_second(steps, first, second):
    @pl.when(pl.program_id(0) < steps)
    def _():
        first()

    @pl.when(pl.program_id(0) >= steps)
    def _():
        second()


def branch_kernel(hidden_ref, att_ref, w_ref, *rest):
    ff = hidden_ref.shape[1]
    rest[-1][...] = (dot(hidden_ref[...], w_ref[:ff, :], NN) + dot(att_ref[...], w_ref[ff:, :], NN)).astype(BF)


def branch_project(hidden, attended, w, place, partial_out):
    rows = hidden.shape[0]
    depth, half = w.shape
    tile = tile_of(half)
    steps = half // tile
    operands = [hidden, attended, w]
    specs = [resident(hidden.shape), resident(attended.shape), pl.BlockSpec((depth, tile), lambda j: (0, j))]
    aliases = None
    if partial_out is not None:
        aliases = {len(operands): 0}
        operands.append(partial_out)
        specs.append(pl.BlockSpec(memory_space=pl.ANY))
    return product(
        branch_kernel,
        operands,
        specs,
        pl.BlockSpec((rows, tile), lambda j: (0, place * steps + j)),
        jax.ShapeDtypeStruct((rows, 2 * half), BF),
        steps,
        2 * rows * half * depth,
        "branch",
        aliases=aliases,
        mebibytes=20,
    )


def d_branch_kernel(steps, count, *refs):
    slope_ref, mine_ref, other_ref = refs[count : count + 3]
    out_ref, cot_ref = refs[-2:]
    join_rows(refs[:count], cot_ref)
    half = mine_ref.shape[1]
    total = dot(cot_ref[:, :half], mine_ref[...], NT) + dot(cot_ref[:, half:], other_ref[...], NT)

    def up_part():
        out_ref[...] = (total * slope_ref[...].astype(F32)).astype(BF)

    def att_part():
        out_ref[...] = total.astype(BF)

    first_or_second(steps, up_part, att_part)


def d_branch_project(cots, place, slope, w, partial_out):
    rows = cots[0].shape[0] * len(cots)
    columns, half = w[0].shape
    tile = tile_of(columns, slope.shape[1])
    steps = slope.shape[1] // tile
    operands = [*cots, slope, *w]
    specs = [resident(c.shape) for c in cots] + [
        pl.BlockSpec((rows, tile), lambda j: (place, jnp.minimum(j, steps - 1))),
        pl.BlockSpec((tile, half), lambda j: (j, 0)),
        pl.BlockSpec((tile, half), lambda j: (j, 0)),
    ]
    aliases = None
    if partial_out is not None:
        aliases = {len(operands): 0}
        operands.append(partial_out)
        specs.append(pl.BlockSpec(memory_space=pl.ANY))
    return product(
        functools.partial(d_branch_kernel, steps, len(cots)),
        operands,
        specs,
        pl.BlockSpec((rows, tile), lambda j: (place, j)),
        jax.ShapeDtypeStruct((slope.shape[0], columns), BF),
        columns // tile,
        4 * rows * half * columns,
        "d_branch",
        aliases=aliases,
        scratch=[pltpu.VMEM((rows, 2 * half), BF)],
    )


def d_normed_kernel(steps, du_ref, dq_ref, dk_ref, dv_ref, um_ref, uo_ref, qm_ref, qo_ref, out_ref):
    def total(wu_ref, wq_ref):
        value = dot(du_ref[...], wu_ref[...], NT)
        for n, ref in enumerate((dq_ref, dk_ref, dv_ref)):
            value = value + dot(ref[...], wq_ref[n], NT)
        out_ref[...] = value.astype(BF)

    first_or_second(steps, lambda: total(um_ref, qm_ref), lambda: total(uo_ref, qo_ref))


def d_normed_project(d_branch, dqkv, w_up, w_qkv):
    rows = d_branch.shape[0]
    half, up_columns = w_up[0].shape
    parts, _, part = w_qkv[0].shape
    tile = min(256, tile_of(half))
    steps = half // tile

    def early(j):
        return jnp.minimum(j, steps - 1)

    def late(j):
        return jnp.maximum(j - steps, 0)

    return product(
        functools.partial(d_normed_kernel, steps),
        [d_branch, *dqkv, *w_up, *w_qkv],
        [resident((rows, up_columns))] + [resident(d.shape) for d in dqkv]
        + [pl.BlockSpec((tile, up_columns), lambda j: (early(j), 0)), pl.BlockSpec((tile, up_columns), lambda j: (late(j), 0))]
        + [pl.BlockSpec((parts, tile, part), lambda j: (0, early(j), 0)), pl.BlockSpec((parts, tile, part), lambda j: (0, late(j), 0))],
        pl.BlockSpec((rows, tile), lambda j: (0, j)),
        jax.ShapeDtypeStruct((rows, 2 * half), BF),
        2 * steps,
        4 * rows * half * (up_columns + parts * part),
        "d_normed",
        mebibytes=18,
    )


def weight_grad_kernel(lefts, rights, with_sum, *refs):
    xs, ys, rest = refs[:lefts], refs[lefts : lefts + rights], refs[lefts + rights :]
    arrived, outs = (rest[0], rest[1:]) if with_sum else (None, rest)
    x_t = jnp.concatenate([x[...] for x in xs], axis=0).T
    start = 0
    for y in ys:
        stop = start + y.shape[1]
        total = dot(x_t, y[...], NN)
        if with_sum:
            total = total + arrived[:, start:stop].astype(F32)
        total = total.astype(BF)
        if len(outs) == 1:
            outs[0][:, start:stop] = total
        else:
            put_block(outs, total, start, stop)
        start = stop


def put_block(outs, total, start, stop):
    at = pl.program_id(0)
    rows = total.shape[0]
    place, n = 0, 0
    while n < len(outs):
        whole = outs[n].shape[0] == rows

        @pl.when(at == place)
        def _(n=n, whole=whole):
            if whole:
                outs[n][:, start:stop] = total
            else:
                outs[n][:, start:stop] = total[: rows // 2]
                outs[n + 1][:, start:stop] = total[rows // 2 :]

        place, n = place + 1, n + (1 if whole else 2)


def weight_grad(xs, rights, widths, half, arrived, name):
    tokens = sum(x.shape[0] for x in xs)
    rows = xs[0].shape[1] // 2
    columns = sum(widths)
    chips = lax.axis_size("fsdp") // 2
    tile = min(256, rows) if arrived is None else rows // chips
    first = half * (rows // tile)
    out = pl.BlockSpec((tile, columns), lambda j: (j, 0))
    extras = [] if arrived is None else [arrived]
    if arrived is None:
        outs, shapes = out, jax.ShapeDtypeStruct((rows, columns), BF)
    else:
        sizes = [tile] * chips if chips != 4 else [tile] * 3 + [tile // 2] * 2
        outs = [pl.BlockSpec((size, columns), lambda j: (0, 0), pipeline_mode=pl.Buffered(1)) for size in sizes]
        shapes = [jax.ShapeDtypeStruct((size, columns), BF) for size in sizes]
    return product(
        functools.partial(weight_grad_kernel, len(xs), len(rights), bool(extras)),
        [*xs, *rights, *extras],
        [pl.BlockSpec((x.shape[0], tile), lambda j: (0, first + j)) for x in xs]
        + [resident((tokens, n)) for n in widths]
        + [out for _ in extras],
        outs,
        shapes,
        rows // tile,
        2 * tokens * rows * columns,
        name,
        mebibytes=14 if arrived is None else 18,
    )


def flip(array, bit):
    count = lax.axis_size("fsdp")
    return lax.ppermute(array, "fsdp", [(s, s ^ bit) for s in range(count)])


def chip_bits():
    bits, bit = [], 2
    while bit < lax.axis_size("fsdp"):
        bits.append(bit)
        bit *= 2
    return bits


def split(array, axis):
    size = array.shape[axis] // 2
    return lax.slice_in_dim(array, 0, size, axis=axis), lax.slice_in_dim(array, size, 2 * size, axis=axis)


def gather_near(own):
    got = {0: own}
    for bit in chip_bits()[:2]:
        got[bit] = flip(own, bit)
    return got


def far_halves(got, axis):
    bits = chip_bits()
    if len(bits) != 2:
        return ()
    return split(got[bits[1]], axis)[0], split(got[bits[0]], axis)[1]


def gather_far(got, axis, halves=()):
    bits = chip_bits()
    if len(bits) == 2:
        x, y = bits
        first, second = halves or far_halves(got, axis)
        return {**got, x | y: jnp.concatenate([flip(first, x), flip(second, y)], axis=axis)}
    got = {0: got[0]}
    for bit in bits:
        for r in list(got):
            got[r | bit] = flip(got[r], bit)
    return got


def gather_direct(own):
    return {0: own, **{r: flip(own, r) for r in range(2, lax.axis_size("fsdp"), 2)}}


def in_place_order(got, axis):
    return jnp.concatenate([got[r] for r in sorted(got)], axis=axis)


def add(a, b):
    return a.astype(F32) + b.astype(F32)


def scatter_first(blocks):
    bits = chip_bits()
    if len(bits) == 2:
        x, y = bits
        own, to_x, to_y, first, second = blocks
        return {0: own, x: to_x, y: to_y}, (flip(first, x), flip(second, y))
    return {2 * p: block for p, block in enumerate(blocks)}, ()


def merge_kernel(x_ref, y_ref, via_x_ref, via_y_ref, to_x_ref, to_y_ref):
    size = via_x_ref.shape[0]
    to_x_ref[:size, :] = x_ref[:size, :]
    to_x_ref[size:, :] = add(x_ref[size:, :], via_y_ref[...]).astype(BF)
    to_y_ref[:size, :] = add(y_ref[:size, :], via_x_ref[...]).astype(BF)
    to_y_ref[size:, :] = y_ref[size:, :]


def scatter_merge(held, arrived):
    bits = chip_bits()
    if not arrived:
        return held
    x, y = bits
    shapes = [jax.ShapeDtypeStruct(held[x].shape, BF)] * 2
    to_x, to_y = pl.pallas_call(
        merge_kernel,
        out_shape=shapes,
        compiler_params=params(),
        cost_estimate=cost(held[x].size, [held[x], held[y], *arrived], shapes),
        name="merge",
    )(held[x], held[y], *arrived)
    return {0: held[0], x: to_x, y: to_y}


def scatter_second(held):
    bits = chip_bits()
    if len(bits) == 2:
        return tuple(flip(part, r) if r else part for r, part in held.items())
    held = dict(held)
    for bit in reversed(bits):
        for r in [r for r in held if not r & bit]:
            total = add(held[r], flip(held.pop(r | bit), bit))
            held[r] = total if bit == bits[0] else total.astype(BF)
    return (held[0],)


def finish_kernel(count, sizes, flipped, *refs):
    total = functools.reduce(add, [r[...] for r in refs[1:count]], refs[0][...].astype(F32))
    start = 0
    for size, out_ref in zip(sizes, refs[count:]):
        piece = total[:, start : start + size]
        if flipped:
            out_ref[...] = piece.T
        elif len(out_ref.shape) == 3:
            part = out_ref.shape[2]
            for n in range(out_ref.shape[0]):
                out_ref[n] = piece[:, n * part : (n + 1) * part]
        else:
            out_ref[...] = piece
        start += size


def finish_grad(parts, shapes, flipped, name):
    sizes = [s[0] if flipped else s[1] if len(s) == 2 else s[0] * s[2] for s in shapes]
    outs = [jax.ShapeDtypeStruct(s, F32) for s in shapes]
    return pl.pallas_call(
        functools.partial(finish_kernel, len(parts), sizes, flipped),
        out_shape=outs,
        compiler_params=params(),
        cost_estimate=cost(4 * parts[0].size, parts, outs),
        name=name,
    )(*parts)


def step(array, by):
    n = lax.axis_size("tp")
    return lax.ppermute(array, "tp", [(i, (i + by) % n) for i in range(n)])


def block_of(part, s):
    rows = part.shape[0] // lax.axis_size("tp")
    return part[s * rows : (s + 1) * rows]


def sum_over_tp(own):
    total = own
    for by in range(1, lax.axis_size("tp")):
        total = total + step(own, by)
    return total


def sum_over_fsdp(stats):
    count = lax.axis_size("fsdp")
    half = stats.shape[1] // 2
    stats = stats[:, :half] + flip(stats[:, half:], 1)
    size = half // (count // 2)
    total = stats[:, :size]
    for r in range(2, count, 2):
        total = total + flip(stats[:, r // 2 * size : (r // 2 + 1) * size], r)
    return total


def local(tokens, gain, bias, w_qkv, w_out, w_up, w_down, cotangent):
    _, own_rows, width = tokens.shape
    groups = lax.axis_size("tp")
    count = lax.axis_size("fsdp")
    heads_here = HEADS // groups
    part = heads_here * HEAD_DIM
    ff = w_up.shape[1]
    length = own_rows * groups
    own_f = lax.axis_index("fsdp").astype(jnp.int32)[None]
    own_t = lax.axis_index("tp").astype(jnp.int32)[None]
    x, g = tokens[0], cotangent[0]
    tables = angle_tables(length)

    n = groups
    more = n - 1

    near_up = gather_near(w_up)
    normed_own, cot_own = enter(x, g, gain, bias, own_f, count)
    normed = [normed_own]
    if more >= 1:
        normed.append(step(normed[-1], 1))
    own_qkv = jnp.swapaxes(w_qkv, 0, 1)
    own_2 = jnp.concatenate([w_down, w_out], axis=0)
    normed, tables = fence(normed, tables)
    if more >= 2:
        normed = normed + [step(normed[-1], 1)]
    near_up, own_qkv, own_2, cot_own, tables = fence(near_up, own_qkv, own_2, cot_own, tables)

    far_up = gather_far(near_up, 0)
    near_qkv = gather_near(own_qkv)
    up_mine = in_place_order(far_up, 0)
    (normed,) = fence(normed)
    while len(normed) < n:
        normed = normed + [step(normed[-1], 1)]
    up_mine, near_qkv, own_2, cot_own, _ = fence(up_mine, near_qkv, own_2, cot_own, normed[:3])

    up = (up_mine, flip(up_mine, 1))
    qkv_mine = in_place_order(gather_far(near_qkv, 1), 1)
    normed, cot_own = fence(normed, cot_own)
    cots = [cot_own]
    if more >= 1:
        cots.append(step(cot_own, 1))
    up, qkv_mine, own_2, normed = fence(up, qkv_mine, own_2, normed)

    wq = (qkv_mine, flip(qkv_mine, 1))
    near_2 = gather_near(own_2)
    hidden, slope = up_project(normed, up)
    cots, hidden, slope = fence(cots, hidden, slope)
    if more >= 2:
        cots = cots + [step(cots[-1], 1)]
    wq, normed, up, hidden, slope = fence(wq, normed, up, hidden, slope)

    qkv = qkv_project(normed, wq)
    qkv, near_2 = fence(qkv, near_2)
    halves_2 = far_halves(near_2, 1)
    mine_2 = in_place_order(gather_far(near_2, 1, halves_2), 1)
    qkv = after(qkv, *halves_2)
    q, k, v, attended, lse = attend_forward(qkv, tables, heads_here, own_t, groups)
    cots, q, k, v, attended, lse = fence(cots, q, k, v, attended, lse)
    early = max(n // 2, 1)
    first_cots = cots[:early]
    while len(cots) < n:
        cots = cots + [step(cots[-1], 1)]
    mine_2, wq, normed, up, hidden, slope, q, k, v, attended, lse, first_cots = fence(
        mine_2, wq, normed, up, hidden, slope, q, k, v, attended, lse, first_cots
    )

    w2 = (mine_2, flip(mine_2, 1))
    branch = branch_project(hidden, attended, w2[0], 0, None)
    branch = branch_project(hidden, attended, w2[1], 1, branch)
    d_branch = d_branch_project(after(first_cots, branch), 0, slope, w2, None)
    cots, branch, d_branch = fence(cots, branch, d_branch)

    arrived = step(block_of(branch, 1), 1) if more else jnp.zeros_like(branch)
    if more:
        d_branch = d_branch_project(cots[early:], 1, slope, w2, d_branch)
    away2 = weight_grad(after(cots, d_branch), [hidden, attended], [ff, part], 1, None, "down_away")
    away_up = weight_grad(after(normed, away2), [d_branch], [ff], 1, None, "up_away")
    arrived, branch, away2, away_up = fence(arrived, branch, away2, away_up)
    if more >= 2:
        arrived = step(add(block_of(branch, 2), arrived).astype(BF), 1)
    away2, away_up, cots, branch, d_branch, wq, normed, up, hidden, attended, q, k, v, lse = fence(
        away2, away_up, cots, branch, d_branch, wq, normed, up, hidden, attended, q, k, v, lse
    )

    theirs2, theirs_up = flip(away2, 1), flip(away_up, 1)
    dqkv = attend_backward(q, k, v, d_branch, ff, lse, tables, own_t, groups)
    mine2 = weight_grad(after(cots, dqkv), [hidden, attended], [ff, part], 0, theirs2, "down_mine")
    arrived, branch, dqkv, mine2 = fence(arrived, branch, dqkv, mine2)
    for s in range(3, n):
        arrived = step(add(block_of(branch, s), arrived).astype(BF), 1)
    mine2, theirs_up, dqkv, branch, d_branch, wq, normed, up = fence(
        mine2, theirs_up, dqkv, branch, d_branch, wq, normed, up
    )

    first2 = scatter_first(mine2)
    d_normed = d_normed_project(d_branch, dqkv, up, wq)
    d_normed, first2 = fence(d_normed, first2)
    to2 = scatter_merge(*first2)
    away_qkv = weight_grad(after(normed, d_normed), list(dqkv), [part] * 3, 1, None, "qkv_away")
    arrived, d_normed, away_qkv = fence(arrived, d_normed, away_qkv)
    d_in = step(block_of(d_normed, 1), 1) if more else jnp.zeros_like(d_normed)
    to2, away_qkv, theirs_up, d_branch, dqkv, branch, normed, arrived = fence(
        to2, away_qkv, theirs_up, d_branch, dqkv, branch, normed, arrived
    )

    parts2 = scatter_second(to2)
    theirs_qkv = flip(away_qkv, 1)
    mine_up = weight_grad(normed, [d_branch], [ff], 0, theirs_up, "up_mine")
    output = leave_output(x, after(branch, mine_up), arrived, own_f, count)
    mine_qkv = weight_grad(after(normed, output), list(dqkv), [part] * 3, 0, theirs_qkv, "qkv_mine")
    d_in, d_normed, mine_up, mine_qkv, output, parts2 = fence(d_in, d_normed, mine_up, mine_qkv, output, parts2)
    if more >= 2:
        d_in = step(add(block_of(d_normed, 2), d_in).astype(BF), 1)

    first_up, first_qkv = scatter_first(mine_up), scatter_first(mine_qkv)
    grad_down, grad_out = finish_grad(parts2, [w_down.shape, w_out.shape], True, "finish_down")
    d_in, d_normed, grad_down, grad_out = fence(d_in, d_normed, grad_down, grad_out)
    for s in range(3, n):
        d_in = step(add(block_of(d_normed, s), d_in).astype(BF), 1)
    first_up, first_qkv, d_normed = fence(first_up, first_qkv, d_normed)

    parts_qkv = scatter_second(scatter_merge(*first_qkv))
    parts_up = scatter_second(scatter_merge(*first_up))
    d_in, d_normed, parts_qkv = fence(d_in, d_normed, parts_qkv)
    in_grad, stats = leave_grad(x, g, d_normed, d_in, gain, own_f, count)
    stats = sum_over_tp(stats)
    stats, parts_up, parts_qkv = fence(stats, parts_up, parts_qkv)
    stats = sum_over_fsdp(stats)
    (grad_up,) = finish_grad(parts_up, [w_up.shape], False, "finish_up")
    (grad_qkv,) = finish_grad(parts_qkv, [own_qkv.shape], False, "finish_qkv")
    grad_qkv = jnp.swapaxes(grad_qkv, 0, 1)
    return (
        output[None],
        in_grad[None],
        stats[0],
        stats[1],
        grad_qkv,
        grad_out,
        grad_up,
        grad_down,
    )


def solution(mesh):
    return jax.shard_map(
        local,
        mesh=mesh,
        in_specs=(
            P("fsdp", "tp", None),
            P(),
            P(),
            P("fsdp", None, "tp"),
            P("tp", "fsdp"),
            P("fsdp", "tp"),
            P("tp", "fsdp"),
            P("fsdp", "tp", None),
        ),
        out_specs=(
            P("fsdp", "tp", None),
            P("fsdp", "tp", None),
            P("fsdp"),
            P("fsdp"),
            P("fsdp", None, "tp"),
            P("tp", "fsdp"),
            P("fsdp", "tp"),
            P("tp", "fsdp"),
        ),
        check_vma=False,
    )
```

profile of v0, /device:TPU:0, one launch (start us, length us, event | category | flops | bytes accessed | tf_op | source)
XLA Modules:
  0.0 380.6 jit_solution(10847247603023487072)
XLA Ops:
  0.6 3.0 collective-permute-start.3
  10.1 1.6 collective-permute-start
  11.7 3.2 fusion.2
  16.1 20.2 %collective-permute-done.refs_1_ = bf16[256,2048]{1,0:T(8,128)(2,1)S(1)} collective-permute-done((bf16[256,2048]{1,0:T(8,128)(2,1)S(1)}, bf16[256,2048]{1,0:T(8,128)(2,1)S(1)}, u32[]{:S(2)}, u32[]{:S(2)}) %collective-permute-start) | collective-permute-done | bytes 1048608 | tf_op jit(solution)/shard_map/ppermute | solution.py:783
  44.5 21.2 %collective-permute-done.5 = bf16[128,2048]{1,0:T(8,128)(2,1)S(1)} collective-permute-done((bf16[128,2048]{1,0:T(8,128)(2,1)S(1)}, bf16[128,2048]{1,0:T(8,128)(2,1)S(1)}, u32[]{:S(2)}, u32[]{:S(2)}) %collective-permute-start.5) | collective-permute-done | bytes 524320 | tf_op jit(solution)/shard_map/ppermute | solution.py:653
  71.0 6.6 %collective-permute-done.11 = bf16[3,128,512]{2,1,0:T(8,128)(2,1)S(1)} collective-permute-done((bf16[3,128,512]{2,1,0:T(8,128)(2,1)S(1)}, bf16[3,128,512]{2,1,0:T(8,128)(2,1)S(1)}, u32[]{:S(2)}, u32[]{:S(2)}) %collective-permute-start.11) | collective-permute-done | bytes 393248 | tf_op jit(solution)/shard_map/ppermute | solution.py:653
  79.2 14.1 %collective-permute-done.2.refs_3_ = bf16[256,2048]{1,0:T(8,128)(2,1)S(1)} collective-permute-done((bf16[256,2048]{1,0:T(8,128)(2,1)S(1)}, bf16[256,2048]{1,0:T(8,128)(2,1)S(1)}, u32[]{:S(2)}, u32[]{:S(2)}) %collective-permute-start.2) | collective-permute-done | bytes 1048608 | tf_op jit(solution)/shard_map/ppermute | solution.py:783
  93.5 1.7 collective-permute-start.16
  95.6 14.6 %up.1 = (bf16[1024,2048]{1,0:T(8,128)(2,1)S(1)}, bf16[1024,2048]{1,0:T(8,128)(2,1)S(1)}) custom-call(bf16[256,2048]{1,0:T(8,128)(2,1)S(1)} %get-tuple-element.479.refs_0_, bf16[256,2048]{1,0:T(8,128)(2,1)S(1)} %collective-permute-done.refs_1_, bf16[256,2048]{1,0:T(8,128)(2,1)S(1)} %collective-permute-done.1.refs_2_, ...), custom_call_target="tpu_custom_call" | custom-call | flops 1073741824 | bytes 2621440 | tf_op jit(solution)/shard_map/up/pallas_call | solution.py:385
  110.2 2.0 copy-done
  112.2 2.0 copy-done.15
  114.2 6.7 %collective-permute-done.9.refs_1_ = bf16[256,2048]{1,0:T(8,128)(2,1)} collective-permute-done((bf16[256,2048]{1,0:T(8,128)(2,1)S(1)}, bf16[256,2048]{1,0:T(8,128)(2,1)}, u32[]{:S(2)}, u32[]{:S(2)}) %collective-permute-start.9) | collective-permute-done | bytes 1048608 | tf_op jit(solution)/shard_map/ppermute | solution.py:783
  122.3 9.3 %qkv.1.q_in.k_in.v_in = f32[1024,1536]{1,0:T(8,128)S(1)} custom-call(bf16[256,2048]{1,0:T(8,128)(2,1)S(1)} %get-tuple-element.479.refs_0_, bf16[256,2048]{1,0:T(8,128)(2,1)S(1)} %collective-permute-done.refs_1_, bf16[256,2048]{1,0:T(8,128)(2,1)S(1)} %collective-permute-done.1.refs_2_, bf16[256,2048]{1,0:T(8,128)(2,1)S(1)} %copy-done.9, ...), custom_call_target="tpu_custom_call" | custom-call | flops 805306368 | bytes 2097152 | tf_op jit(solution)/shard_map/qkv/pallas_call | solution.py:385
  133.9 1.6 collective-permute-start.19
  136.0 11.4 %attend_forward.1 = (bf16[1024,512]{1,0:T(8,128)(2,1)S(1)}, bf16[1024,512]{1,0:T(8,128)(2,1)S(1)}, bf16[1024,512]{1,0:T(8,128)(2,1)S(1)}, bf16[1024,512]{1,0:T(8,128)(2,1)S(1)}, f32[4,8,1024]{2,1,0:T(8,128)S(1)}) custom-call(s32[1]{0:T(128)} %bitcast.6.me_ref, f32[1024,1536]{1,0:T(8,128)S(1)} %qkv.1.q_in.k_in.v_in, f32[1024,1536]{1,0:T(8,128)S(1)} %qkv.1.q_in.k_in.v_in, ...), custom_call_target="tpu_custom_call" | custom-call | flops 1073741824 | bytes 1523712 | tf_op jit(solution)/shard_map/attend_forward/pallas_call | solution.py:257
  147.8 2.2 constant_dynamic-update-slice_fusion.14
  151.5 1.6 constant_dynamic-update-slice_fusion.12
  154.1 6.2 %branch.2.rest_0_ = bf16[1024,2048]{1,0:T(8,128)(2,1)S(1)} custom-call(bf16[1024,2048]{1,0:T(8,128)(2,1)S(1)} %copy-done.1, bf16[1024,512]{1,0:T(8,128)(2,1)S(1)} %get-tuple-element.405.att_ref.refs_5_, bf16[2560,1024]{1,0:T(8,128)(2,1)S(1)} %constant_dynamic-update-slice_fusion.10.w_ref.refs_3_), custom_call_target="tpu_custom_call" | custom-call | flops 671088640 | bytes 1835008 | tf_op jit(solution)/shard_map/branch/pallas_call | solution.py:385
  160.4 2.0 collective-permute-done.20.w_ref.refs_4_
  162.4 6.2 %branch.3.own_ref = bf16[1024,2048]{1,0:T(8,128)(2,1)S(1)} custom-call(bf16[1024,2048]{1,0:T(8,128)(2,1)S(1)} %copy-done.1, bf16[1024,512]{1,0:T(8,128)(2,1)S(1)} %get-tuple-element.405.att_ref.refs_5_, bf16[2560,1024]{1,0:T(8,128)(2,1)S(1)} %collective-permute-done.20.w_ref.refs_4_, ...), custom_call_target="tpu_custom_call", output_to_operand_aliasing={{}: (3, {})} | custom-call | flops 671088640 | bytes 2359296 | tf_op jit(solution)/shard_map/branch/pallas_call | solution.py:385
  168.7 8.6 %d_branch.2.refs_5_ = bf16[1024,2560]{1,0:T(8,128)(2,1)S(1)} custom-call(bf16[256,2048]{1,0:T(8,128)(2,1)S(1)} %copy-done.18, bf16[256,2048]{1,0:T(8,128)(2,1)} %collective-permute-done.9.refs_1_, bf16[1024,2048]{1,0:T(8,128)(2,1)S(1)} %copy-done.16, bf16[2560,1024]{1,0:T(8,128)(2,1)S(1)} %constant_dynamic-update-slice_fusion.10.w_ref.refs_3_, ...), custom_call_target="tpu_custom_call" | custom-call | flops 671088640 | bytes 2752512 | tf_op jit(solution)/shard_map/d_branch/pallas_call | solution.py:385
  177.3 4.2 %collective-permute-done.17.refs_1_.refs_3_ = bf16[256,2048]{1,0:T(8,128)(2,1)S(1)} collective-permute-done((bf16[256,2048]{1,0:T(8,128)(2,1)}, bf16[256,2048]{1,0:T(8,128)(2,1)S(1)}, u32[]{:S(2)}, u32[]{:S(2)}) %collective-permute-start.17) | collective-permute-done | bytes 1048608 | tf_op jit(solution)/shard_map/ppermute | solution.py:783
  181.9 8.6 %d_branch.3.refs_4_.g_in.du_ref = bf16[1024,2560]{1,0:T(8,128)(2,1)S(1)} custom-call(bf16[256,2048]{1,0:T(8,128)(2,1)} %collective-permute-done.13.refs_0_.refs_2_, bf16[256,2048]{1,0:T(8,128)(2,1)S(1)} %collective-permute-done.17.refs_1_.refs_3_, bf16[1024,2048]{1,0:T(8,128)(2,1)S(1)} %copy-done.16, ...), custom_call_target="tpu_custom_call", output_to_operand_aliasing={{}: (5, {})} | custom-call | flops 671088640 | bytes 3407872 | tf_op jit(solution)/shard_map/d_branch/pallas_call | solution.py:385
  190.5 7.5 %down_away.1 = bf16[1024,2560]{1,0:T(8,128)(2,1)S(1)} custom-call(bf16[256,2048]{1,0:T(8,128)(2,1)S(1)} %copy-done.18, bf16[256,2048]{1,0:T(8,128)(2,1)} %collective-permute-done.9.refs_1_, bf16[256,2048]{1,0:T(8,128)(2,1)} %collective-permute-done.13.refs_0_.refs_2_, bf16[256,2048]{1,0:T(8,128)(2,1)S(1)} %collective-permute-done.17.refs_1_.refs_3_, ...), custom_call_target="tpu_custom_call" | custom-call | flops 671088640 | bytes 1835008 | tf_op jit(solution)/shard_map/down_away/pallas_call | solution.py:385
  198.1 6.8 %up_away.1 = bf16[1024,2048]{1,0:T(8,128)(2,1)} custom-call(bf16[256,2048]{1,0:T(8,128)(2,1)S(1)} %copy-done.3, bf16[256,2048]{1,0:T(8,128)(2,1)S(1)} %copy-done.5, bf16[256,2048]{1,0:T(8,128)(2,1)S(1)} %copy-done.7, bf16[256,2048]{1,0:T(8,128)(2,1)S(1)} %copy-done.10, bf16[1024,2560]{1,0:T(8,128)(2,1)S(1)} %d_branch.3.refs_4_.g_in.du_ref), custom_call_target="tpu_custom_call" | custom-call | flops 536870912 | bytes 1703936 | tf_op jit(solution)/shard_map/up_away/pallas_call | solution.py:385
  204.9 3.6 collective-permute-done.21
  210.5 16.8 %attend_backward.1 = (bf16[1024,512]{1,0:T(8,128)(2,1)S(1)}, bf16[1024,512]{1,0:T(8,128)(2,1)S(1)}, bf16[1024,512]{1,0:T(8,128)(2,1)S(1)}) custom-call(s32[1]{0:T(128)} %bitcast.6.me_ref, bf16[1024,512]{1,0:T(8,128)(2,1)S(1)} %copy-done.36, bf16[1024,512]{1,0:T(8,128)(2,1)S(1)} %copy-done.38, bf16[1024,512]{1,0:T(8,128)(2,1)S(1)} %copy-done.40, ...), custom_call_target="tpu_custom_call" | custom-call | flops 2684354560 | bytes 1114112 | tf_op jit(solution)/shard_map/attend_backward/pallas_call | solution.py:353
  227.4 2.4 copy-done.23
  229.8 2.5 copy-done.24
  232.3 8.7 %down_mine.1 = (bf16[256,2560]{1,0:T(8,128)(2,1)S(1)}, bf16[256,2560]{1,0:T(8,128)(2,1)S(1)}, bf16[256,2560]{1,0:T(8,128)(2,1)S(1)}, bf16[128,2560]{1,0:T(8,128)(2,1)S(1)}, bf16[128,2560]{1,0:T(8,128)(2,1)S(1)}) custom-call(bf16[256,2048]{1,0:T(8,128)(2,1)S(1)} %copy-done.18, bf16[256,2048]{1,0:T(8,128)(2,1)} %collective-permute-done.9.refs_1_, ...), custom_call_target="tpu_custom_call" | custom-call | flops 671088640 | bytes 2490368 | tf_op jit(solution)/shard_map/down_mine/pallas_call | solution.py:385
  241.0 2.1 add_convert_fusion.2
  245.5 19.1 %d_normed.1.own_ref = bf16[1024,2048]{1,0:T(8,128)(2,1)S(1)} custom-call(bf16[1024,2560]{1,0:T(8,128)(2,1)S(1)} %d_branch.3.refs_4_.g_in.du_ref, bf16[1024,512]{1,0:T(8,128)(2,1)S(1)} %get-tuple-element.483.dq_ref.refs_4_, bf16[1024,512]{1,0:T(8,128)(2,1)S(1)} %get-tuple-element.484.dk_ref.refs_5_, bf16[1024,512]{1,0:T(8,128)(2,1)S(1)} %get-tuple-element.485.dv_ref.refs_6_, ...), custom_call_target="tpu_custom_call" | custom-call | flops 1879048192 | bytes 3407872 | tf_op jit(solution)/shard_map/d_normed/pallas_call | solution.py:385
  265.8 4.4 %qkv_away.1 = bf16[1024,1536]{1,0:T(8,128)(2,1)S(1)} custom-call(bf16[256,2048]{1,0:T(8,128)(2,1)S(1)} %copy-done.3, bf16[256,2048]{1,0:T(8,128)(2,1)S(1)} %copy-done.5, bf16[256,2048]{1,0:T(8,128)(2,1)S(1)} %copy-done.7, bf16[256,2048]{1,0:T(8,128)(2,1)S(1)} %copy-done.10, bf16[1024,512]{1,0:T(8,128)(2,1)S(1)} %get-tuple-element.483.dq_ref.refs_4_, ...), custom_call_target="tpu_custom_call" | custom-call | flops 402653184 | bytes 1310720 | tf_op jit(solution)/shard_map/qkv_away/pallas_call | solution.py:385
  273.8 7.1 %up_mine.1 = (bf16[256,2048]{1,0:T(8,128)(2,1)S(1)}, bf16[256,2048]{1,0:T(8,128)(2,1)S(1)}, bf16[256,2048]{1,0:T(8,128)(2,1)S(1)}, bf16[128,2048]{1,0:T(8,128)(2,1)S(1)}, bf16[128,2048]{1,0:T(8,128)(2,1)S(1)}) custom-call(bf16[256,2048]{1,0:T(8,128)(2,1)S(1)} %copy-done.3, bf16[256,2048]{1,0:T(8,128)(2,1)S(1)} %copy-done.5, bf16[256,2048]{1,0:T(8,128)(2,1)S(1)} %copy-done.7, ...), custom_call_target="tpu_custom_call" | custom-call | flops 536870912 | bytes 2228224 | tf_op jit(solution)/shard_map/up_mine/pallas_call | solution.py:385
  282.3 6.0 %qkv_mine.1 = (bf16[256,1536]{1,0:T(8,128)(2,1)S(1)}, bf16[256,1536]{1,0:T(8,128)(2,1)S(1)}, bf16[256,1536]{1,0:T(8,128)(2,1)S(1)}, bf16[128,1536]{1,0:T(8,128)(2,1)S(1)}, bf16[128,1536]{1,0:T(8,128)(2,1)S(1)}) custom-call(bf16[256,2048]{1,0:T(8,128)(2,1)S(1)} %copy-done.3, bf16[256,2048]{1,0:T(8,128)(2,1)S(1)} %copy-done.5, ...), custom_call_target="tpu_custom_call" | custom-call | flops 402653184 | bytes 1703936 | tf_op jit(solution)/shard_map/qkv_mine/pallas_call | solution.py:385
  288.4 11.2 %collective-permute-done.28 = bf16[256,2048]{1,0:T(8,128)(2,1)S(1)} collective-permute-done((bf16[256,2048]{1,0:T(8,128)(2,1)S(1)}, bf16[256,2048]{1,0:T(8,128)(2,1)S(1)}, u32[]{:S(2)}, u32[]{:S(2)}) %collective-permute-start.28) | collective-permute-done | bytes 1048608 | tf_op jit(solution)/shard_map/ppermute | solution.py:783
  299.6 1.9 collective-permute-done.30.refs_1_
  307.8 2.1 finish_down.1
  310.0 19.5 %collective-permute-done.32 = bf16[256,2048]{1,0:T(8,128)(2,1)S(1)} collective-permute-done((bf16[256,2048]{1,0:T(8,128)(2,1)S(1)}, bf16[256,2048]{1,0:T(8,128)(2,1)S(1)}, u32[]{:S(2)}, u32[]{:S(2)}) %collective-permute-start.32) | collective-permute-done | bytes 1048608 | tf_op jit(solution)/shard_map/ppermute | solution.py:783
  335.0 16.1 %collective-permute-done.38.refs_1_ = bf16[256,1536]{1,0:T(8,128)(2,1)S(1)} collective-permute-done((bf16[256,1536]{1,0:T(8,128)(2,1)S(1)}, bf16[256,1536]{1,0:T(8,128)(2,1)S(1)}, u32[]{:S(2)}, u32[]{:S(2)}) %collective-permute-start.38) | collective-permute-done | bytes 786464 | tf_op jit(solution)/shard_map/ppermute | solution.py:653
  352.0 3.6 collective-permute-done.33.in_ref
  355.6 3.9 %leave_grad.1 = (f32[256,2048]{1,0:T(8,128)}, f32[2,2048]{1,0:T(2,128)S(1)}) custom-call(s32[1]{0:T(128)} %bitcast.me_ref, bf16[256,2048]{1,0:T(8,128)(2,1)S(1)} %bitcast.14, bf16[256,2048]{1,0:T(8,128)(2,1)S(1)} %bitcast.16, bf16[1024,2048]{1,0:T(8,128)(2,1)S(1)} %d_normed.1.own_ref, bf16[256,2048]{1,0:T(8,128)(2,1)S(1)} %collective-permute-done.33.in_ref, ...), custom_call_target="tpu_custom_call" | custom-call | flops 1310720 | bytes 788480 | tf_op jit(solution)/shard_map/leave_grad/pallas_call | solution.py:159
  359.8 1.6 collective-permute-start.40
  361.5 1.7 collective-permute-done.42
  364.1 1.6 collective-permute-done.40
  365.7 5.2 %collective-permute-done.43.refs_1_ = bf16[256,2048]{1,0:T(8,128)(2,1)S(1)} collective-permute-done((bf16[256,2048]{1,0:T(8,128)(2,1)S(1)}, bf16[256,2048]{1,0:T(8,128)(2,1)S(1)}, u32[]{:S(2)}, u32[]{:S(2)}) %collective-permute-start.43) | collective-permute-done | bytes 1048608 | tf_op jit(solution)/shard_map/ppermute | solution.py:653
  374.0 1.9 collective-permute-start.48
  377.7 1.7 finish_up.1
  (211 shorter events, 60.4 us)
Async XLA Ops:
  0.6 35.7 %collective-permute-start.3 = (bf16[256,2048]{1,0:T(8,128)(2,1)}, bf16[256,2048]{1,0:T(8,128)(2,1)S(1)}, u32[]{:S(2)}, u32[]{:S(2)}) collective-permute-start(bf16[256,2048]{1,0:T(8,128)(2,1)} %param.13), channel_id=1, source_target_pairs={{0,8},{4,12},{8,0},{12,4},{16,24},{20,28},{24,16},{28,20},{1,9},{5... | collective-permute-start | bytes 3145736 | tf_op jit(solution)/shard_map/ppermute | solution.py:653
  3.6 32.7 %collective-permute-start.4 = (bf16[256,2048]{1,0:T(8,128)(2,1)}, bf16[256,2048]{1,0:T(8,128)(2,1)}, u32[]{:S(2)}, u32[]{:S(2)}) collective-permute-start(bf16[256,2048]{1,0:T(8,128)(2,1)} %param.13), channel_id=1, source_target_pairs={{0,16},{4,20},{8,24},{12,28},{16,0},{20,4},{24,8},{28,12},{1,17},{... | collective-permute-start | bytes 3145736 | tf_op jit(solution)/shard_map/ppermute | solution.py:653
  10.1 26.3 %collective-permute-start = (bf16[256,2048]{1,0:T(8,128)(2,1)S(1)}, bf16[256,2048]{1,0:T(8,128)(2,1)S(1)}, u32[]{:S(2)}, u32[]{:S(2)}) collective-permute-start(bf16[256,2048]{1,0:T(8,128)(2,1)S(1)} %get-tuple-element.479.refs_0_), channel_id=1, source_target_pairs={{0,1},{1,2},{2,3},{3,0},{4,5},{5,6},{6,7},{7,4},{8,9},{9,10},{10,1... | collective-permute-start | bytes 3145736 | tf_op jit(solution)/shard_map/ppermute | solution.py:783
  36.4 29.5 %collective-permute-start.8 = (bf16[3,256,512]{2,1,0:T(8,128)(2,1)S(1)}, bf16[3,256,512]{2,1,0:T(8,128)(2,1)S(1)}, u32[]{:S(2)}, u32[]{:S(2)}) collective-permute-start(bf16[3,256,512]{2,1,0:T(8,128)(2,1)S(1)} %bitcast.22), channel_id=1, source_target_pairs={{0,16},{4,20},{8,24},{12,28},{16,0},{20,4},{24,8},{28,12},{1,17},{... | collective-permute-start | bytes 2359304 | tf_op jit(solution)/shard_map/ppermute | solution.py:653
  36.9 28.9 %collective-permute-start.7 = (bf16[3,256,512]{2,1,0:T(8,128)(2,1)S(1)}, bf16[3,256,512]{2,1,0:T(8,128)(2,1)S(1)}, u32[]{:S(2)}, u32[]{:S(2)}) collective-permute-start(bf16[3,256,512]{2,1,0:T(8,128)(2,1)S(1)} %bitcast.23), channel_id=1, source_target_pairs={{0,8},{4,12},{8,0},{12,4},{16,24},{20,28},{24,16},{28,20},{1,9},{5... | collective-permute-start | bytes 2359304 | tf_op jit(solution)/shard_map/ppermute | solution.py:653
  38.6 27.1 %collective-permute-start.5 = (bf16[128,2048]{1,0:T(8,128)(2,1)S(1)}, bf16[128,2048]{1,0:T(8,128)(2,1)S(1)}, u32[]{:S(2)}, u32[]{:S(2)}) collective-permute-start(bf16[128,2048]{1,0:T(8,128)(2,1)S(1)} %slice.60), channel_id=1, source_target_pairs={{0,8},{4,12},{8,0},{12,4},{16,24},{20,28},{24,16},{28,20},{1,9},{5... | collective-permute-start | bytes 1572872 | tf_op jit(solution)/shard_map/ppermute | solution.py:653
  40.1 25.6 %collective-permute-start.6 = (bf16[128,2048]{1,0:T(8,128)(2,1)S(1)}, bf16[128,2048]{1,0:T(8,128)(2,1)S(1)}, u32[]{:S(2)}, u32[]{:S(2)}) collective-permute-start(bf16[128,2048]{1,0:T(8,128)(2,1)S(1)} %slice.61), channel_id=1, source_target_pairs={{0,16},{4,20},{8,24},{12,28},{16,0},{20,4},{24,8},{28,12},{1,17},{... | collective-permute-start | bytes 1572872 | tf_op jit(solution)/shard_map/ppermute | solution.py:653
  41.7 24.2 %collective-permute-start.1 = (bf16[256,2048]{1,0:T(8,128)(2,1)S(1)}, bf16[256,2048]{1,0:T(8,128)(2,1)S(1)}, u32[]{:S(2)}, u32[]{:S(2)}) collective-permute-start(bf16[256,2048]{1,0:T(8,128)(2,1)S(1)} %collective-permute-done.refs_1_), channel_id=1, source_target_pairs={{0,1},{1,2},{2,3},{3,0},{4,5},{5,6},{6,7},{7,4},{8,9},{9,10},{10,1... | collective-permute-start | bytes 3145736 | tf_op jit(solution)/shard_map/ppermute | solution.py:783
  65.9 27.4 %collective-permute-start.10 = (bf16[1024,2048]{1,0:T(8,128)(2,1)S(1)}, bf16[1024,2048]{1,0:T(8,128)(2,1)S(1)}, u32[]{:S(2)}, u32[]{:S(2)}) collective-permute-start(bf16[1024,2048]{1,0:T(8,128)(2,1)S(1)} %constant_dynamic-update-slice_fusion.refs_4_.um_ref), channel_id=1, source_target_pairs={{0,4},{4,0},{8,12},{12,8},{16,20},{20,16},{24,28},{28,24},{1,5},{5... | collective-permute-start | bytes 12582920 | tf_op jit(solution)/shard_map/ppermute | solution.py:653
  65.9 27.4 %collective-permute-start.2 = (bf16[256,2048]{1,0:T(8,128)(2,1)S(1)}, bf16[256,2048]{1,0:T(8,128)(2,1)S(1)}, u32[]{:S(2)}, u32[]{:S(2)}) collective-permute-start(bf16[256,2048]{1,0:T(8,128)(2,1)S(1)} %collective-permute-done.1.refs_2_), channel_id=1, source_target_pairs={{0,1},{1,2},{2,3},{3,0},{4,5},{5,6},{6,7},{7,4},{8,9},{9,10},{10,1... | collective-permute-start | bytes 3145736 | tf_op jit(solution)/shard_map/ppermute | solution.py:783
  66.1 11.5 %collective-permute-start.11 = (bf16[3,128,512]{2,1,0:T(8,128)(2,1)S(1)}, bf16[3,128,512]{2,1,0:T(8,128)(2,1)S(1)}, u32[]{:S(2)}, u32[]{:S(2)}) collective-permute-start(bf16[3,128,512]{2,1,0:T(8,128)(2,1)S(1)} %slice.62), channel_id=1, source_target_pairs={{0,8},{4,12},{8,0},{12,4},{16,24},{20,28},{24,16},{28,20},{1,9},{5... | collective-permute-start | bytes 1179656 | tf_op jit(solution)/shard_map/ppermute | solution.py:653
  67.0 11.4 %collective-permute-start.12 = (bf16[3,128,512]{2,1,0:T(8,128)(2,1)S(1)}, bf16[3,128,512]{2,1,0:T(8,128)(2,1)S(1)}, u32[]{:S(2)}, u32[]{:S(2)}) collective-permute-start(bf16[3,128,512]{2,1,0:T(8,128)(2,1)S(1)} %slice.63), channel_id=1, source_target_pairs={{0,16},{4,20},{8,24},{12,28},{16,0},{20,4},{24,8},{28,12},{1,17},{... | collective-permute-start | bytes 1179656 | tf_op jit(solution)/shard_map/ppermute | solution.py:653
  93.3 27.7 %collective-permute-start.14 = (bf16[3,1024,512]{2,1,0:T(8,128)(2,1)}, bf16[3,1024,512]{2,1,0:T(8,128)(2,1)}, u32[]{:S(2)}, u32[]{:S(2)}) collective-permute-start(bf16[3,1024,512]{2,1,0:T(8,128)(2,1)} %constant_dynamic-update-slice_fusion.5.refs_4_.qm_ref), channel_id=1, source_target_pairs={{0,4},{4,0},{8,12},{12,8},{16,20},{20,16},{24,28},{28,24},{1,5},{5... | collective-permute-start | bytes 9437192 | tf_op jit(solution)/shard_map/ppermute | solution.py:653
  93.4 27.5 %collective-permute-start.9 = (bf16[256,2048]{1,0:T(8,128)(2,1)S(1)}, bf16[256,2048]{1,0:T(8,128)(2,1)}, u32[]{:S(2)}, u32[]{:S(2)}) collective-permute-start(bf16[256,2048]{1,0:T(8,128)(2,1)S(1)} %get-tuple-element.400.refs_0_), channel_id=1, source_target_pairs={{0,1},{1,2},{2,3},{3,0},{4,5},{5,6},{6,7},{7,4},{8,9},{9,10},{10,1... | collective-permute-start | bytes 3145736 | tf_op jit(solution)/shard_map/ppermute | solution.py:783
  93.5 38.2 %collective-permute-start.16 = (bf16[2560,256]{1,0:T(8,128)(2,1)}, bf16[2560,256]{1,0:T(8,128)(2,1)}, u32[]{:S(2)}, u32[]{:S(2)}) collective-permute-start(bf16[2560,256]{1,0:T(8,128)(2,1)} %pad_maximum_fusion), channel_id=1, source_target_pairs={{0,16},{4,20},{8,24},{12,28},{16,0},{20,4},{24,8},{28,12},{1,17},{... | collective-permute-start | bytes 3932168 | tf_op jit(solution)/shard_map/ppermute | solution.py:653
  95.1 36.5 %collective-permute-start.15 = (bf16[2560,256]{1,0:T(8,128)(2,1)}, bf16[2560,256]{1,0:T(8,128)(2,1)}, u32[]{:S(2)}, u32[]{:S(2)}) collective-permute-start(bf16[2560,256]{1,0:T(8,128)(2,1)} %pad_maximum_fusion), channel_id=1, source_target_pairs={{0,8},{4,12},{8,0},{12,4},{16,24},{20,28},{24,16},{28,20},{1,9},{5... | collective-permute-start | bytes 3932168 | tf_op jit(solution)/shard_map/ppermute | solution.py:653
  120.8 27.0 %collective-permute-start.13 = (bf16[256,2048]{1,0:T(8,128)(2,1)}, bf16[256,2048]{1,0:T(8,128)(2,1)}, u32[]{:S(2)}, u32[]{:S(2)}) collective-permute-start(bf16[256,2048]{1,0:T(8,128)(2,1)} %collective-permute-done.9.refs_1_), channel_id=1, source_target_pairs={{0,1},{1,2},{2,3},{3,0},{4,5},{5,6},{6,7},{7,4},{8,9},{9,10},{10,1... | collective-permute-start | bytes 3145736 | tf_op jit(solution)/shard_map/ppermute | solution.py:783
  133.9 19.5 %collective-permute-start.19 = (bf16[2560,128]{1,0:T(8,128)(2,1)S(1)}, bf16[2560,128]{1,0:T(8,128)(2,1)S(1)}, u32[]{:S(2)}, u32[]{:S(2)}) collective-permute-start(bf16[2560,128]{1,0:T(8,128)(2,1)S(1)} %slice.65), channel_id=1, source_target_pairs={{0,16},{4,20},{8,24},{12,28},{16,0},{20,4},{24,8},{28,12},{1,17},{... | collective-permute-start | bytes 1966088 | tf_op jit(solution)/shard_map/ppermute | solution.py:653
  135.5 17.6 %collective-permute-start.18 = (bf16[2560,128]{1,0:T(8,128)(2,1)S(1)}, bf16[2560,128]{1,0:T(8,128)(2,1)S(1)}, u32[]{:S(2)}, u32[]{:S(2)}) collective-permute-start(bf16[2560,128]{1,0:T(8,128)(2,1)S(1)} %slice.64), channel_id=1, source_target_pairs={{0,8},{4,12},{8,0},{12,4},{16,24},{20,28},{24,16},{28,20},{1,9},{5... | collective-permute-start | bytes 1966088 | tf_op jit(solution)/shard_map/ppermute | solution.py:653
  153.7 8.7 %collective-permute-start.20 = (bf16[2560,1024]{1,0:T(8,128)(2,1)S(1)}, bf16[2560,1024]{1,0:T(8,128)(2,1)S(1)}, u32[]{:S(2)}, u32[]{:S(2)}) collective-permute-start(bf16[2560,1024]{1,0:T(8,128)(2,1)S(1)} %constant_dynamic-update-slice_fusion.10.w_ref.refs_3_), channel_id=1, source_target_pairs={{0,4},{4,0},{8,12},{12,8},{16,20},{20,16},{24,28},{28,24},{1,5},{5... | collective-permute-start | bytes 15728648 | tf_op jit(solution)/shard_map/ppermute | solution.py:653
  153.8 27.7 %collective-permute-start.17 = (bf16[256,2048]{1,0:T(8,128)(2,1)}, bf16[256,2048]{1,0:T(8,128)(2,1)S(1)}, u32[]{:S(2)}, u32[]{:S(2)}) collective-permute-start(bf16[256,2048]{1,0:T(8,128)(2,1)} %collective-permute-done.13.refs_0_.refs_2_), channel_id=1, source_target_pairs={{0,1},{1,2},{2,3},{3,0},{4,5},{5,6},{6,7},{7,4},{8,9},{9,10},{10,1... | collective-permute-start | bytes 3145736 | tf_op jit(solution)/shard_map/ppermute | solution.py:783
  181.6 27.0 %collective-permute-start.21 = (bf16[256,2048]{1,0:T(8,128)(2,1)S(1)}, bf16[256,2048]{1,0:T(8,128)(2,1)S(1)}, u32[]{:S(2)}, u32[]{:S(2)}) collective-permute-start(bf16[256,2048]{1,0:T(8,128)(2,1)S(1)} %slice.66), channel_id=1, source_target_pairs={{0,1},{1,2},{2,3},{3,0},{4,5},{5,6},{6,7},{7,4},{8,9},{9,10},{10,1... | collective-permute-start | bytes 3145736 | tf_op jit(solution)/shard_map/ppermute | solution.py:783
  208.6 18.8 %collective-permute-start.23 = (bf16[1024,2560]{1,0:T(8,128)(2,1)S(1)}, bf16[1024,2560]{1,0:T(8,128)(2,1)S(1)}, u32[]{:S(2)}, u32[]{:S(2)}) collective-permute-start(bf16[1024,2560]{1,0:T(8,128)(2,1)S(1)} %down_away.1), channel_id=1, source_target_pairs={{0,4},{4,0},{8,12},{12,8},{16,20},{20,16},{24,28},{28,24},{1,5},{5... | collective-permute-start | bytes 15728648 | tf_op jit(solution)/shard_map/ppermute | solution.py:653
  208.6 34.8 %collective-permute-start.25 = (bf16[1024,2048]{1,0:T(8,128)(2,1)}, bf16[1024,2048]{1,0:T(8,128)(2,1)}, u32[]{:S(2)}, u32[]{:S(2)}) collective-permute-start(bf16[1024,2048]{1,0:T(8,128)(2,1)} %up_away.1), channel_id=1, source_target_pairs={{0,4},{4,0},{8,12},{12,8},{16,20},{20,16},{24,28},{28,24},{1,5},{5... | collective-permute-start | bytes 12582920 | tf_op jit(solution)/shard_map/ppermute | solution.py:653
  210.4 30.5 %collective-permute-start.22 = (bf16[256,2048]{1,0:T(8,128)(2,1)}, bf16[256,2048]{1,0:T(8,128)(2,1)}, u32[]{:S(2)}, u32[]{:S(2)}) collective-permute-start(bf16[256,2048]{1,0:T(8,128)(2,1)} %add_convert_fusion.3), channel_id=1, source_target_pairs={{0,1},{1,2},{2,3},{3,0},{4,5},{5,6},{6,7},{7,4},{8,9},{9,10},{10,1... | collective-permute-start | bytes 3145736 | tf_op jit(solution)/shard_map/ppermute | solution.py:783
  243.1 27.2 %collective-permute-start.24 = (bf16[256,2048]{1,0:T(8,128)(2,1)S(1)}, bf16[256,2048]{1,0:T(8,128)(2,1)S(1)}, u32[]{:S(2)}, u32[]{:S(2)}) collective-permute-start(bf16[256,2048]{1,0:T(8,128)(2,1)S(1)} %add_convert_fusion.2), channel_id=1, source_target_pairs={{0,1},{1,2},{2,3},{3,0},{4,5},{5,6},{6,7},{7,4},{8,9},{9,10},{10,1... | collective-permute-start | bytes 3145736 | tf_op jit(solution)/shard_map/ppermute | solution.py:783
  243.4 21.2 %collective-permute-start.26 = (bf16[128,2560]{1,0:T(8,128)(2,1)S(1)}, bf16[128,2560]{1,0:T(8,128)(2,1)S(1)}, u32[]{:S(2)}, u32[]{:S(2)}) collective-permute-start(bf16[128,2560]{1,0:T(8,128)(2,1)S(1)} %get-tuple-element.442), channel_id=1, source_target_pairs={{0,8},{4,12},{8,0},{12,4},{16,24},{20,28},{24,16},{28,20},{1,9},{5... | collective-permute-start | bytes 1966088 | tf_op jit(solution)/shard_map/ppermute | solution.py:653
  245.0 19.6 %collective-permute-start.27 = (bf16[128,2560]{1,0:T(8,128)(2,1)S(1)}, bf16[128,2560]{1,0:T(8,128)(2,1)S(1)}, u32[]{:S(2)}, u32[]{:S(2)}) collective-permute-start(bf16[128,2560]{1,0:T(8,128)(2,1)S(1)} %get-tuple-element.443), channel_id=1, source_target_pairs={{0,16},{4,20},{8,24},{12,28},{16,0},{20,4},{24,8},{28,12},{1,17},{... | collective-permute-start | bytes 1966088 | tf_op jit(solution)/shard_map/ppermute | solution.py:653
  270.3 12.1 %collective-permute-start.29 = (bf16[1024,1536]{1,0:T(8,128)(2,1)S(1)}, bf16[1024,1536]{1,0:T(8,128)(2,1)S(1)}, u32[]{:S(2)}, u32[]{:S(2)}) collective-permute-start(bf16[1024,1536]{1,0:T(8,128)(2,1)S(1)} %qkv_away.1), channel_id=1, source_target_pairs={{0,4},{4,0},{8,12},{12,8},{16,20},{20,16},{24,28},{28,24},{1,5},{5... | collective-permute-start | bytes 9437192 | tf_op jit(solution)/shard_map/ppermute | solution.py:653
  270.3 31.2 %collective-permute-start.30 = (bf16[256,2560]{1,0:T(8,128)(2,1)S(1)}, bf16[256,2560]{1,0:T(8,128)(2,1)S(1)}, u32[]{:S(2)}, u32[]{:S(2)}) collective-permute-start(bf16[256,2560]{1,0:T(8,128)(2,1)S(1)} %get-tuple-element.493), channel_id=1, source_target_pairs={{0,8},{4,12},{8,0},{12,4},{16,24},{20,28},{24,16},{28,20},{1,9},{5... | collective-permute-start | bytes 3932168 | tf_op jit(solution)/shard_map/ppermute | solution.py:653
  271.8 30.9 %collective-permute-start.31 = (bf16[256,2560]{1,0:T(8,128)(2,1)S(1)}, bf16[256,2560]{1,0:T(8,128)(2,1)S(1)}, u32[]{:S(2)}, u32[]{:S(2)}) collective-permute-start(bf16[256,2560]{1,0:T(8,128)(2,1)S(1)} %get-tuple-element.494), channel_id=1, source_target_pairs={{0,16},{4,20},{8,24},{12,28},{16,0},{20,4},{24,8},{28,12},{1,17},{... | collective-permute-start | bytes 3932168 | tf_op jit(solution)/shard_map/ppermute | solution.py:653
  272.5 27.1 %collective-permute-start.28 = (bf16[256,2048]{1,0:T(8,128)(2,1)S(1)}, bf16[256,2048]{1,0:T(8,128)(2,1)S(1)}, u32[]{:S(2)}, u32[]{:S(2)}) collective-permute-start(bf16[256,2048]{1,0:T(8,128)(2,1)S(1)} %slice.69), channel_id=1, source_target_pairs={{0,1},{1,2},{2,3},{3,0},{4,5},{5,6},{6,7},{7,4},{8,9},{9,10},{10,1... | collective-permute-start | bytes 3145736 | tf_op jit(solution)/shard_map/ppermute | solution.py:783
  303.1 26.3 %collective-permute-start.32 = (bf16[256,2048]{1,0:T(8,128)(2,1)S(1)}, bf16[256,2048]{1,0:T(8,128)(2,1)S(1)}, u32[]{:S(2)}, u32[]{:S(2)}) collective-permute-start(bf16[256,2048]{1,0:T(8,128)(2,1)S(1)} %add_convert_fusion.1), channel_id=1, source_target_pairs={{0,1},{1,2},{2,3},{3,0},{4,5},{5,6},{6,7},{7,4},{8,9},{9,10},{10,1... | collective-permute-start | bytes 3145736 | tf_op jit(solution)/shard_map/ppermute | solution.py:783
  303.8 26.5 %collective-permute-start.36 = (bf16[128,1536]{1,0:T(8,128)(2,1)S(1)}, bf16[128,1536]{1,0:T(8,128)(2,1)S(1)}, u32[]{:S(2)}, u32[]{:S(2)}) collective-permute-start(bf16[128,1536]{1,0:T(8,128)(2,1)S(1)} %get-tuple-element.513), channel_id=1, source_target_pairs={{0,8},{4,12},{8,0},{12,4},{16,24},{20,28},{24,16},{28,20},{1,9},{5... | collective-permute-start | bytes 1179656 | tf_op jit(solution)/shard_map/ppermute | solution.py:653
  304.9 25.3 %collective-permute-start.37 = (bf16[128,1536]{1,0:T(8,128)(2,1)S(1)}, bf16[128,1536]{1,0:T(8,128)(2,1)S(1)}, u32[]{:S(2)}, u32[]{:S(2)}) collective-permute-start(bf16[128,1536]{1,0:T(8,128)(2,1)S(1)} %get-tuple-element.514), channel_id=1, source_target_pairs={{0,16},{4,20},{8,24},{12,28},{16,0},{20,4},{24,8},{28,12},{1,17},{... | collective-permute-start | bytes 1179656 | tf_op jit(solution)/shard_map/ppermute | solution.py:653
  306.5 23.8 %collective-permute-start.34 = (bf16[128,2048]{1,0:T(8,128)(2,1)S(1)}, bf16[128,2048]{1,0:T(8,128)(2,1)S(1)}, u32[]{:S(2)}, u32[]{:S(2)}) collective-permute-start(bf16[128,2048]{1,0:T(8,128)(2,1)S(1)} %get-tuple-element.508), channel_id=1, source_target_pairs={{0,8},{4,12},{8,0},{12,4},{16,24},{20,28},{24,16},{28,20},{1,9},{5... | collective-permute-start | bytes 1572872 | tf_op jit(solution)/shard_map/ppermute | solution.py:653
  307.0 23.3 %collective-permute-start.35 = (bf16[128,2048]{1,0:T(8,128)(2,1)S(1)}, bf16[128,2048]{1,0:T(8,128)(2,1)S(1)}, u32[]{:S(2)}, u32[]{:S(2)}) collective-permute-start(bf16[128,2048]{1,0:T(8,128)(2,1)S(1)} %get-tuple-element.509), channel_id=1, source_target_pairs={{0,16},{4,20},{8,24},{12,28},{16,0},{20,4},{24,8},{28,12},{1,17},{... | collective-permute-start | bytes 1572872 | tf_op jit(solution)/shard_map/ppermute | solution.py:653
  329.9 25.7 %collective-permute-start.33 = (bf16[256,2048]{1,0:T(8,128)(2,1)S(1)}, bf16[256,2048]{1,0:T(8,128)(2,1)S(1)}, u32[]{:S(2)}, u32[]{:S(2)}) collective-permute-start(bf16[256,2048]{1,0:T(8,128)(2,1)S(1)} %add_convert_fusion), channel_id=1, source_target_pairs={{0,1},{1,2},{2,3},{3,0},{4,5},{5,6},{6,7},{7,4},{8,9},{9,10},{10,1... | collective-permute-start | bytes 3145736 | tf_op jit(solution)/shard_map/ppermute | solution.py:783
  330.5 20.5 %collective-permute-start.38 = (bf16[256,1536]{1,0:T(8,128)(2,1)S(1)}, bf16[256,1536]{1,0:T(8,128)(2,1)S(1)}, u32[]{:S(2)}, u32[]{:S(2)}) collective-permute-start(bf16[256,1536]{1,0:T(8,128)(2,1)S(1)} %get-tuple-element.521), channel_id=1, source_target_pairs={{0,8},{4,12},{8,0},{12,4},{16,24},{20,28},{24,16},{28,20},{1,9},{5... | collective-permute-start | bytes 2359304 | tf_op jit(solution)/shard_map/ppermute | solution.py:653
  331.5 20.5 %collective-permute-start.39 = (bf16[256,1536]{1,0:T(8,128)(2,1)S(1)}, bf16[256,1536]{1,0:T(8,128)(2,1)S(1)}, u32[]{:S(2)}, u32[]{:S(2)}) collective-permute-start(bf16[256,1536]{1,0:T(8,128)(2,1)S(1)} %get-tuple-element.522), channel_id=1, source_target_pairs={{0,16},{4,20},{8,24},{12,28},{16,0},{20,4},{24,8},{28,12},{1,17},{... | collective-permute-start | bytes 2359304 | tf_op jit(solution)/shard_map/ppermute | solution.py:653
  333.4 37.6 %collective-permute-start.43 = (bf16[256,2048]{1,0:T(8,128)(2,1)S(1)}, bf16[256,2048]{1,0:T(8,128)(2,1)S(1)}, u32[]{:S(2)}, u32[]{:S(2)}) collective-permute-start(bf16[256,2048]{1,0:T(8,128)(2,1)S(1)} %get-tuple-element.532), channel_id=1, source_target_pairs={{0,8},{4,12},{8,0},{12,4},{16,24},{20,28},{24,16},{28,20},{1,9},{5... | collective-permute-start | bytes 3145736 | tf_op jit(solution)/shard_map/ppermute | solution.py:653
  334.1 37.5 %collective-permute-start.44 = (bf16[256,2048]{1,0:T(8,128)(2,1)S(1)}, bf16[256,2048]{1,0:T(8,128)(2,1)S(1)}, u32[]{:S(2)}, u32[]{:S(2)}) collective-permute-start(bf16[256,2048]{1,0:T(8,128)(2,1)S(1)} %get-tuple-element.533), channel_id=1, source_target_pairs={{0,16},{4,20},{8,24},{12,28},{16,0},{20,4},{24,8},{28,12},{1,17},{... | collective-permute-start | bytes 3145736 | tf_op jit(solution)/shard_map/ppermute | solution.py:653
  359.5 3.7 collective-permute-start.42
  359.5 4.6 %collective-permute-start.41 = (f32[2,2048]{1,0:T(2,128)S(1)}, f32[2,2048]{1,0:T(2,128)S(1)}, u32[]{:S(2)}, u32[]{:S(2)}) collective-permute-start(f32[2,2048]{1,0:T(2,128)S(1)} %get-tuple-element.526), channel_id=1, source_target_pairs={{0,2},{1,3},{2,0},{3,1},{4,6},{5,7},{6,4},{7,5},{8,10},{9,11},{10,... | collective-permute-start | bytes 49160 | tf_op jit(solution)/shard_map/ppermute | solution.py:783
  359.8 5.9 %collective-permute-start.40 = (f32[2,2048]{1,0:T(2,128)S(1)}, f32[2,2048]{1,0:T(2,128)S(1)}, u32[]{:S(2)}, u32[]{:S(2)}) collective-permute-start(f32[2,2048]{1,0:T(2,128)S(1)} %get-tuple-element.526), channel_id=1, source_target_pairs={{0,1},{1,2},{2,3},{3,0},{4,5},{5,6},{6,7},{7,4},{8,9},{9,10},{10,1... | collective-permute-start | bytes 49160 | tf_op jit(solution)/shard_map/ppermute | solution.py:783
  372.7 6.7 %collective-permute-start.46 = (f32[2,256]{1,0:T(2,128)S(1)}, f32[2,256]{1,0:T(2,128)S(1)}, u32[]{:S(2)}, u32[]{:S(2)}) collective-permute-start(f32[2,256]{1,0:T(2,128)S(1)} %get-tuple-element.546), channel_id=1, source_target_pairs={{0,8},{4,12},{8,0},{12,4},{16,24},{20,28},{24,16},{28,20},{1,9},{5... | collective-permute-start | bytes 6152 | tf_op jit(solution)/shard_map/ppermute | solution.py:653
  374.0 5.4 %collective-permute-start.48 = (f32[2,256]{1,0:T(2,128)S(1)}, f32[2,256]{1,0:T(2,128)S(1)}, u32[]{:S(2)}, u32[]{:S(2)}) collective-permute-start(f32[2,256]{1,0:T(2,128)S(1)} %get-tuple-element.547), channel_id=1, source_target_pairs={{0,24},{4,28},{8,16},{12,20},{16,8},{20,12},{24,0},{28,4},{1,25},{... | collective-permute-start | bytes 6152 | tf_op jit(solution)/shard_map/ppermute | solution.py:653
  375.9 3.6 collective-permute-start.47
  (50 other events, 769.9 us)
where the time goes:
time: 387 us; the launch traced here: 381 us
  Pallas kernels  154 us (40%)
  waiting for transfers between devices  145 us (37%)
  starting transfers between devices  38.6 us (10%)
  local copies, waits for them, and re-layouts  32.5 us (8%)
  other arithmetic  8.61 us (2%)
    pallas_call x13, Pallas kernels, product(): pl.pallas_call(body, grid=(steps,), in_specs=specs, out_specs=out_specs,...  113 us
    ppermute x15, waiting for transfers between devices, step(): return lax.ppermute(array, 'tp', [(i, (i + by) % n) for i in range(n)])  87.8 us
    ppermute x34, waiting for transfers between devices, flip(): return lax.ppermute(array, 'fsdp', [(s, s ^ bit) for s in range(count)])  57.1 us
    ppermute x34, starting transfers between devices, flip(): return lax.ppermute(array, 'fsdp', [(s, s ^ bit) for s in range(count)])  31.7 us
    unnamed x110, local copies, waits for them, and re-layouts  27.2 us
    pallas_call x1, Pallas kernels, attend_backward(): pl.pallas_call(functools.partial(attend_backward_kernel, block, count), g...  16.8 us
    pallas_call x1, Pallas kernels, attend_forward(): pl.pallas_call(functools.partial(attend_forward_kernel, block, count), gr...  11.4 us
  transfers between devices with their start and end apart: 49, of which 24 were waited for; matrix products, arithmetic and copies ran while one was open for 6% of the time, Pallas kernels for 40%

commit v1 on v0

--- a/solution.py
+++ b/solution.py
@@ -879,64 +879,66 @@
     d_branch = d_branch_project(after(first_cots, branch), 0, slope, w2, None)
     cots, branch, d_branch = fence(cots, branch, d_branch)
 
-    arrived = step(block_of(branch, 1), 1) if more else jnp.zeros_like(branch)
+    halves = split(block_of(branch, 1), 1) if more else ()
+    arrived = [step(halves[0], 1)] if more else []
+    away2 = weight_grad(cots, [hidden, attended], [ff, part], 1, None, "down_away")
     if more:
-        d_branch = d_branch_project(cots[early:], 1, slope, w2, d_branch)
-    away2 = weight_grad(after(cots, d_branch), [hidden, attended], [ff, part], 1, None, "down_away")
-    away_up = weight_grad(after(normed, away2), [d_branch], [ff], 1, None, "up_away")
-    arrived, branch, away2, away_up = fence(arrived, branch, away2, away_up)
+        d_branch = d_branch_project(after(cots[early:], away2), 1, slope, w2, d_branch)
+    arrived, halves, away2, cots, d_branch = fence(arrived, halves, away2, cots, d_branch)
+    if more:
+        arrived = arrived + [step(halves[1], 1)]
+    theirs2 = flip(away2, 1)
+    away_up = weight_grad(after(normed, d_branch), [d_branch], [ff], 1, None, "up_away")
+    mine2 = weight_grad(after(cots, away_up), [hidden, attended], [ff, part], 0, theirs2, "down_mine")
+    arrived, mine2, away_up, branch, d_branch = fence(arrived, mine2, away_up, branch, d_branch)
+    arrived = jnp.concatenate(arrived, axis=1) if more else jnp.zeros_like(branch)
     if more >= 2:
         arrived = step(add(block_of(branch, 2), arrived).astype(BF), 1)
-    away2, away_up, cots, branch, d_branch, wq, normed, up, hidden, attended, q, k, v, lse = fence(
-        away2, away_up, cots, branch, d_branch, wq, normed, up, hidden, attended, q, k, v, lse
-    )
-
-    theirs2, theirs_up = flip(away2, 1), flip(away_up, 1)
+    mine2, away_up, branch, d_branch, wq, normed, up, q, k, v, lse = fence(
+        mine2, away_up, branch, d_branch, wq, normed, up, q, k, v, lse
+    )
+
+    first2 = scatter_first(mine2)
     dqkv = attend_backward(q, k, v, d_branch, ff, lse, tables, own_t, groups)
-    mine2 = weight_grad(after(cots, dqkv), [hidden, attended], [ff, part], 0, theirs2, "down_mine")
-    arrived, branch, dqkv, mine2 = fence(arrived, branch, dqkv, mine2)
+    dqkv, first2 = fence(dqkv, first2)
+    to2 = scatter_merge(*first2)
+    away_qkv = weight_grad(after(normed, *jax.tree.leaves(to2)), list(dqkv), [part] * 3, 1, None, "qkv_away")
+    arrived, branch, dqkv, away_qkv = fence(arrived, branch, dqkv, away_qkv)
     for s in range(3, n):
         arrived = step(add(block_of(branch, s), arrived).astype(BF), 1)
-    mine2, theirs_up, dqkv, branch, d_branch, wq, normed, up = fence(
-        mine2, theirs_up, dqkv, branch, d_branch, wq, normed, up
-    )
-
-    first2 = scatter_first(mine2)
+    to2, away_up, away_qkv, dqkv, branch, d_branch, wq, normed, up = fence(
+        to2, away_up, away_qkv, dqkv, branch, d_branch, wq, normed, up
+    )
+
+    parts2 = scatter_second(to2)
+    theirs_up, theirs_qkv = flip(away_up, 1), flip(away_qkv, 1)
     d_normed = d_normed_project(d_branch, dqkv, up, wq)
-    d_normed, first2 = fence(d_normed, first2)
-    to2 = scatter_merge(*first2)
-    away_qkv = weight_grad(after(normed, d_normed), list(dqkv), [part] * 3, 1, None, "qkv_away")
-    arrived, d_normed, away_qkv = fence(arrived, d_normed, away_qkv)
+    mine_up = weight_grad(after(normed, d_normed), [d_branch], [ff], 0, theirs_up, "up_mine")
+    arrived, d_normed, mine_up, parts2 = fence(arrived, d_normed, mine_up, parts2)
     d_in = step(block_of(d_normed, 1), 1) if more else jnp.zeros_like(d_normed)
-    to2, away_qkv, theirs_up, d_branch, dqkv, branch, normed, arrived = fence(
-        to2, away_qkv, theirs_up, d_branch, dqkv, branch, normed, arrived
-    )
-
-    parts2 = scatter_second(to2)
-    theirs_qkv = flip(away_qkv, 1)
-    mine_up = weight_grad(normed, [d_branch], [ff], 0, theirs_up, "up_mine")
-    output = leave_output(x, after(branch, mine_up), arrived, own_f, count)
-    mine_qkv = weight_grad(after(normed, output), list(dqkv), [part] * 3, 0, theirs_qkv, "qkv_mine")
-    d_in, d_normed, mine_up, mine_qkv, output, parts2 = fence(d_in, d_normed, mine_up, mine_qkv, output, parts2)
+    mine_up, theirs_qkv, dqkv, branch, normed, arrived = fence(mine_up, theirs_qkv, dqkv, branch, normed, arrived)
+
+    first_up = scatter_first(mine_up)
+    mine_qkv = weight_grad(normed, list(dqkv), [part] * 3, 0, theirs_qkv, "qkv_mine")
+    first_qkv = scatter_first(mine_qkv)
+    output = leave_output(x, after(branch, mine_qkv[0]), arrived, own_f, count)
+    d_in, d_normed, output, first_up, first_qkv = fence(d_in, d_normed, output, first_up, first_qkv)
     if more >= 2:
         d_in = step(add(block_of(d_normed, 2), d_in).astype(BF), 1)
 
-    first_up, first_qkv = scatter_first(mine_up), scatter_first(mine_qkv)
+    parts_up = scatter_second(scatter_merge(*first_up))
     grad_down, grad_out = finish_grad(parts2, [w_down.shape, w_out.shape], True, "finish_down")
-    d_in, d_normed, grad_down, grad_out = fence(d_in, d_normed, grad_down, grad_out)
+    d_in, d_normed, grad_down, grad_out, parts_up = fence(d_in, d_normed, grad_down, grad_out, parts_up)
     for s in range(3, n):
         d_in = step(add(block_of(d_normed, s), d_in).astype(BF), 1)
-    first_up, first_qkv, d_normed = fence(first_up, first_qkv, d_normed)
 
     parts_qkv = scatter_second(scatter_merge(*first_qkv))
-    parts_up = scatter_second(scatter_merge(*first_up))
-    d_in, d_normed, parts_qkv = fence(d_in, d_normed, parts_qkv)
+    (grad_up,) = finish_grad(parts_up, [w_up.shape], False, "finish_up")
+    d_in, d_normed, parts_qkv, grad_up = fence(d_in, d_normed, parts_qkv, grad_up)
     in_grad, stats = leave_grad(x, g, d_normed, d_in, gain, own_f, count)
     stats = sum_over_tp(stats)
-    stats, parts_up, parts_qkv = fence(stats, parts_up, parts_qkv)
     stats = sum_over_fsdp(stats)
-    (grad_up,) = finish_grad(parts_up, [w_up.shape], False, "finish_up")
-    (grad_qkv,) = finish_grad(parts_qkv, [own_qkv.shape], False, "finish_qkv")
+    (grad_qkv,) = finish_grad(after(parts_qkv, in_grad), [own_qkv.shape], False, "finish_qkv")
     grad_qkv = jnp.swapaxes(grad_qkv, 0, 1)
     return (
         output[None],

time: 387 us -> 380 us (0.982)
  waiting for transfers between devices: 145 us -> 135 us
  Pallas kernels: 154 us -> 160 us
  local copies, waits for them, and re-layouts: 32.5 us -> 26.9 us
  starting transfers between devices: 38.6 us -> 43 us
    ppermute x15 -> x16, waiting for transfers between devices: 87.8 us -> 60.2 us  [step(): return lax.ppermute(array, 'tp', [(i, (i + by) % n) for i in range(n)])]
    ppermute x34, waiting for transfers between devices: 57.1 us -> 74.5 us  [flip(): return lax.ppermute(array, 'fsdp', [(s, s ^ bit) for s in range(count)])]
    unnamed x110 -> x136, local copies, waits for them, and re-layouts: 27.2 us -> 20.6 us
    ppermute x15 -> x16, starting transfers between devices: 6.86 us -> 11.1 us  [step(): return lax.ppermute(array, 'tp', [(i, (i + by) % n) for i in range(n)])]
  transfers between devices with their start and end apart: 49 -> 50, of which waited for: 24 -> 26; matrix products, arithmetic and copies ran while one was open for 6% -> 6% of each run, Pallas kernels for 40% -> 42%
where the time goes in v1:
time: 380 us; the launch traced here: 373 us
  Pallas kernels  160 us (42%)
  waiting for transfers between devices  135 us (36%)
  starting transfers between devices  43 us (11%)
  local copies, waits for them, and re-layouts  26.9 us (7%)
  other arithmetic  6.91 us (2%)
    pallas_call x13, Pallas kernels, product(): pl.pallas_call(body, grid=(steps,), in_specs=specs, out_specs=out_specs,...  115 us
    ppermute x34, waiting for transfers between devices, flip(): return lax.ppermute(array, 'fsdp', [(s, s ^ bit) for s in range(count)])  74.5 us
    ppermute x16, waiting for transfers between devices, step(): return lax.ppermute(array, 'tp', [(i, (i + by) % n) for i in range(n)])  60.2 us
    ppermute x34, starting transfers between devices, flip(): return lax.ppermute(array, 'fsdp', [(s, s ^ bit) for s in range(count)])  31.9 us
    unnamed x136, local copies, waits for them, and re-layouts  20.6 us
    pallas_call x1, Pallas kernels, attend_backward(): pl.pallas_call(functools.partial(attend_backward_kernel, block, count), g...  16.8 us
    pallas_call x1, Pallas kernels, attend_forward(): pl.pallas_call(functools.partial(attend_forward_kernel, block, count), gr...  11.4 us
    ppermute x16, starting transfers between devices, step(): return lax.ppermute(array, 'tp', [(i, (i + by) % n) for i in range(n)])  11.1 us
  transfers between devices with their start and end apart: 50, of which 26 were waited for; matrix products, arithmetic and copies ran while one was open for 6% of the time, Pallas kernels for 42%

profile of v1, /device:TPU:0, one launch (start us, length us, event | category | flops | bytes accessed | tf_op | source)
XLA Modules:
  0.0 373.5 jit_solution(9235790636782866876)
XLA Ops:
  0.6 3.0 collective-permute-start.3
  10.1 1.6 collective-permute-start
  11.7 3.2 fusion.2
  16.1 20.3 %collective-permute-done.refs_1_ = bf16[256,2048]{1,0:T(8,128)(2,1)S(1)} collective-permute-done((bf16[256,2048]{1,0:T(8,128)(2,1)S(1)}, bf16[256,2048]{1,0:T(8,128)(2,1)S(1)}, u32[]{:S(2)}, u32[]{:S(2)}) %collective-permute-start) | collective-permute-done | bytes 1048608 | tf_op jit(solution)/shard_map/ppermute | solution.py:783
  41.4 1.6 collective-permute-start.6
  44.3 21.2 %collective-permute-done.5 = bf16[128,2048]{1,0:T(8,128)(2,1)S(1)} collective-permute-done((bf16[128,2048]{1,0:T(8,128)(2,1)S(1)}, bf16[128,2048]{1,0:T(8,128)(2,1)S(1)}, u32[]{:S(2)}, u32[]{:S(2)}) %collective-permute-start.5) | collective-permute-done | bytes 524320 | tf_op jit(solution)/shard_map/ppermute | solution.py:653
  71.0 6.5 %collective-permute-done.11 = bf16[3,128,512]{2,1,0:T(8,128)(2,1)S(1)} collective-permute-done((bf16[3,128,512]{2,1,0:T(8,128)(2,1)S(1)}, bf16[3,128,512]{2,1,0:T(8,128)(2,1)S(1)}, u32[]{:S(2)}, u32[]{:S(2)}) %collective-permute-start.11) | collective-permute-done | bytes 393248 | tf_op jit(solution)/shard_map/ppermute | solution.py:653
  79.7 13.6 %collective-permute-done.2.refs_3_ = bf16[256,2048]{1,0:T(8,128)(2,1)S(1)} collective-permute-done((bf16[256,2048]{1,0:T(8,128)(2,1)S(1)}, bf16[256,2048]{1,0:T(8,128)(2,1)S(1)}, u32[]{:S(2)}, u32[]{:S(2)}) %collective-permute-start.2) | collective-permute-done | bytes 1048608 | tf_op jit(solution)/shard_map/ppermute | solution.py:783
  93.5 1.6 collective-permute-start.15
  95.6 14.5 %up.1 = (bf16[1024,2048]{1,0:T(8,128)(2,1)S(1)}, bf16[1024,2048]{1,0:T(8,128)(2,1)S(1)}) custom-call(bf16[256,2048]{1,0:T(8,128)(2,1)S(1)} %get-tuple-element.486.refs_0_, bf16[256,2048]{1,0:T(8,128)(2,1)S(1)} %collective-permute-done.refs_1_, bf16[256,2048]{1,0:T(8,128)(2,1)S(1)} %collective-permute-done.1.refs_2_, ...), custom_call_target="tpu_custom_call" | custom-call | flops 1073741824 | bytes 2621440 | tf_op jit(solution)/shard_map/up/pallas_call | solution.py:385
  110.1 1.9 copy-done
  112.1 2.0 copy-done.21
  114.0 6.8 %collective-permute-done.9.refs_1_ = bf16[256,2048]{1,0:T(8,128)(2,1)} collective-permute-done((bf16[256,2048]{1,0:T(8,128)(2,1)S(1)}, bf16[256,2048]{1,0:T(8,128)(2,1)}, u32[]{:S(2)}, u32[]{:S(2)}) %collective-permute-start.9) | collective-permute-done | bytes 1048608 | tf_op jit(solution)/shard_map/ppermute | solution.py:783
  122.3 9.3 %qkv.1.q_in.k_in.v_in = f32[1024,1536]{1,0:T(8,128)S(1)} custom-call(bf16[256,2048]{1,0:T(8,128)(2,1)S(1)} %get-tuple-element.486.refs_0_, bf16[256,2048]{1,0:T(8,128)(2,1)S(1)} %collective-permute-done.refs_1_, bf16[256,2048]{1,0:T(8,128)(2,1)S(1)} %collective-permute-done.1.refs_2_, bf16[256,2048]{1,0:T(8,128)(2,1)S(1)} %copy-done.12, ...), custom_call_target="tpu_custom_call" | custom-call | flops 805306368 | bytes 2097152 | tf_op jit(solution)/shard_map/qkv/pallas_call | solution.py:385
  136.0 11.4 %attend_forward.1 = (bf16[1024,512]{1,0:T(8,128)(2,1)S(1)}, bf16[1024,512]{1,0:T(8,128)(2,1)S(1)}, bf16[1024,512]{1,0:T(8,128)(2,1)S(1)}, bf16[1024,512]{1,0:T(8,128)(2,1)S(1)}, f32[4,8,1024]{2,1,0:T(8,128)S(1)}) custom-call(s32[1]{0:T(128)} %bitcast.6.me_ref, f32[1024,1536]{1,0:T(8,128)S(1)} %qkv.1.q_in.k_in.v_in, f32[1024,1536]{1,0:T(8,128)S(1)} %qkv.1.q_in.k_in.v_in, ...), custom_call_target="tpu_custom_call" | custom-call | flops 1073741824 | bytes 1523712 | tf_op jit(solution)/shard_map/attend_forward/pallas_call | solution.py:257
  147.5 2.5 constant_dynamic-update-slice_fusion.14
  151.5 1.6 constant_dynamic-update-slice_fusion.12
  154.1 6.2 %branch.2.rest_0_ = bf16[1024,2048]{1,0:T(8,128)(2,1)S(1)} custom-call(bf16[1024,2048]{1,0:T(8,128)(2,1)S(1)} %copy-done.1, bf16[1024,512]{1,0:T(8,128)(2,1)S(1)} %get-tuple-element.350.att_ref.refs_5_, bf16[2560,1024]{1,0:T(8,128)(2,1)S(1)} %constant_dynamic-update-slice_fusion.10.w_ref.refs_3_), custom_call_target="tpu_custom_call" | custom-call | flops 671088640 | bytes 1835008 | tf_op jit(solution)/shard_map/branch/pallas_call | solution.py:385
  160.3 2.0 collective-permute-done.20.w_ref.refs_4_
  162.4 6.2 %branch.3.own_ref = bf16[1024,2048]{1,0:T(8,128)(2,1)S(1)} custom-call(bf16[1024,2048]{1,0:T(8,128)(2,1)S(1)} %copy-done.1, bf16[1024,512]{1,0:T(8,128)(2,1)S(1)} %get-tuple-element.350.att_ref.refs_5_, bf16[2560,1024]{1,0:T(8,128)(2,1)S(1)} %collective-permute-done.20.w_ref.refs_4_, ...), custom_call_target="tpu_custom_call", output_to_operand_aliasing={{}: (3, {})} | custom-call | flops 671088640 | bytes 2359296 | tf_op jit(solution)/shard_map/branch/pallas_call | solution.py:385
  168.6 8.6 %d_branch.2.refs_5_ = bf16[1024,2560]{1,0:T(8,128)(2,1)S(1)} custom-call(bf16[256,2048]{1,0:T(8,128)(2,1)S(1)} %copy-done.25, bf16[256,2048]{1,0:T(8,128)(2,1)} %collective-permute-done.9.refs_1_, bf16[1024,2048]{1,0:T(8,128)(2,1)S(1)} %copy-done.22, bf16[2560,1024]{1,0:T(8,128)(2,1)S(1)} %constant_dynamic-update-slice_fusion.10.w_ref.refs_3_, ...), custom_call_target="tpu_custom_call" | custom-call | flops 671088640 | bytes 2752512 | tf_op jit(solution)/shard_map/d_branch/pallas_call | solution.py:385
  177.2 4.3 %collective-permute-done.17.refs_3_.refs_1_ = bf16[256,2048]{1,0:T(8,128)(2,1)S(1)} collective-permute-done((bf16[256,2048]{1,0:T(8,128)(2,1)}, bf16[256,2048]{1,0:T(8,128)(2,1)S(1)}, u32[]{:S(2)}, u32[]{:S(2)}) %collective-permute-start.17) | collective-permute-done | bytes 1048608 | tf_op jit(solution)/shard_map/ppermute | solution.py:783
  181.9 8.9 %down_away.1 = bf16[1024,2560]{1,0:T(8,128)(2,1)} custom-call(bf16[256,2048]{1,0:T(8,128)(2,1)S(1)} %copy-done.25, bf16[256,2048]{1,0:T(8,128)(2,1)} %collective-permute-done.9.refs_1_, bf16[256,2048]{1,0:T(8,128)(2,1)} %collective-permute-done.13.refs_2_.refs_0_, bf16[256,2048]{1,0:T(8,128)(2,1)S(1)} %collective-permute-done.17.refs_3_.refs_1_, ...), custom_call_target="tpu_custom_call" | custom-call | flops 671088640 | bytes 1835008 | tf_op jit(solution)/shard_map/down_away/pallas_call | solution.py:385
  190.9 8.8 %d_branch.3.refs_4_.g_in.du_ref = bf16[1024,2560]{1,0:T(8,128)(2,1)S(1)} custom-call(bf16[256,2048]{1,0:T(8,128)(2,1)} %collective-permute-done.13.refs_2_.refs_0_, bf16[256,2048]{1,0:T(8,128)(2,1)S(1)} %collective-permute-done.17.refs_3_.refs_1_, bf16[1024,2048]{1,0:T(8,128)(2,1)S(1)} %copy-done.23, ...), custom_call_target="tpu_custom_call", output_to_operand_aliasing={{}: (5, {})} | custom-call | flops 671088640 | bytes 3407872 | tf_op jit(solution)/shard_map/d_branch/pallas_call | solution.py:385
  199.9 6.8 %up_away.1 = bf16[1024,2048]{1,0:T(8,128)(2,1)} custom-call(bf16[256,2048]{1,0:T(8,128)(2,1)S(1)} %copy-done.3, bf16[256,2048]{1,0:T(8,128)(2,1)S(1)} %copy-done.6, bf16[256,2048]{1,0:T(8,128)(2,1)S(1)} %copy-done.9, bf16[256,2048]{1,0:T(8,128)(2,1)S(1)} %copy-done.13, bf16[1024,2560]{1,0:T(8,128)(2,1)S(1)} %d_branch.3.refs_4_.g_in.du_ref), custom_call_target="tpu_custom_call" | custom-call | flops 536870912 | bytes 1703936 | tf_op jit(solution)/shard_map/up_away/pallas_call | solution.py:385
  206.7 1.9 collective-permute-done.23.refs_6_
  208.7 8.7 %down_mine.1 = (bf16[256,2560]{1,0:T(8,128)(2,1)S(1)}, bf16[256,2560]{1,0:T(8,128)(2,1)S(1)}, bf16[256,2560]{1,0:T(8,128)(2,1)S(1)}, bf16[128,2560]{1,0:T(8,128)(2,1)S(1)}, bf16[128,2560]{1,0:T(8,128)(2,1)S(1)}) custom-call(bf16[256,2048]{1,0:T(8,128)(2,1)S(1)} %copy-done.26, bf16[256,2048]{1,0:T(8,128)(2,1)} %collective-permute-done.9.refs_1_, ...), custom_call_target="tpu_custom_call" | custom-call | flops 671088640 | bytes 2490368 | tf_op jit(solution)/shard_map/down_mine/pallas_call | solution.py:385
  220.6 16.8 %attend_backward.1 = (bf16[1024,512]{1,0:T(8,128)(2,1)S(1)}, bf16[1024,512]{1,0:T(8,128)(2,1)S(1)}, bf16[1024,512]{1,0:T(8,128)(2,1)S(1)}) custom-call(s32[1]{0:T(128)} %bitcast.6.me_ref, bf16[1024,512]{1,0:T(8,128)(2,1)S(1)} %copy-done.48, bf16[1024,512]{1,0:T(8,128)(2,1)S(1)} %copy-done.50, bf16[1024,512]{1,0:T(8,128)(2,1)S(1)} %copy-done.52, ...), custom_call_target="tpu_custom_call" | custom-call | flops 2684354560 | bytes 1114112 | tf_op jit(solution)/shard_map/attend_backward/pallas_call | solution.py:353
  237.6 1.8 merge.3
  239.6 5.3 %qkv_away.1 = bf16[1024,1536]{1,0:T(8,128)(2,1)} custom-call(bf16[256,2048]{1,0:T(8,128)(2,1)S(1)} %copy-done.3, bf16[256,2048]{1,0:T(8,128)(2,1)S(1)} %copy-done.6, bf16[256,2048]{1,0:T(8,128)(2,1)S(1)} %copy-done.9, bf16[256,2048]{1,0:T(8,128)(2,1)S(1)} %copy-done.14, bf16[1024,512]{1,0:T(8,128)(2,1)S(1)} %get-tuple-element.490.refs_4_.dq_ref, ...), custom_call_target="tpu_custom_call" | custom-call | flops 402653184 | bytes 1310720 | tf_op jit(solution)/shard_map/qkv_away/pallas_call | solution.py:385
  249.1 1.7 collective-permute-start.27
  250.8 19.1 %d_normed.1.own_ref = bf16[1024,2048]{1,0:T(8,128)(2,1)S(1)} custom-call(bf16[1024,2560]{1,0:T(8,128)(2,1)S(1)} %d_branch.3.refs_4_.g_in.du_ref, bf16[1024,512]{1,0:T(8,128)(2,1)S(1)} %get-tuple-element.490.refs_4_.dq_ref, bf16[1024,512]{1,0:T(8,128)(2,1)S(1)} %get-tuple-element.491.refs_5_.dk_ref, bf16[1024,512]{1,0:T(8,128)(2,1)S(1)} %get-tuple-element.492.refs_6_.dv_ref, ...), custom_call_target="tpu_custom_call" | custom-call | flops 1879048192 | bytes 3407872 | tf_op jit(solution)/shard_map/d_normed/pallas_call | solution.py:385
  270.0 6.2 %up_mine.1 = (bf16[256,2048]{1,0:T(8,128)(2,1)S(1)}, bf16[256,2048]{1,0:T(8,128)(2,1)S(1)}, bf16[256,2048]{1,0:T(8,128)(2,1)S(1)}, bf16[128,2048]{1,0:T(8,128)(2,1)S(1)}, bf16[128,2048]{1,0:T(8,128)(2,1)S(1)}) custom-call(bf16[256,2048]{1,0:T(8,128)(2,1)S(1)} %copy-done.4, bf16[256,2048]{1,0:T(8,128)(2,1)S(1)} %copy-done.7, ...), custom_call_target="tpu_custom_call" | custom-call | flops 536870912 | bytes 2228224 | tf_op jit(solution)/shard_map/up_mine/pallas_call | solution.py:385
  277.7 2.4 collective-permute-start.31
  281.4 6.1 %qkv_mine.1 = (bf16[256,1536]{1,0:T(8,128)(2,1)S(1)}, bf16[256,1536]{1,0:T(8,128)(2,1)S(1)}, bf16[256,1536]{1,0:T(8,128)(2,1)S(1)}, bf16[128,1536]{1,0:T(8,128)(2,1)S(1)}, bf16[128,1536]{1,0:T(8,128)(2,1)S(1)}) custom-call(bf16[256,2048]{1,0:T(8,128)(2,1)S(1)} %copy-done.4, bf16[256,2048]{1,0:T(8,128)(2,1)S(1)} %copy-done.7, ...), custom_call_target="tpu_custom_call" | custom-call | flops 402653184 | bytes 1703936 | tf_op jit(solution)/shard_map/qkv_mine/pallas_call | solution.py:385
  290.3 2.6 leave_output.1
  292.9 8.0 %collective-permute-done.35.via_x_ref = bf16[128,1536]{1,0:T(8,128)(2,1)S(1)} collective-permute-done((bf16[128,1536]{1,0:T(8,128)(2,1)S(1)}, bf16[128,1536]{1,0:T(8,128)(2,1)S(1)}, u32[]{:S(2)}, u32[]{:S(2)}) %collective-permute-start.35) | collective-permute-done | bytes 393248 | tf_op jit(solution)/shard_map/ppermute | solution.py:653
  301.3 2.5 collective-permute-done.31
  306.9 3.9 %finish_down.1 = (f32[2048,256]{1,0:T(8,128)}, f32[512,256]{1,0:T(8,128)}) custom-call(bf16[256,2560]{1,0:T(8,128)(2,1)S(1)} %copy-done.46, bf16[256,2560]{1,0:T(8,128)(2,1)} %collective-permute-done.29.refs_1_, bf16[256,2560]{1,0:T(8,128)(2,1)} %collective-permute-done.30.refs_2_), custom_call_target="tpu_custom_call" | custom-call | flops 327680 | bytes 819200 | tf_op jit(solution)/shard_map/finish_down/pallas_call | solution.py:772
  310.8 16.3 %collective-permute-done.38.refs_1_ = bf16[256,2048]{1,0:T(8,128)(2,1)S(1)} collective-permute-done((bf16[256,2048]{1,0:T(8,128)(2,1)S(1)}, bf16[256,2048]{1,0:T(8,128)(2,1)S(1)}, u32[]{:S(2)}, u32[]{:S(2)}) %collective-permute-start.38) | collective-permute-done | bytes 1048608 | tf_op jit(solution)/shard_map/ppermute | solution.py:653
  327.6 3.5 collective-permute-done.37
  333.6 1.7 finish_up.1
  335.2 12.5 %collective-permute-done.41.refs_1_ = bf16[256,1536]{1,0:T(8,128)(2,1)S(1)} collective-permute-done((bf16[256,1536]{1,0:T(8,128)(2,1)S(1)}, bf16[256,1536]{1,0:T(8,128)(2,1)S(1)}, u32[]{:S(2)}, u32[]{:S(2)}) %collective-permute-start.41) | collective-permute-done | bytes 786464 | tf_op jit(solution)/shard_map/ppermute | solution.py:653
  348.2 6.6 %collective-permute-done.40.in_ref = bf16[256,2048]{1,0:T(8,128)(2,1)S(1)} collective-permute-done((bf16[256,2048]{1,0:T(8,128)(2,1)S(1)}, bf16[256,2048]{1,0:T(8,128)(2,1)S(1)}, u32[]{:S(2)}, u32[]{:S(2)}) %collective-permute-start.40) | collective-permute-done | bytes 1048608 | tf_op jit(solution)/shard_map/ppermute | solution.py:783
  354.8 3.9 %leave_grad.1 = (f32[256,2048]{1,0:T(8,128)}, f32[2,2048]{1,0:T(2,128)S(1)}) custom-call(s32[1]{0:T(128)} %bitcast.me_ref, bf16[256,2048]{1,0:T(8,128)(2,1)S(1)} %bitcast.14, bf16[256,2048]{1,0:T(8,128)(2,1)S(1)} %bitcast.16, bf16[1024,2048]{1,0:T(8,128)(2,1)S(1)} %d_normed.1.own_ref, bf16[256,2048]{1,0:T(8,128)(2,1)S(1)} %collective-permute-done.40.in_ref, ...), custom_call_target="tpu_custom_call" | custom-call | flops 1310720 | bytes 788480 | tf_op jit(solution)/shard_map/leave_grad/pallas_call | solution.py:159
  358.9 3.7 collective-permute-start.45
  362.6 1.7 collective-permute-done.43
  367.9 1.8 collective-permute-start.49
  (239 shorter events, 57.9 us)
Async XLA Ops:
  0.6 35.7 %collective-permute-start.3 = (bf16[256,2048]{1,0:T(8,128)(2,1)}, bf16[256,2048]{1,0:T(8,128)(2,1)S(1)}, u32[]{:S(2)}, u32[]{:S(2)}) collective-permute-start(bf16[256,2048]{1,0:T(8,128)(2,1)} %param.13), channel_id=1, source_target_pairs={{0,8},{4,12},{8,0},{12,4},{16,24},{20,28},{24,16},{28,20},{1,9},{5... | collective-permute-start | bytes 3145736 | tf_op jit(solution)/shard_map/ppermute | solution.py:653
  3.6 32.7 %collective-permute-start.4 = (bf16[256,2048]{1,0:T(8,128)(2,1)}, bf16[256,2048]{1,0:T(8,128)(2,1)}, u32[]{:S(2)}, u32[]{:S(2)}) collective-permute-start(bf16[256,2048]{1,0:T(8,128)(2,1)} %param.13), channel_id=1, source_target_pairs={{0,16},{4,20},{8,24},{12,28},{16,0},{20,4},{24,8},{28,12},{1,17},{... | collective-permute-start | bytes 3145736 | tf_op jit(solution)/shard_map/ppermute | solution.py:653
  10.1 26.3 %collective-permute-start = (bf16[256,2048]{1,0:T(8,128)(2,1)S(1)}, bf16[256,2048]{1,0:T(8,128)(2,1)S(1)}, u32[]{:S(2)}, u32[]{:S(2)}) collective-permute-start(bf16[256,2048]{1,0:T(8,128)(2,1)S(1)} %get-tuple-element.486.refs_0_), channel_id=1, source_target_pairs={{0,1},{1,2},{2,3},{3,0},{4,5},{5,6},{6,7},{7,4},{8,9},{9,10},{10,1... | collective-permute-start | bytes 3145736 | tf_op jit(solution)/shard_map/ppermute | solution.py:783
  36.4 29.5 %collective-permute-start.7 = (bf16[3,256,512]{2,1,0:T(8,128)(2,1)S(1)}, bf16[3,256,512]{2,1,0:T(8,128)(2,1)S(1)}, u32[]{:S(2)}, u32[]{:S(2)}) collective-permute-start(bf16[3,256,512]{2,1,0:T(8,128)(2,1)S(1)} %bitcast.22), channel_id=1, source_target_pairs={{0,8},{4,12},{8,0},{12,4},{16,24},{20,28},{24,16},{28,20},{1,9},{5... | collective-permute-start | bytes 2359304 | tf_op jit(solution)/shard_map/ppermute | solution.py:653
  37.0 28.9 %collective-permute-start.8 = (bf16[3,256,512]{2,1,0:T(8,128)(2,1)S(1)}, bf16[3,256,512]{2,1,0:T(8,128)(2,1)S(1)}, u32[]{:S(2)}, u32[]{:S(2)}) collective-permute-start(bf16[3,256,512]{2,1,0:T(8,128)(2,1)S(1)} %bitcast.23), channel_id=1, source_target_pairs={{0,16},{4,20},{8,24},{12,28},{16,0},{20,4},{24,8},{28,12},{1,17},{... | collective-permute-start | bytes 2359304 | tf_op jit(solution)/shard_map/ppermute | solution.py:653
  38.6 27.0 %collective-permute-start.5 = (bf16[128,2048]{1,0:T(8,128)(2,1)S(1)}, bf16[128,2048]{1,0:T(8,128)(2,1)S(1)}, u32[]{:S(2)}, u32[]{:S(2)}) collective-permute-start(bf16[128,2048]{1,0:T(8,128)(2,1)S(1)} %slice.66), channel_id=1, source_target_pairs={{0,8},{4,12},{8,0},{12,4},{16,24},{20,28},{24,16},{28,20},{1,9},{5... | collective-permute-start | bytes 1572872 | tf_op jit(solution)/shard_map/ppermute | solution.py:653
  40.1 25.7 %collective-permute-start.1 = (bf16[256,2048]{1,0:T(8,128)(2,1)S(1)}, bf16[256,2048]{1,0:T(8,128)(2,1)S(1)}, u32[]{:S(2)}, u32[]{:S(2)}) collective-permute-start(bf16[256,2048]{1,0:T(8,128)(2,1)S(1)} %collective-permute-done.refs_1_), channel_id=1, source_target_pairs={{0,1},{1,2},{2,3},{3,0},{4,5},{5,6},{6,7},{7,4},{8,9},{9,10},{10,1... | collective-permute-start | bytes 3145736 | tf_op jit(solution)/shard_map/ppermute | solution.py:783
  41.4 24.4 %collective-permute-start.6 = (bf16[128,2048]{1,0:T(8,128)(2,1)S(1)}, bf16[128,2048]{1,0:T(8,128)(2,1)S(1)}, u32[]{:S(2)}, u32[]{:S(2)}) collective-permute-start(bf16[128,2048]{1,0:T(8,128)(2,1)S(1)} %slice.67), channel_id=1, source_target_pairs={{0,16},{4,20},{8,24},{12,28},{16,0},{20,4},{24,8},{28,12},{1,17},{... | collective-permute-start | bytes 1572872 | tf_op jit(solution)/shard_map/ppermute | solution.py:653
  65.9 27.4 %collective-permute-start.10 = (bf16[1024,2048]{1,0:T(8,128)(2,1)S(1)}, bf16[1024,2048]{1,0:T(8,128)(2,1)S(1)}, u32[]{:S(2)}, u32[]{:S(2)}) collective-permute-start(bf16[1024,2048]{1,0:T(8,128)(2,1)S(1)} %constant_dynamic-update-slice_fusion.refs_4_.um_ref), channel_id=1, source_target_pairs={{0,4},{4,0},{8,12},{12,8},{16,20},{20,16},{24,28},{28,24},{1,5},{5... | collective-permute-start | bytes 12582920 | tf_op jit(solution)/shard_map/ppermute | solution.py:653
  66.0 27.4 %collective-permute-start.2 = (bf16[256,2048]{1,0:T(8,128)(2,1)S(1)}, bf16[256,2048]{1,0:T(8,128)(2,1)S(1)}, u32[]{:S(2)}, u32[]{:S(2)}) collective-permute-start(bf16[256,2048]{1,0:T(8,128)(2,1)S(1)} %collective-permute-done.1.refs_2_), channel_id=1, source_target_pairs={{0,1},{1,2},{2,3},{3,0},{4,5},{5,6},{6,7},{7,4},{8,9},{9,10},{10,1... | collective-permute-start | bytes 3145736 | tf_op jit(solution)/shard_map/ppermute | solution.py:783
  66.1 11.5 %collective-permute-start.11 = (bf16[3,128,512]{2,1,0:T(8,128)(2,1)S(1)}, bf16[3,128,512]{2,1,0:T(8,128)(2,1)S(1)}, u32[]{:S(2)}, u32[]{:S(2)}) collective-permute-start(bf16[3,128,512]{2,1,0:T(8,128)(2,1)S(1)} %slice.68), channel_id=1, source_target_pairs={{0,8},{4,12},{8,0},{12,4},{16,24},{20,28},{24,16},{28,20},{1,9},{5... | collective-permute-start | bytes 1179656 | tf_op jit(solution)/shard_map/ppermute | solution.py:653
  67.7 11.2 %collective-permute-start.12 = (bf16[3,128,512]{2,1,0:T(8,128)(2,1)S(1)}, bf16[3,128,512]{2,1,0:T(8,128)(2,1)S(1)}, u32[]{:S(2)}, u32[]{:S(2)}) collective-permute-start(bf16[3,128,512]{2,1,0:T(8,128)(2,1)S(1)} %slice.69), channel_id=1, source_target_pairs={{0,16},{4,20},{8,24},{12,28},{16,0},{20,4},{24,8},{28,12},{1,17},{... | collective-permute-start | bytes 1179656 | tf_op jit(solution)/shard_map/ppermute | solution.py:653
  93.3 27.7 %collective-permute-start.14 = (bf16[3,1024,512]{2,1,0:T(8,128)(2,1)}, bf16[3,1024,512]{2,1,0:T(8,128)(2,1)}, u32[]{:S(2)}, u32[]{:S(2)}) collective-permute-start(bf16[3,1024,512]{2,1,0:T(8,128)(2,1)} %constant_dynamic-update-slice_fusion.5.refs_4_.qm_ref), channel_id=1, source_target_pairs={{0,4},{4,0},{8,12},{12,8},{16,20},{20,16},{24,28},{28,24},{1,5},{5... | collective-permute-start | bytes 9437192 | tf_op jit(solution)/shard_map/ppermute | solution.py:653
  93.4 27.5 %collective-permute-start.9 = (bf16[256,2048]{1,0:T(8,128)(2,1)S(1)}, bf16[256,2048]{1,0:T(8,128)(2,1)}, u32[]{:S(2)}, u32[]{:S(2)}) collective-permute-start(bf16[256,2048]{1,0:T(8,128)(2,1)S(1)} %get-tuple-element.380.refs_0_), channel_id=1, source_target_pairs={{0,1},{1,2},{2,3},{3,0},{4,5},{5,6},{6,7},{7,4},{8,9},{9,10},{10,1... | collective-permute-start | bytes 3145736 | tf_op jit(solution)/shard_map/ppermute | solution.py:783
  93.5 38.2 %collective-permute-start.15 = (bf16[2560,256]{1,0:T(8,128)(2,1)}, bf16[2560,256]{1,0:T(8,128)(2,1)}, u32[]{:S(2)}, u32[]{:S(2)}) collective-permute-start(bf16[2560,256]{1,0:T(8,128)(2,1)} %pad_maximum_fusion), channel_id=1, source_target_pairs={{0,8},{4,12},{8,0},{12,4},{16,24},{20,28},{24,16},{28,20},{1,9},{5... | collective-permute-start | bytes 3932168 | tf_op jit(solution)/shard_map/ppermute | solution.py:653
  95.1 36.6 %collective-permute-start.16 = (bf16[2560,256]{1,0:T(8,128)(2,1)}, bf16[2560,256]{1,0:T(8,128)(2,1)}, u32[]{:S(2)}, u32[]{:S(2)}) collective-permute-start(bf16[2560,256]{1,0:T(8,128)(2,1)} %pad_maximum_fusion), channel_id=1, source_target_pairs={{0,16},{4,20},{8,24},{12,28},{16,0},{20,4},{24,8},{28,12},{1,17},{... | collective-permute-start | bytes 3932168 | tf_op jit(solution)/shard_map/ppermute | solution.py:653
  120.9 29.1 %collective-permute-start.13 = (bf16[256,2048]{1,0:T(8,128)(2,1)}, bf16[256,2048]{1,0:T(8,128)(2,1)}, u32[]{:S(2)}, u32[]{:S(2)}) collective-permute-start(bf16[256,2048]{1,0:T(8,128)(2,1)} %collective-permute-done.9.refs_1_), channel_id=1, source_target_pairs={{0,1},{1,2},{2,3},{3,0},{4,5},{5,6},{6,7},{7,4},{8,9},{9,10},{10,1... | collective-permute-start | bytes 3145736 | tf_op jit(solution)/shard_map/ppermute | solution.py:783
  132.8 20.4 %collective-permute-start.18 = (bf16[2560,128]{1,0:T(8,128)(2,1)S(1)}, bf16[2560,128]{1,0:T(8,128)(2,1)S(1)}, u32[]{:S(2)}, u32[]{:S(2)}) collective-permute-start(bf16[2560,128]{1,0:T(8,128)(2,1)S(1)} %slice.70), channel_id=1, source_target_pairs={{0,8},{4,12},{8,0},{12,4},{16,24},{20,28},{24,16},{28,20},{1,9},{5... | collective-permute-start | bytes 1966088 | tf_op jit(solution)/shard_map/ppermute | solution.py:653
  135.5 17.9 %collective-permute-start.19 = (bf16[2560,128]{1,0:T(8,128)(2,1)S(1)}, bf16[2560,128]{1,0:T(8,128)(2,1)S(1)}, u32[]{:S(2)}, u32[]{:S(2)}) collective-permute-start(bf16[2560,128]{1,0:T(8,128)(2,1)S(1)} %slice.71), channel_id=1, source_target_pairs={{0,16},{4,20},{8,24},{12,28},{16,0},{20,4},{24,8},{28,12},{1,17},{... | collective-permute-start | bytes 1966088 | tf_op jit(solution)/shard_map/ppermute | solution.py:653
  153.6 8.7 %collective-permute-start.20 = (bf16[2560,1024]{1,0:T(8,128)(2,1)S(1)}, bf16[2560,1024]{1,0:T(8,128)(2,1)S(1)}, u32[]{:S(2)}, u32[]{:S(2)}) collective-permute-start(bf16[2560,1024]{1,0:T(8,128)(2,1)S(1)} %constant_dynamic-update-slice_fusion.10.w_ref.refs_3_), channel_id=1, source_target_pairs={{0,4},{4,0},{8,12},{12,8},{16,20},{20,16},{24,28},{28,24},{1,5},{5... | collective-permute-start | bytes 15728648 | tf_op jit(solution)/shard_map/ppermute | solution.py:653
  153.7 27.8 %collective-permute-start.17 = (bf16[256,2048]{1,0:T(8,128)(2,1)}, bf16[256,2048]{1,0:T(8,128)(2,1)S(1)}, u32[]{:S(2)}, u32[]{:S(2)}) collective-permute-start(bf16[256,2048]{1,0:T(8,128)(2,1)} %collective-permute-done.13.refs_2_.refs_0_), channel_id=1, source_target_pairs={{0,1},{1,2},{2,3},{3,0},{4,5},{5,6},{6,7},{7,4},{8,9},{9,10},{10,1... | collective-permute-start | bytes 3145736 | tf_op jit(solution)/shard_map/ppermute | solution.py:783
  181.6 18.0 %collective-permute-start.21 = (bf16[256,1024]{1,0:T(8,128)(2,1)S(1)}, bf16[256,1024]{1,0:T(8,128)(2,1)S(1)}, u32[]{:S(2)}, u32[]{:S(2)}) collective-permute-start(bf16[256,1024]{1,0:T(8,128)(2,1)S(1)} %get-tuple-element.547), channel_id=1, source_target_pairs={{0,1},{1,2},{2,3},{3,0},{4,5},{5,6},{6,7},{7,4},{8,9},{9,10},{10,1... | collective-permute-start | bytes 1572872 | tf_op jit(solution)/shard_map/ppermute | solution.py:783
  199.7 8.9 %collective-permute-start.23 = (bf16[1024,2560]{1,0:T(8,128)(2,1)}, bf16[1024,2560]{1,0:T(8,128)(2,1)S(1)}, u32[]{:S(2)}, u32[]{:S(2)}) collective-permute-start(bf16[1024,2560]{1,0:T(8,128)(2,1)} %down_away.1), channel_id=1, source_target_pairs={{0,4},{4,0},{8,12},{12,8},{16,20},{20,16},{24,28},{28,24},{1,5},{5... | collective-permute-start | bytes 15728648 | tf_op jit(solution)/shard_map/ppermute | solution.py:653
  199.8 17.7 %collective-permute-start.22 = (bf16[256,1024]{1,0:T(8,128)(2,1)S(1)}, bf16[256,1024]{1,0:T(8,128)(2,1)S(1)}, u32[]{:S(2)}, u32[]{:S(2)}) collective-permute-start(bf16[256,1024]{1,0:T(8,128)(2,1)S(1)} %get-tuple-element.366), channel_id=1, source_target_pairs={{0,1},{1,2},{2,3},{3,0},{4,5},{5,6},{6,7},{7,4},{8,9},{9,10},{10,1... | collective-permute-start | bytes 1572872 | tf_op jit(solution)/shard_map/ppermute | solution.py:783
  217.8 27.3 %collective-permute-start.24 = (bf16[256,2048]{1,0:T(8,128)(2,1)S(1)}, bf16[256,2048]{1,0:T(8,128)(2,1)S(1)}, u32[]{:S(2)}, u32[]{:S(2)}) collective-permute-start(bf16[256,2048]{1,0:T(8,128)(2,1)S(1)} %add_convert_fusion.3), channel_id=1, source_target_pairs={{0,1},{1,2},{2,3},{3,0},{4,5},{5,6},{6,7},{7,4},{8,9},{9,10},{10,1... | collective-permute-start | bytes 3145736 | tf_op jit(solution)/shard_map/ppermute | solution.py:783
  218.5 19.0 %collective-permute-start.25 = (bf16[128,2560]{1,0:T(8,128)(2,1)S(1)}, bf16[128,2560]{1,0:T(8,128)(2,1)S(1)}, u32[]{:S(2)}, u32[]{:S(2)}) collective-permute-start(bf16[128,2560]{1,0:T(8,128)(2,1)S(1)} %get-tuple-element.420), channel_id=1, source_target_pairs={{0,8},{4,12},{8,0},{12,4},{16,24},{20,28},{24,16},{28,20},{1,9},{5... | collective-permute-start | bytes 1966088 | tf_op jit(solution)/shard_map/ppermute | solution.py:653
  219.3 18.2 %collective-permute-start.26 = (bf16[128,2560]{1,0:T(8,128)(2,1)S(1)}, bf16[128,2560]{1,0:T(8,128)(2,1)S(1)}, u32[]{:S(2)}, u32[]{:S(2)}) collective-permute-start(bf16[128,2560]{1,0:T(8,128)(2,1)S(1)} %get-tuple-element.421), channel_id=1, source_target_pairs={{0,16},{4,20},{8,24},{12,28},{16,0},{20,4},{24,8},{28,12},{1,17},{... | collective-permute-start | bytes 1966088 | tf_op jit(solution)/shard_map/ppermute | solution.py:653
  245.1 24.8 %collective-permute-start.28 = (bf16[1024,2048]{1,0:T(8,128)(2,1)}, bf16[1024,2048]{1,0:T(8,128)(2,1)S(1)}, u32[]{:S(2)}, u32[]{:S(2)}) collective-permute-start(bf16[1024,2048]{1,0:T(8,128)(2,1)} %up_away.1), channel_id=1, source_target_pairs={{0,4},{4,0},{8,12},{12,8},{16,20},{20,16},{24,28},{28,24},{1,5},{5... | collective-permute-start | bytes 12582920 | tf_op jit(solution)/shard_map/ppermute | solution.py:653
  245.1 35.0 %collective-permute-start.32 = (bf16[1024,1536]{1,0:T(8,128)(2,1)}, bf16[1024,1536]{1,0:T(8,128)(2,1)S(1)}, u32[]{:S(2)}, u32[]{:S(2)}) collective-permute-start(bf16[1024,1536]{1,0:T(8,128)(2,1)} %qkv_away.1), channel_id=1, source_target_pairs={{0,4},{4,0},{8,12},{12,8},{16,20},{20,16},{24,28},{28,24},{1,5},{5... | collective-permute-start | bytes 9437192 | tf_op jit(solution)/shard_map/ppermute | solution.py:653
  245.7 31.0 %collective-permute-start.29 = (bf16[256,2560]{1,0:T(8,128)(2,1)}, bf16[256,2560]{1,0:T(8,128)(2,1)}, u32[]{:S(2)}, u32[]{:S(2)}) collective-permute-start(bf16[256,2560]{1,0:T(8,128)(2,1)} %get-tuple-element.474), channel_id=1, source_target_pairs={{0,8},{4,12},{8,0},{12,4},{16,24},{20,28},{24,16},{28,20},{1,9},{5... | collective-permute-start | bytes 3932168 | tf_op jit(solution)/shard_map/ppermute | solution.py:653
  246.9 30.7 %collective-permute-start.30 = (bf16[256,2560]{1,0:T(8,128)(2,1)}, bf16[256,2560]{1,0:T(8,128)(2,1)}, u32[]{:S(2)}, u32[]{:S(2)}) collective-permute-start(bf16[256,2560]{1,0:T(8,128)(2,1)} %get-tuple-element.475), channel_id=1, source_target_pairs={{0,16},{4,20},{8,24},{12,28},{16,0},{20,4},{24,8},{28,12},{1,17},{... | collective-permute-start | bytes 3932168 | tf_op jit(solution)/shard_map/ppermute | solution.py:653
  249.1 27.1 %collective-permute-start.27 = (bf16[256,2048]{1,0:T(8,128)(2,1)}, bf16[256,2048]{1,0:T(8,128)(2,1)}, u32[]{:S(2)}, u32[]{:S(2)}) collective-permute-start(bf16[256,2048]{1,0:T(8,128)(2,1)} %add_convert_fusion.2), channel_id=1, source_target_pairs={{0,1},{1,2},{2,3},{3,0},{4,5},{5,6},{6,7},{7,4},{8,9},{9,10},{10,1... | collective-permute-start | bytes 3145736 | tf_op jit(solution)/shard_map/ppermute | solution.py:783
  277.7 26.0 %collective-permute-start.31 = (bf16[256,2048]{1,0:T(8,128)(2,1)S(1)}, bf16[256,2048]{1,0:T(8,128)(2,1)S(1)}, u32[]{:S(2)}, u32[]{:S(2)}) collective-permute-start(bf16[256,2048]{1,0:T(8,128)(2,1)S(1)} %slice.76), channel_id=1, source_target_pairs={{0,1},{1,2},{2,3},{3,0},{4,5},{5,6},{6,7},{7,4},{8,9},{9,10},{10,1... | collective-permute-start | bytes 3145736 | tf_op jit(solution)/shard_map/ppermute | solution.py:783
  280.1 21.1 %collective-permute-start.33 = (bf16[128,2048]{1,0:T(8,128)(2,1)S(1)}, bf16[128,2048]{1,0:T(8,128)(2,1)S(1)}, u32[]{:S(2)}, u32[]{:S(2)}) collective-permute-start(bf16[128,2048]{1,0:T(8,128)(2,1)S(1)} %get-tuple-element.500), channel_id=1, source_target_pairs={{0,8},{4,12},{8,0},{12,4},{16,24},{20,28},{24,16},{28,20},{1,9},{5... | collective-permute-start | bytes 1572872 | tf_op jit(solution)/shard_map/ppermute | solution.py:653
  280.7 20.6 %collective-permute-start.34 = (bf16[128,2048]{1,0:T(8,128)(2,1)S(1)}, bf16[128,2048]{1,0:T(8,128)(2,1)S(1)}, u32[]{:S(2)}, u32[]{:S(2)}) collective-permute-start(bf16[128,2048]{1,0:T(8,128)(2,1)S(1)} %get-tuple-element.501), channel_id=1, source_target_pairs={{0,16},{4,20},{8,24},{12,28},{16,0},{20,4},{24,8},{28,12},{1,17},{... | collective-permute-start | bytes 1572872 | tf_op jit(solution)/shard_map/ppermute | solution.py:653
  287.5 13.5 %collective-permute-start.35 = (bf16[128,1536]{1,0:T(8,128)(2,1)S(1)}, bf16[128,1536]{1,0:T(8,128)(2,1)S(1)}, u32[]{:S(2)}, u32[]{:S(2)}) collective-permute-start(bf16[128,1536]{1,0:T(8,128)(2,1)S(1)} %get-tuple-element.504), channel_id=1, source_target_pairs={{0,8},{4,12},{8,0},{12,4},{16,24},{20,28},{24,16},{28,20},{1,9},{5... | collective-permute-start | bytes 1179656 | tf_op jit(solution)/shard_map/ppermute | solution.py:653
  288.8 12.5 %collective-permute-start.36 = (bf16[128,1536]{1,0:T(8,128)(2,1)S(1)}, bf16[128,1536]{1,0:T(8,128)(2,1)S(1)}, u32[]{:S(2)}, u32[]{:S(2)}) collective-permute-start(bf16[128,1536]{1,0:T(8,128)(2,1)S(1)} %get-tuple-element.505), channel_id=1, source_target_pairs={{0,16},{4,20},{8,24},{12,28},{16,0},{20,4},{24,8},{28,12},{1,17},{... | collective-permute-start | bytes 1179656 | tf_op jit(solution)/shard_map/ppermute | solution.py:653
  304.0 23.0 %collective-permute-start.38 = (bf16[256,2048]{1,0:T(8,128)(2,1)S(1)}, bf16[256,2048]{1,0:T(8,128)(2,1)S(1)}, u32[]{:S(2)}, u32[]{:S(2)}) collective-permute-start(bf16[256,2048]{1,0:T(8,128)(2,1)S(1)} %get-tuple-element.519), channel_id=1, source_target_pairs={{0,8},{4,12},{8,0},{12,4},{16,24},{20,28},{24,16},{28,20},{1,9},{5... | collective-permute-start | bytes 3145736 | tf_op jit(solution)/shard_map/ppermute | solution.py:653
  304.9 22.7 %collective-permute-start.39 = (bf16[256,2048]{1,0:T(8,128)(2,1)S(1)}, bf16[256,2048]{1,0:T(8,128)(2,1)S(1)}, u32[]{:S(2)}, u32[]{:S(2)}) collective-permute-start(bf16[256,2048]{1,0:T(8,128)(2,1)S(1)} %get-tuple-element.520), channel_id=1, source_target_pairs={{0,16},{4,20},{8,24},{12,28},{16,0},{20,4},{24,8},{28,12},{1,17},{... | collective-permute-start | bytes 3145736 | tf_op jit(solution)/shard_map/ppermute | solution.py:653
  306.9 24.3 %collective-permute-start.37 = (bf16[256,2048]{1,0:T(8,128)(2,1)S(1)}, bf16[256,2048]{1,0:T(8,128)(2,1)S(1)}, u32[]{:S(2)}, u32[]{:S(2)}) collective-permute-start(bf16[256,2048]{1,0:T(8,128)(2,1)S(1)} %add_convert_fusion.1), channel_id=1, source_target_pairs={{0,1},{1,2},{2,3},{3,0},{4,5},{5,6},{6,7},{7,4},{8,9},{9,10},{10,1... | collective-permute-start | bytes 3145736 | tf_op jit(solution)/shard_map/ppermute | solution.py:783
  331.5 23.3 %collective-permute-start.40 = (bf16[256,2048]{1,0:T(8,128)(2,1)S(1)}, bf16[256,2048]{1,0:T(8,128)(2,1)S(1)}, u32[]{:S(2)}, u32[]{:S(2)}) collective-permute-start(bf16[256,2048]{1,0:T(8,128)(2,1)S(1)} %add_convert_fusion), channel_id=1, source_target_pairs={{0,1},{1,2},{2,3},{3,0},{4,5},{5,6},{6,7},{7,4},{8,9},{9,10},{10,1... | collective-permute-start | bytes 3145736 | tf_op jit(solution)/shard_map/ppermute | solution.py:783
  331.8 15.9 %collective-permute-start.41 = (bf16[256,1536]{1,0:T(8,128)(2,1)S(1)}, bf16[256,1536]{1,0:T(8,128)(2,1)S(1)}, u32[]{:S(2)}, u32[]{:S(2)}) collective-permute-start(bf16[256,1536]{1,0:T(8,128)(2,1)S(1)} %get-tuple-element.528), channel_id=1, source_target_pairs={{0,8},{4,12},{8,0},{12,4},{16,24},{20,28},{24,16},{28,20},{1,9},{5... | collective-permute-start | bytes 2359304 | tf_op jit(solution)/shard_map/ppermute | solution.py:653
  332.6 15.7 %collective-permute-start.42 = (bf16[256,1536]{1,0:T(8,128)(2,1)S(1)}, bf16[256,1536]{1,0:T(8,128)(2,1)S(1)}, u32[]{:S(2)}, u32[]{:S(2)}) collective-permute-start(bf16[256,1536]{1,0:T(8,128)(2,1)S(1)} %get-tuple-element.529), channel_id=1, source_target_pairs={{0,16},{4,20},{8,24},{12,28},{16,0},{20,4},{24,8},{28,12},{1,17},{... | collective-permute-start | bytes 2359304 | tf_op jit(solution)/shard_map/ppermute | solution.py:653
  358.7 5.5 %collective-permute-start.43 = (f32[2,2048]{1,0:T(2,128)S(1)}, f32[2,2048]{1,0:T(2,128)S(1)}, u32[]{:S(2)}, u32[]{:S(2)}) collective-permute-start(f32[2,2048]{1,0:T(2,128)S(1)} %get-tuple-element.536), channel_id=1, source_target_pairs={{0,1},{1,2},{2,3},{3,0},{4,5},{5,6},{6,7},{7,4},{8,9},{9,10},{10,1... | collective-permute-start | bytes 49160 | tf_op jit(solution)/shard_map/ppermute | solution.py:783
  358.7 5.5 %collective-permute-start.44 = (f32[2,2048]{1,0:T(2,128)S(1)}, f32[2,2048]{1,0:T(2,128)S(1)}, u32[]{:S(2)}, u32[]{:S(2)}) collective-permute-start(f32[2,2048]{1,0:T(2,128)S(1)} %get-tuple-element.536), channel_id=1, source_target_pairs={{0,2},{1,3},{2,0},{3,1},{4,6},{5,7},{6,4},{7,5},{8,10},{9,11},{10,... | collective-permute-start | bytes 49160 | tf_op jit(solution)/shard_map/ppermute | solution.py:783
  358.9 6.0 %collective-permute-start.45 = (f32[2,2048]{1,0:T(2,128)S(1)}, f32[2,2048]{1,0:T(2,128)S(1)}, u32[]{:S(2)}, u32[]{:S(2)}) collective-permute-start(f32[2,2048]{1,0:T(2,128)S(1)} %get-tuple-element.536), channel_id=1, source_target_pairs={{0,3},{1,0},{2,1},{3,2},{4,7},{5,4},{6,5},{7,6},{8,11},{9,8},{10,9... | collective-permute-start | bytes 49160 | tf_op jit(solution)/shard_map/ppermute | solution.py:783
  366.1 5.0 %collective-permute-start.47 = (f32[2,256]{1,0:T(2,128)S(1)}, f32[2,256]{1,0:T(2,128)S(1)}, u32[]{:S(2)}, u32[]{:S(2)}) collective-permute-start(f32[2,256]{1,0:T(2,128)S(1)} %get-tuple-element.548), channel_id=1, source_target_pairs={{0,8},{4,12},{8,0},{12,4},{16,24},{20,28},{24,16},{28,20},{1,9},{5... | collective-permute-start | bytes 6152 | tf_op jit(solution)/shard_map/ppermute | solution.py:653
  367.9 4.5 %collective-permute-start.49 = (f32[2,256]{1,0:T(2,128)S(1)}, f32[2,256]{1,0:T(2,128)S(1)}, u32[]{:S(2)}, u32[]{:S(2)}) collective-permute-start(f32[2,256]{1,0:T(2,128)S(1)} %get-tuple-element.549), channel_id=1, source_target_pairs={{0,24},{4,28},{8,16},{12,20},{16,8},{20,12},{24,0},{28,4},{1,25},{... | collective-permute-start | bytes 6152 | tf_op jit(solution)/shard_map/ppermute | solution.py:653
  (64 other events, 959.9 us)

commit v2 on v1

--- a/solution.py
+++ b/solution.py
@@ -126,7 +126,59 @@
     )(me, x, part, arrived)
 
 
-def leave_grad_kernel(count, me_ref, x_ref, cot_ref, own_ref, in_ref, gain_ref, out_ref, stats_ref, d_ref, xhat_ref):
+def standardize_kernel(count, me_ref, x_ref, out_ref, row_ref):
+    x = x_ref[...].astype(F32)
+    centered = x - jnp.mean(x, axis=-1, keepdims=True)
+    row_ref[...] = centered * lax.rsqrt(jnp.mean(centered * centered, axis=-1, keepdims=True) + 1e-05)
+    size = x.shape[1] // count
+    for place, r in enumerate(place_order(count)):
+        at = pl.ds(pl.multiple_of((me_ref[0] ^ r) * size, size), size)
+        out_ref[:, place * size : (place + 1) * size] = row_ref[:, at]
+
+
+def standardize(x, me, count):
+    whole = pl.BlockSpec(x.shape, lambda j, me: (0, 0))
+    shape = jax.ShapeDtypeStruct(x.shape, F32)
+    return pl.pallas_call(
+        functools.partial(standardize_kernel, count),
+        grid_spec=pltpu.PrefetchScalarGridSpec(
+            num_scalar_prefetch=1,
+            grid=(1,),
+            in_specs=[whole],
+            out_specs=whole,
+            scratch_shapes=[pltpu.VMEM(x.shape, F32)],
+        ),
+        out_shape=shape,
+        compiler_params=params(),
+        cost_estimate=cost(8 * x.size, [x], [shape]),
+        name="standardize",
+    )(me, x)
+
+
+def norm_sums_kernel(xhat_ref, own_ref, in_ref, out_ref):
+    d = own_ref[...].astype(F32) + in_ref[...].astype(F32)
+    out_ref[0:1, :] = jnp.sum(d * xhat_ref[...], axis=0, keepdims=True)
+    out_ref[1:2, :] = jnp.sum(d, axis=0, keepdims=True)
+
+
+def norm_sums(xhat, part, arrived):
+    rows, width = xhat.shape
+    tile = min(512, width)
+    spec = pl.BlockSpec((rows, tile), lambda j: (0, j))
+    shape = jax.ShapeDtypeStruct((2, width), F32)
+    return pl.pallas_call(
+        norm_sums_kernel,
+        grid=(width // tile,),
+        in_specs=[spec] * 3,
+        out_specs=pl.BlockSpec((2, tile), lambda j: (0, j)),
+        out_shape=shape,
+        compiler_params=params(),
+        cost_estimate=cost(4 * xhat.size, [xhat, arrived, arrived], [shape]),
+        name="norm_sums",
+    )(xhat, part, arrived)
+
+
+def leave_grad_kernel(count, me_ref, x_ref, cot_ref, own_ref, in_ref, gain_ref, out_ref, d_ref):
     size = x_ref.shape[1] // count
     for place, r in enumerate(place_order(count)):
         at = pl.ds(pl.multiple_of((me_ref[0] ^ r) * size, size), size)
@@ -136,14 +188,7 @@
     centered = x - jnp.mean(x, axis=-1, keepdims=True)
     inverse = lax.rsqrt(jnp.mean(centered * centered, axis=-1, keepdims=True) + 1e-05)
     xhat = centered * inverse
-    d = d_ref[...]
-    xhat_ref[...] = xhat
-    for place, r in enumerate(place_order(count)):
-        at = pl.ds(pl.multiple_of((me_ref[0] ^ r) * size, size), size)
-        here = slice(place * size, (place + 1) * size)
-        stats_ref[0:1, here] = jnp.sum(d_ref[:, at] * xhat_ref[:, at], axis=0, keepdims=True)
-        stats_ref[1:2, here] = jnp.sum(d_ref[:, at], axis=0, keepdims=True)
-    d_hat = d * gain_ref[...]
+    d_hat = d_ref[...] * gain_ref[...]
     out_ref[...] = cot_ref[...].astype(F32) + inverse * (
         d_hat
         - jnp.mean(d_hat, axis=-1, keepdims=True)
@@ -154,20 +199,19 @@
 def leave_grad(x, cot, part, arrived, gain, me, count):
     whole = pl.BlockSpec(x.shape, lambda j, me: (0, 0))
     line = pl.BlockSpec((1, x.shape[1]), lambda j, me: (0, 0))
-    two = pl.BlockSpec((2, x.shape[1]), lambda j, me: (0, 0))
-    shapes = [jax.ShapeDtypeStruct(x.shape, F32), jax.ShapeDtypeStruct((2, x.shape[1]), F32)]
+    shape = jax.ShapeDtypeStruct(x.shape, F32)
     return pl.pallas_call(
         functools.partial(leave_grad_kernel, count),
         grid_spec=pltpu.PrefetchScalarGridSpec(
             num_scalar_prefetch=1,
             grid=(1,),
             in_specs=[whole] * 4 + [line],
-            out_specs=[whole, two],
-            scratch_shapes=[pltpu.VMEM(x.shape, F32)] * 2,
+            out_specs=whole,
+            scratch_shapes=[pltpu.VMEM(x.shape, F32)],
         ),
-        out_shape=shapes,
+        out_shape=shape,
         compiler_params=params(),
-        cost_estimate=cost(20 * x.size, [x, cot, x, arrived], shapes),
+        cost_estimate=cost(20 * x.size, [x, cot, x, arrived], [shape]),
         name="leave_grad",
     )(me, x, cot, part, arrived, gain[None])
 
@@ -934,11 +978,13 @@
 
     parts_qkv = scatter_second(scatter_merge(*first_qkv))
     (grad_up,) = finish_grad(parts_up, [w_up.shape], False, "finish_up")
-    d_in, d_normed, parts_qkv, grad_up = fence(d_in, d_normed, parts_qkv, grad_up)
-    in_grad, stats = leave_grad(x, g, d_normed, d_in, gain, own_f, count)
-    stats = sum_over_tp(stats)
+    xhat = standardize(after(x, grad_up), own_f, count)
+    (grad_qkv,) = finish_grad(parts_qkv, [own_qkv.shape], False, "finish_qkv")
+    d_in, d_normed, grad_qkv, grad_up, xhat = fence(d_in, d_normed, grad_qkv, grad_up, xhat)
+    stats = norm_sums(xhat, d_normed, d_in)
+    in_grad = leave_grad(x, g, d_normed, after(d_in, stats), gain, own_f, count)
+    stats, in_grad = fence(sum_over_tp(stats), in_grad)
     stats = sum_over_fsdp(stats)
-    (grad_qkv,) = finish_grad(after(parts_qkv, in_grad), [own_qkv.shape], False, "finish_qkv")
     grad_qkv = jnp.swapaxes(grad_qkv, 0, 1)
     return (
         output[None],

time: 380 us -> 378 us (level)
    ppermute x16, waiting for transfers between devices: 60.2 us -> 54.1 us  [step(): return lax.ppermute(array, 'tp', [(i, (i + by) % n) for i in range(n)])]
  transfers between devices with their start and end apart: 50 -> 50, of which waited for: 26 -> 26; matrix products, arithmetic and copies ran while one was open for 6% -> 6% of each run, Pallas kernels for 42% -> 43%
where the time goes in v2:
time: 378 us; the launch traced here: 371 us
  Pallas kernels  161 us (43%)
  waiting for transfers between devices  132 us (35%)
  starting transfers between devices  43 us (11%)
  local copies, waits for them, and re-layouts  27 us (7%)
  other arithmetic  6.91 us (2%)
    pallas_call x13, Pallas kernels, product(): pl.pallas_call(body, grid=(steps,), in_specs=specs, out_specs=out_specs,...  115 us
    ppermute x34, waiting for transfers between devices, flip(): return lax.ppermute(array, 'fsdp', [(s, s ^ bit) for s in range(count)])  77.5 us
    ppermute x16, waiting for transfers between devices, step(): return lax.ppermute(array, 'tp', [(i, (i + by) % n) for i in range(n)])  54.1 us
    ppermute x34, starting transfers between devices, flip(): return lax.ppermute(array, 'fsdp', [(s, s ^ bit) for s in range(count)])  31.9 us
    unnamed x136, local copies, waits for them, and re-layouts  20.6 us
    pallas_call x1, Pallas kernels, attend_backward(): pl.pallas_call(functools.partial(attend_backward_kernel, block, count), g...  16.8 us
    pallas_call x1, Pallas kernels, attend_forward(): pl.pallas_call(functools.partial(attend_forward_kernel, block, count), gr...  11.4 us
    ppermute x16, starting transfers between devices, step(): return lax.ppermute(array, 'tp', [(i, (i + by) % n) for i in range(n)])  11.1 us
  transfers between devices with their start and end apart: 50, of which 26 were waited for; matrix products, arithmetic and copies ran while one was open for 6% of the time, Pallas kernels for 43%

profile of v2, /device:TPU:0, one launch (start us, length us, event | category | flops | bytes accessed | tf_op | source)
XLA Modules:
  0.0 371.4 jit_solution(2215959632788265527)
XLA Ops:
  0.6 3.0 collective-permute-start.3
  10.1 1.6 collective-permute-start
  11.7 3.2 fusion.2
  16.1 20.3 %collective-permute-done.refs_1_ = bf16[256,2048]{1,0:T(8,128)(2,1)S(1)} collective-permute-done((bf16[256,2048]{1,0:T(8,128)(2,1)S(1)}, bf16[256,2048]{1,0:T(8,128)(2,1)S(1)}, u32[]{:S(2)}, u32[]{:S(2)}) %collective-permute-start) | collective-permute-done | bytes 1048608 | tf_op jit(solution)/shard_map/ppermute | solution.py:827
  41.4 1.6 collective-permute-start.6
  44.3 21.2 %collective-permute-done.5 = bf16[128,2048]{1,0:T(8,128)(2,1)S(1)} collective-permute-done((bf16[128,2048]{1,0:T(8,128)(2,1)S(1)}, bf16[128,2048]{1,0:T(8,128)(2,1)S(1)}, u32[]{:S(2)}, u32[]{:S(2)}) %collective-permute-start.5) | collective-permute-done | bytes 524320 | tf_op jit(solution)/shard_map/ppermute | solution.py:697
  71.0 6.5 %collective-permute-done.11 = bf16[3,128,512]{2,1,0:T(8,128)(2,1)S(1)} collective-permute-done((bf16[3,128,512]{2,1,0:T(8,128)(2,1)S(1)}, bf16[3,128,512]{2,1,0:T(8,128)(2,1)S(1)}, u32[]{:S(2)}, u32[]{:S(2)}) %collective-permute-start.11) | collective-permute-done | bytes 393248 | tf_op jit(solution)/shard_map/ppermute | solution.py:697
  79.7 13.6 %collective-permute-done.2.refs_3_ = bf16[256,2048]{1,0:T(8,128)(2,1)S(1)} collective-permute-done((bf16[256,2048]{1,0:T(8,128)(2,1)S(1)}, bf16[256,2048]{1,0:T(8,128)(2,1)S(1)}, u32[]{:S(2)}, u32[]{:S(2)}) %collective-permute-start.2) | collective-permute-done | bytes 1048608 | tf_op jit(solution)/shard_map/ppermute | solution.py:827
  93.5 1.6 collective-permute-start.15
  95.6 14.5 %up.1 = (bf16[1024,2048]{1,0:T(8,128)(2,1)S(1)}, bf16[1024,2048]{1,0:T(8,128)(2,1)S(1)}) custom-call(bf16[256,2048]{1,0:T(8,128)(2,1)S(1)} %get-tuple-element.484.refs_0_, bf16[256,2048]{1,0:T(8,128)(2,1)S(1)} %collective-permute-done.refs_1_, bf16[256,2048]{1,0:T(8,128)(2,1)S(1)} %collective-permute-done.1.refs_2_, ...), custom_call_target="tpu_custom_call" | custom-call | flops 1073741824 | bytes 2621440 | tf_op jit(solution)/shard_map/up/pallas_call | solution.py:429
  110.1 1.9 copy-done
  112.1 2.0 copy-done.21
  114.0 6.8 %collective-permute-done.9.refs_1_ = bf16[256,2048]{1,0:T(8,128)(2,1)} collective-permute-done((bf16[256,2048]{1,0:T(8,128)(2,1)S(1)}, bf16[256,2048]{1,0:T(8,128)(2,1)}, u32[]{:S(2)}, u32[]{:S(2)}) %collective-permute-start.9) | collective-permute-done | bytes 1048608 | tf_op jit(solution)/shard_map/ppermute | solution.py:827
  122.3 9.3 %qkv.1.q_in.k_in.v_in = f32[1024,1536]{1,0:T(8,128)S(1)} custom-call(bf16[256,2048]{1,0:T(8,128)(2,1)S(1)} %get-tuple-element.484.refs_0_, bf16[256,2048]{1,0:T(8,128)(2,1)S(1)} %collective-permute-done.refs_1_, bf16[256,2048]{1,0:T(8,128)(2,1)S(1)} %collective-permute-done.1.refs_2_, bf16[256,2048]{1,0:T(8,128)(2,1)S(1)} %copy-done.12, ...), custom_call_target="tpu_custom_call" | custom-call | flops 805306368 | bytes 2097152 | tf_op jit(solution)/shard_map/qkv/pallas_call | solution.py:429
  136.0 11.4 %attend_forward.1 = (bf16[1024,512]{1,0:T(8,128)(2,1)S(1)}, bf16[1024,512]{1,0:T(8,128)(2,1)S(1)}, bf16[1024,512]{1,0:T(8,128)(2,1)S(1)}, bf16[1024,512]{1,0:T(8,128)(2,1)S(1)}, f32[4,8,1024]{2,1,0:T(8,128)S(1)}) custom-call(s32[1]{0:T(128)} %bitcast.6.me_ref, f32[1024,1536]{1,0:T(8,128)S(1)} %qkv.1.q_in.k_in.v_in, f32[1024,1536]{1,0:T(8,128)S(1)} %qkv.1.q_in.k_in.v_in, ...), custom_call_target="tpu_custom_call" | custom-call | flops 1073741824 | bytes 1523712 | tf_op jit(solution)/shard_map/attend_forward/pallas_call | solution.py:301
  147.5 2.5 constant_dynamic-update-slice_fusion.14
  151.5 1.6 constant_dynamic-update-slice_fusion.12
  154.1 6.2 %branch.2.rest_0_ = bf16[1024,2048]{1,0:T(8,128)(2,1)S(1)} custom-call(bf16[1024,2048]{1,0:T(8,128)(2,1)S(1)} %copy-done.1, bf16[1024,512]{1,0:T(8,128)(2,1)S(1)} %get-tuple-element.348.att_ref.refs_5_, bf16[2560,1024]{1,0:T(8,128)(2,1)S(1)} %constant_dynamic-update-slice_fusion.10.w_ref.refs_3_), custom_call_target="tpu_custom_call" | custom-call | flops 671088640 | bytes 1835008 | tf_op jit(solution)/shard_map/branch/pallas_call | solution.py:429
  160.3 2.0 collective-permute-done.20.w_ref.refs_4_
  162.4 6.2 %branch.3.own_ref = bf16[1024,2048]{1,0:T(8,128)(2,1)S(1)} custom-call(bf16[1024,2048]{1,0:T(8,128)(2,1)S(1)} %copy-done.1, bf16[1024,512]{1,0:T(8,128)(2,1)S(1)} %get-tuple-element.348.att_ref.refs_5_, bf16[2560,1024]{1,0:T(8,128)(2,1)S(1)} %collective-permute-done.20.w_ref.refs_4_, ...), custom_call_target="tpu_custom_call", output_to_operand_aliasing={{}: (3, {})} | custom-call | flops 671088640 | bytes 2359296 | tf_op jit(solution)/shard_map/branch/pallas_call | solution.py:429
  168.6 8.6 %d_branch.2.refs_5_ = bf16[1024,2560]{1,0:T(8,128)(2,1)S(1)} custom-call(bf16[256,2048]{1,0:T(8,128)(2,1)S(1)} %copy-done.27, bf16[256,2048]{1,0:T(8,128)(2,1)} %collective-permute-done.9.refs_1_, bf16[1024,2048]{1,0:T(8,128)(2,1)S(1)} %copy-done.22, bf16[2560,1024]{1,0:T(8,128)(2,1)S(1)} %constant_dynamic-update-slice_fusion.10.w_ref.refs_3_, ...), custom_call_target="tpu_custom_call" | custom-call | flops 671088640 | bytes 2752512 | tf_op jit(solution)/shard_map/d_branch/pallas_call | solution.py:429
  177.2 4.3 %collective-permute-done.17.refs_3_.refs_1_ = bf16[256,2048]{1,0:T(8,128)(2,1)S(1)} collective-permute-done((bf16[256,2048]{1,0:T(8,128)(2,1)}, bf16[256,2048]{1,0:T(8,128)(2,1)S(1)}, u32[]{:S(2)}, u32[]{:S(2)}) %collective-permute-start.17) | collective-permute-done | bytes 1048608 | tf_op jit(solution)/shard_map/ppermute | solution.py:827
  181.9 8.9 %down_away.1 = bf16[1024,2560]{1,0:T(8,128)(2,1)} custom-call(bf16[256,2048]{1,0:T(8,128)(2,1)S(1)} %copy-done.27, bf16[256,2048]{1,0:T(8,128)(2,1)} %collective-permute-done.9.refs_1_, bf16[256,2048]{1,0:T(8,128)(2,1)} %collective-permute-done.13.refs_2_.refs_0_, bf16[256,2048]{1,0:T(8,128)(2,1)S(1)} %collective-permute-done.17.refs_3_.refs_1_, ...), custom_call_target="tpu_custom_call" | custom-call | flops 671088640 | bytes 1835008 | tf_op jit(solution)/shard_map/down_away/pallas_call | solution.py:429
  190.9 8.8 %d_branch.3.refs_4_.g_in.du_ref = bf16[1024,2560]{1,0:T(8,128)(2,1)S(1)} custom-call(bf16[256,2048]{1,0:T(8,128)(2,1)} %collective-permute-done.13.refs_2_.refs_0_, bf16[256,2048]{1,0:T(8,128)(2,1)S(1)} %collective-permute-done.17.refs_3_.refs_1_, bf16[1024,2048]{1,0:T(8,128)(2,1)S(1)} %copy-done.23, ...), custom_call_target="tpu_custom_call", output_to_operand_aliasing={{}: (5, {})} | custom-call | flops 671088640 | bytes 3407872 | tf_op jit(solution)/shard_map/d_branch/pallas_call | solution.py:429
  199.9 6.8 %up_away.1 = bf16[1024,2048]{1,0:T(8,128)(2,1)} custom-call(bf16[256,2048]{1,0:T(8,128)(2,1)S(1)} %copy-done.3, bf16[256,2048]{1,0:T(8,128)(2,1)S(1)} %copy-done.6, bf16[256,2048]{1,0:T(8,128)(2,1)S(1)} %copy-done.9, bf16[256,2048]{1,0:T(8,128)(2,1)S(1)} %copy-done.13, bf16[1024,2560]{1,0:T(8,128)(2,1)S(1)} %d_branch.3.refs_4_.g_in.du_ref), custom_call_target="tpu_custom_call" | custom-call | flops 536870912 | bytes 1703936 | tf_op jit(solution)/shard_map/up_away/pallas_call | solution.py:429
  206.7 2.0 collective-permute-done.23.refs_6_
  208.7 8.7 %down_mine.1 = (bf16[256,2560]{1,0:T(8,128)(2,1)S(1)}, bf16[256,2560]{1,0:T(8,128)(2,1)S(1)}, bf16[256,2560]{1,0:T(8,128)(2,1)S(1)}, bf16[128,2560]{1,0:T(8,128)(2,1)S(1)}, bf16[128,2560]{1,0:T(8,128)(2,1)S(1)}) custom-call(bf16[256,2048]{1,0:T(8,128)(2,1)S(1)} %copy-done.28, bf16[256,2048]{1,0:T(8,128)(2,1)} %collective-permute-done.9.refs_1_, ...), custom_call_target="tpu_custom_call" | custom-call | flops 671088640 | bytes 2490368 | tf_op jit(solution)/shard_map/down_mine/pallas_call | solution.py:429
  220.8 16.8 %attend_backward.1 = (bf16[1024,512]{1,0:T(8,128)(2,1)S(1)}, bf16[1024,512]{1,0:T(8,128)(2,1)S(1)}, bf16[1024,512]{1,0:T(8,128)(2,1)S(1)}) custom-call(s32[1]{0:T(128)} %bitcast.6.me_ref, bf16[1024,512]{1,0:T(8,128)(2,1)S(1)} %copy-done.48, bf16[1024,512]{1,0:T(8,128)(2,1)S(1)} %copy-done.50, bf16[1024,512]{1,0:T(8,128)(2,1)S(1)} %copy-done.52, ...), custom_call_target="tpu_custom_call" | custom-call | flops 2684354560 | bytes 1114112 | tf_op jit(solution)/shard_map/attend_backward/pallas_call | solution.py:397
  237.7 1.8 merge.3
  239.7 5.3 %qkv_away.1 = bf16[1024,1536]{1,0:T(8,128)(2,1)} custom-call(bf16[256,2048]{1,0:T(8,128)(2,1)S(1)} %copy-done.3, bf16[256,2048]{1,0:T(8,128)(2,1)S(1)} %copy-done.6, bf16[256,2048]{1,0:T(8,128)(2,1)S(1)} %copy-done.9, bf16[256,2048]{1,0:T(8,128)(2,1)S(1)} %copy-done.14, bf16[1024,512]{1,0:T(8,128)(2,1)S(1)} %get-tuple-element.488.refs_4_.dq_ref, ...), custom_call_target="tpu_custom_call" | custom-call | flops 402653184 | bytes 1310720 | tf_op jit(solution)/shard_map/qkv_away/pallas_call | solution.py:429
  249.3 1.7 collective-permute-start.27
  251.0 19.1 %d_normed.1.own_ref = bf16[1024,2048]{1,0:T(8,128)(2,1)S(1)} custom-call(bf16[1024,2560]{1,0:T(8,128)(2,1)S(1)} %d_branch.3.refs_4_.g_in.du_ref, bf16[1024,512]{1,0:T(8,128)(2,1)S(1)} %get-tuple-element.488.refs_4_.dq_ref, bf16[1024,512]{1,0:T(8,128)(2,1)S(1)} %get-tuple-element.489.refs_5_.dk_ref, bf16[1024,512]{1,0:T(8,128)(2,1)S(1)} %get-tuple-element.490.refs_6_.dv_ref, ...), custom_call_target="tpu_custom_call" | custom-call | flops 1879048192 | bytes 3407872 | tf_op jit(solution)/shard_map/d_normed/pallas_call | solution.py:429
  270.1 6.2 %up_mine.1 = (bf16[256,2048]{1,0:T(8,128)(2,1)S(1)}, bf16[256,2048]{1,0:T(8,128)(2,1)S(1)}, bf16[256,2048]{1,0:T(8,128)(2,1)S(1)}, bf16[128,2048]{1,0:T(8,128)(2,1)S(1)}, bf16[128,2048]{1,0:T(8,128)(2,1)S(1)}) custom-call(bf16[256,2048]{1,0:T(8,128)(2,1)S(1)} %copy-done.4, bf16[256,2048]{1,0:T(8,128)(2,1)S(1)} %copy-done.7, ...), custom_call_target="tpu_custom_call" | custom-call | flops 536870912 | bytes 2228224 | tf_op jit(solution)/shard_map/up_mine/pallas_call | solution.py:429
  277.8 2.3 collective-permute-start.31
  281.4 6.0 %qkv_mine.1 = (bf16[256,1536]{1,0:T(8,128)(2,1)S(1)}, bf16[256,1536]{1,0:T(8,128)(2,1)S(1)}, bf16[256,1536]{1,0:T(8,128)(2,1)S(1)}, bf16[128,1536]{1,0:T(8,128)(2,1)S(1)}, bf16[128,1536]{1,0:T(8,128)(2,1)S(1)}) custom-call(bf16[256,2048]{1,0:T(8,128)(2,1)S(1)} %copy-done.4, bf16[256,2048]{1,0:T(8,128)(2,1)S(1)} %copy-done.7, ...), custom_call_target="tpu_custom_call" | custom-call | flops 402653184 | bytes 1703936 | tf_op jit(solution)/shard_map/qkv_mine/pallas_call | solution.py:429
  290.3 2.6 leave_output.1
  292.9 8.0 %collective-permute-done.35.via_x_ref = bf16[128,1536]{1,0:T(8,128)(2,1)S(1)} collective-permute-done((bf16[128,1536]{1,0:T(8,128)(2,1)S(1)}, bf16[128,1536]{1,0:T(8,128)(2,1)S(1)}, u32[]{:S(2)}, u32[]{:S(2)}) %collective-permute-start.35) | collective-permute-done | bytes 393248 | tf_op jit(solution)/shard_map/ppermute | solution.py:697
  301.3 2.5 collective-permute-done.31
  307.0 3.9 %finish_down.1 = (f32[2048,256]{1,0:T(8,128)}, f32[512,256]{1,0:T(8,128)}) custom-call(bf16[256,2560]{1,0:T(8,128)(2,1)S(1)} %copy-done.46, bf16[256,2560]{1,0:T(8,128)(2,1)} %collective-permute-done.29.refs_1_, bf16[256,2560]{1,0:T(8,128)(2,1)} %collective-permute-done.30.refs_2_), custom_call_target="tpu_custom_call" | custom-call | flops 327680 | bytes 819200 | tf_op jit(solution)/shard_map/finish_down/pallas_call | solution.py:816
  310.8 16.3 %collective-permute-done.38.refs_1_ = bf16[256,2048]{1,0:T(8,128)(2,1)S(1)} collective-permute-done((bf16[256,2048]{1,0:T(8,128)(2,1)S(1)}, bf16[256,2048]{1,0:T(8,128)(2,1)S(1)}, u32[]{:S(2)}, u32[]{:S(2)}) %collective-permute-start.38) | collective-permute-done | bytes 1048608 | tf_op jit(solution)/shard_map/ppermute | solution.py:697
  327.7 3.5 collective-permute-done.37
  333.6 14.2 %collective-permute-done.41.refs_1_ = bf16[256,1536]{1,0:T(8,128)(2,1)S(1)} collective-permute-done((bf16[256,1536]{1,0:T(8,128)(2,1)S(1)}, bf16[256,1536]{1,0:T(8,128)(2,1)S(1)}, u32[]{:S(2)}, u32[]{:S(2)}) %collective-permute-start.41) | collective-permute-done | bytes 786464 | tf_op jit(solution)/shard_map/ppermute | solution.py:697
  349.6 1.7 finish_up.1
  352.1 2.8 collective-permute-done.40.in_ref
  357.4 2.5 collective-permute-start.45
  359.9 3.2 leave_grad.1
  366.1 1.8 collective-permute-start.49
  368.8 1.8 collective-permute-done.49
  (241 shorter events, 60.2 us)
Async XLA Ops:
  0.6 35.7 %collective-permute-start.3 = (bf16[256,2048]{1,0:T(8,128)(2,1)}, bf16[256,2048]{1,0:T(8,128)(2,1)S(1)}, u32[]{:S(2)}, u32[]{:S(2)}) collective-permute-start(bf16[256,2048]{1,0:T(8,128)(2,1)} %param.13), channel_id=1, source_target_pairs={{0,8},{4,12},{8,0},{12,4},{16,24},{20,28},{24,16},{28,20},{1,9},{5... | collective-permute-start | bytes 3145736 | tf_op jit(solution)/shard_map/ppermute | solution.py:697
  3.6 32.7 %collective-permute-start.4 = (bf16[256,2048]{1,0:T(8,128)(2,1)}, bf16[256,2048]{1,0:T(8,128)(2,1)}, u32[]{:S(2)}, u32[]{:S(2)}) collective-permute-start(bf16[256,2048]{1,0:T(8,128)(2,1)} %param.13), channel_id=1, source_target_pairs={{0,16},{4,20},{8,24},{12,28},{16,0},{20,4},{24,8},{28,12},{1,17},{... | collective-permute-start | bytes 3145736 | tf_op jit(solution)/shard_map/ppermute | solution.py:697
  10.1 26.3 %collective-permute-start = (bf16[256,2048]{1,0:T(8,128)(2,1)S(1)}, bf16[256,2048]{1,0:T(8,128)(2,1)S(1)}, u32[]{:S(2)}, u32[]{:S(2)}) collective-permute-start(bf16[256,2048]{1,0:T(8,128)(2,1)S(1)} %get-tuple-element.484.refs_0_), channel_id=1, source_target_pairs={{0,1},{1,2},{2,3},{3,0},{4,5},{5,6},{6,7},{7,4},{8,9},{9,10},{10,1... | collective-permute-start | bytes 3145736 | tf_op jit(solution)/shard_map/ppermute | solution.py:827
  36.4 29.5 %collective-permute-start.7 = (bf16[3,256,512]{2,1,0:T(8,128)(2,1)S(1)}, bf16[3,256,512]{2,1,0:T(8,128)(2,1)S(1)}, u32[]{:S(2)}, u32[]{:S(2)}) collective-permute-start(bf16[3,256,512]{2,1,0:T(8,128)(2,1)S(1)} %bitcast.24), channel_id=1, source_target_pairs={{0,8},{4,12},{8,0},{12,4},{16,24},{20,28},{24,16},{28,20},{1,9},{5... | collective-permute-start | bytes 2359304 | tf_op jit(solution)/shard_map/ppermute | solution.py:697
  37.0 28.9 %collective-permute-start.8 = (bf16[3,256,512]{2,1,0:T(8,128)(2,1)S(1)}, bf16[3,256,512]{2,1,0:T(8,128)(2,1)S(1)}, u32[]{:S(2)}, u32[]{:S(2)}) collective-permute-start(bf16[3,256,512]{2,1,0:T(8,128)(2,1)S(1)} %bitcast.25), channel_id=1, source_target_pairs={{0,16},{4,20},{8,24},{12,28},{16,0},{20,4},{24,8},{28,12},{1,17},{... | collective-permute-start | bytes 2359304 | tf_op jit(solution)/shard_map/ppermute | solution.py:697
  38.6 27.0 %collective-permute-start.5 = (bf16[128,2048]{1,0:T(8,128)(2,1)S(1)}, bf16[128,2048]{1,0:T(8,128)(2,1)S(1)}, u32[]{:S(2)}, u32[]{:S(2)}) collective-permute-start(bf16[128,2048]{1,0:T(8,128)(2,1)S(1)} %slice.66), channel_id=1, source_target_pairs={{0,8},{4,12},{8,0},{12,4},{16,24},{20,28},{24,16},{28,20},{1,9},{5... | collective-permute-start | bytes 1572872 | tf_op jit(solution)/shard_map/ppermute | solution.py:697
  40.1 25.7 %collective-permute-start.1 = (bf16[256,2048]{1,0:T(8,128)(2,1)S(1)}, bf16[256,2048]{1,0:T(8,128)(2,1)S(1)}, u32[]{:S(2)}, u32[]{:S(2)}) collective-permute-start(bf16[256,2048]{1,0:T(8,128)(2,1)S(1)} %collective-permute-done.refs_1_), channel_id=1, source_target_pairs={{0,1},{1,2},{2,3},{3,0},{4,5},{5,6},{6,7},{7,4},{8,9},{9,10},{10,1... | collective-permute-start | bytes 3145736 | tf_op jit(solution)/shard_map/ppermute | solution.py:827
  41.4 24.4 %collective-permute-start.6 = (bf16[128,2048]{1,0:T(8,128)(2,1)S(1)}, bf16[128,2048]{1,0:T(8,128)(2,1)S(1)}, u32[]{:S(2)}, u32[]{:S(2)}) collective-permute-start(bf16[128,2048]{1,0:T(8,128)(2,1)S(1)} %slice.67), channel_id=1, source_target_pairs={{0,16},{4,20},{8,24},{12,28},{16,0},{20,4},{24,8},{28,12},{1,17},{... | collective-permute-start | bytes 1572872 | tf_op jit(solution)/shard_map/ppermute | solution.py:697
  65.9 27.4 %collective-permute-start.10 = (bf16[1024,2048]{1,0:T(8,128)(2,1)S(1)}, bf16[1024,2048]{1,0:T(8,128)(2,1)S(1)}, u32[]{:S(2)}, u32[]{:S(2)}) collective-permute-start(bf16[1024,2048]{1,0:T(8,128)(2,1)S(1)} %constant_dynamic-update-slice_fusion.refs_4_.um_ref), channel_id=1, source_target_pairs={{0,4},{4,0},{8,12},{12,8},{16,20},{20,16},{24,28},{28,24},{1,5},{5... | collective-permute-start | bytes 12582920 | tf_op jit(solution)/shard_map/ppermute | solution.py:697
  66.0 27.4 %collective-permute-start.2 = (bf16[256,2048]{1,0:T(8,128)(2,1)S(1)}, bf16[256,2048]{1,0:T(8,128)(2,1)S(1)}, u32[]{:S(2)}, u32[]{:S(2)}) collective-permute-start(bf16[256,2048]{1,0:T(8,128)(2,1)S(1)} %collective-permute-done.1.refs_2_), channel_id=1, source_target_pairs={{0,1},{1,2},{2,3},{3,0},{4,5},{5,6},{6,7},{7,4},{8,9},{9,10},{10,1... | collective-permute-start | bytes 3145736 | tf_op jit(solution)/shard_map/ppermute | solution.py:827
  66.1 11.5 %collective-permute-start.11 = (bf16[3,128,512]{2,1,0:T(8,128)(2,1)S(1)}, bf16[3,128,512]{2,1,0:T(8,128)(2,1)S(1)}, u32[]{:S(2)}, u32[]{:S(2)}) collective-permute-start(bf16[3,128,512]{2,1,0:T(8,128)(2,1)S(1)} %slice.68), channel_id=1, source_target_pairs={{0,8},{4,12},{8,0},{12,4},{16,24},{20,28},{24,16},{28,20},{1,9},{5... | collective-permute-start | bytes 1179656 | tf_op jit(solution)/shard_map/ppermute | solution.py:697
  67.7 11.2 %collective-permute-start.12 = (bf16[3,128,512]{2,1,0:T(8,128)(2,1)S(1)}, bf16[3,128,512]{2,1,0:T(8,128)(2,1)S(1)}, u32[]{:S(2)}, u32[]{:S(2)}) collective-permute-start(bf16[3,128,512]{2,1,0:T(8,128)(2,1)S(1)} %slice.69), channel_id=1, source_target_pairs={{0,16},{4,20},{8,24},{12,28},{16,0},{20,4},{24,8},{28,12},{1,17},{... | collective-permute-start | bytes 1179656 | tf_op jit(solution)/shard_map/ppermute | solution.py:697
  93.3 27.7 %collective-permute-start.14 = (bf16[3,1024,512]{2,1,0:T(8,128)(2,1)}, bf16[3,1024,512]{2,1,0:T(8,128)(2,1)}, u32[]{:S(2)}, u32[]{:S(2)}) collective-permute-start(bf16[3,1024,512]{2,1,0:T(8,128)(2,1)} %constant_dynamic-update-slice_fusion.5.refs_4_.qm_ref), channel_id=1, source_target_pairs={{0,4},{4,0},{8,12},{12,8},{16,20},{20,16},{24,28},{28,24},{1,5},{5... | collective-permute-start | bytes 9437192 | tf_op jit(solution)/shard_map/ppermute | solution.py:697
  93.4 27.5 %collective-permute-start.9 = (bf16[256,2048]{1,0:T(8,128)(2,1)S(1)}, bf16[256,2048]{1,0:T(8,128)(2,1)}, u32[]{:S(2)}, u32[]{:S(2)}) collective-permute-start(bf16[256,2048]{1,0:T(8,128)(2,1)S(1)} %get-tuple-element.378.refs_0_), channel_id=1, source_target_pairs={{0,1},{1,2},{2,3},{3,0},{4,5},{5,6},{6,7},{7,4},{8,9},{9,10},{10,1... | collective-permute-start | bytes 3145736 | tf_op jit(solution)/shard_map/ppermute | solution.py:827
  93.5 38.2 %collective-permute-start.15 = (bf16[2560,256]{1,0:T(8,128)(2,1)}, bf16[2560,256]{1,0:T(8,128)(2,1)}, u32[]{:S(2)}, u32[]{:S(2)}) collective-permute-start(bf16[2560,256]{1,0:T(8,128)(2,1)} %pad_maximum_fusion), channel_id=1, source_target_pairs={{0,8},{4,12},{8,0},{12,4},{16,24},{20,28},{24,16},{28,20},{1,9},{5... | collective-permute-start | bytes 3932168 | tf_op jit(solution)/shard_map/ppermute | solution.py:697
  95.1 36.6 %collective-permute-start.16 = (bf16[2560,256]{1,0:T(8,128)(2,1)}, bf16[2560,256]{1,0:T(8,128)(2,1)}, u32[]{:S(2)}, u32[]{:S(2)}) collective-permute-start(bf16[2560,256]{1,0:T(8,128)(2,1)} %pad_maximum_fusion), channel_id=1, source_target_pairs={{0,16},{4,20},{8,24},{12,28},{16,0},{20,4},{24,8},{28,12},{1,17},{... | collective-permute-start | bytes 3932168 | tf_op jit(solution)/shard_map/ppermute | solution.py:697
  120.9 29.1 %collective-permute-start.13 = (bf16[256,2048]{1,0:T(8,128)(2,1)}, bf16[256,2048]{1,0:T(8,128)(2,1)}, u32[]{:S(2)}, u32[]{:S(2)}) collective-permute-start(bf16[256,2048]{1,0:T(8,128)(2,1)} %collective-permute-done.9.refs_1_), channel_id=1, source_target_pairs={{0,1},{1,2},{2,3},{3,0},{4,5},{5,6},{6,7},{7,4},{8,9},{9,10},{10,1... | collective-permute-start | bytes 3145736 | tf_op jit(solution)/shard_map/ppermute | solution.py:827
  132.8 20.4 %collective-permute-start.18 = (bf16[2560,128]{1,0:T(8,128)(2,1)S(1)}, bf16[2560,128]{1,0:T(8,128)(2,1)S(1)}, u32[]{:S(2)}, u32[]{:S(2)}) collective-permute-start(bf16[2560,128]{1,0:T(8,128)(2,1)S(1)} %slice.70), channel_id=1, source_target_pairs={{0,8},{4,12},{8,0},{12,4},{16,24},{20,28},{24,16},{28,20},{1,9},{5... | collective-permute-start | bytes 1966088 | tf_op jit(solution)/shard_map/ppermute | solution.py:697
  135.5 17.9 %collective-permute-start.19 = (bf16[2560,128]{1,0:T(8,128)(2,1)S(1)}, bf16[2560,128]{1,0:T(8,128)(2,1)S(1)}, u32[]{:S(2)}, u32[]{:S(2)}) collective-permute-start(bf16[2560,128]{1,0:T(8,128)(2,1)S(1)} %slice.71), channel_id=1, source_target_pairs={{0,16},{4,20},{8,24},{12,28},{16,0},{20,4},{24,8},{28,12},{1,17},{... | collective-permute-start | bytes 1966088 | tf_op jit(solution)/shard_map/ppermute | solution.py:697
  153.6 8.7 %collective-permute-start.20 = (bf16[2560,1024]{1,0:T(8,128)(2,1)S(1)}, bf16[2560,1024]{1,0:T(8,128)(2,1)S(1)}, u32[]{:S(2)}, u32[]{:S(2)}) collective-permute-start(bf16[2560,1024]{1,0:T(8,128)(2,1)S(1)} %constant_dynamic-update-slice_fusion.10.w_ref.refs_3_), channel_id=1, source_target_pairs={{0,4},{4,0},{8,12},{12,8},{16,20},{20,16},{24,28},{28,24},{1,5},{5... | collective-permute-start | bytes 15728648 | tf_op jit(solution)/shard_map/ppermute | solution.py:697
  153.7 27.8 %collective-permute-start.17 = (bf16[256,2048]{1,0:T(8,128)(2,1)}, bf16[256,2048]{1,0:T(8,128)(2,1)S(1)}, u32[]{:S(2)}, u32[]{:S(2)}) collective-permute-start(bf16[256,2048]{1,0:T(8,128)(2,1)} %collective-permute-done.13.refs_2_.refs_0_), channel_id=1, source_target_pairs={{0,1},{1,2},{2,3},{3,0},{4,5},{5,6},{6,7},{7,4},{8,9},{9,10},{10,1... | collective-permute-start | bytes 3145736 | tf_op jit(solution)/shard_map/ppermute | solution.py:827
  181.6 18.0 %collective-permute-start.21 = (bf16[256,1024]{1,0:T(8,128)(2,1)S(1)}, bf16[256,1024]{1,0:T(8,128)(2,1)S(1)}, u32[]{:S(2)}, u32[]{:S(2)}) collective-permute-start(bf16[256,1024]{1,0:T(8,128)(2,1)S(1)} %get-tuple-element.543), channel_id=1, source_target_pairs={{0,1},{1,2},{2,3},{3,0},{4,5},{5,6},{6,7},{7,4},{8,9},{9,10},{10,1... | collective-permute-start | bytes 1572872 | tf_op jit(solution)/shard_map/ppermute | solution.py:827
  199.7 8.9 %collective-permute-start.23 = (bf16[1024,2560]{1,0:T(8,128)(2,1)}, bf16[1024,2560]{1,0:T(8,128)(2,1)S(1)}, u32[]{:S(2)}, u32[]{:S(2)}) collective-permute-start(bf16[1024,2560]{1,0:T(8,128)(2,1)} %down_away.1), channel_id=1, source_target_pairs={{0,4},{4,0},{8,12},{12,8},{16,20},{20,16},{24,28},{28,24},{1,5},{5... | collective-permute-start | bytes 15728648 | tf_op jit(solution)/shard_map/ppermute | solution.py:697
  199.8 17.7 %collective-permute-start.22 = (bf16[256,1024]{1,0:T(8,128)(2,1)S(1)}, bf16[256,1024]{1,0:T(8,128)(2,1)S(1)}, u32[]{:S(2)}, u32[]{:S(2)}) collective-permute-start(bf16[256,1024]{1,0:T(8,128)(2,1)S(1)} %get-tuple-element.364), channel_id=1, source_target_pairs={{0,1},{1,2},{2,3},{3,0},{4,5},{5,6},{6,7},{7,4},{8,9},{9,10},{10,1... | collective-permute-start | bytes 1572872 | tf_op jit(solution)/shard_map/ppermute | solution.py:827
  217.9 27.5 %collective-permute-start.24 = (bf16[256,2048]{1,0:T(8,128)(2,1)S(1)}, bf16[256,2048]{1,0:T(8,128)(2,1)S(1)}, u32[]{:S(2)}, u32[]{:S(2)}) collective-permute-start(bf16[256,2048]{1,0:T(8,128)(2,1)S(1)} %add_convert_fusion.3), channel_id=1, source_target_pairs={{0,1},{1,2},{2,3},{3,0},{4,5},{5,6},{6,7},{7,4},{8,9},{9,10},{10,1... | collective-permute-start | bytes 3145736 | tf_op jit(solution)/shard_map/ppermute | solution.py:827
  218.7 19.0 %collective-permute-start.25 = (bf16[128,2560]{1,0:T(8,128)(2,1)S(1)}, bf16[128,2560]{1,0:T(8,128)(2,1)S(1)}, u32[]{:S(2)}, u32[]{:S(2)}) collective-permute-start(bf16[128,2560]{1,0:T(8,128)(2,1)S(1)} %get-tuple-element.418), channel_id=1, source_target_pairs={{0,8},{4,12},{8,0},{12,4},{16,24},{20,28},{24,16},{28,20},{1,9},{5... | collective-permute-start | bytes 1966088 | tf_op jit(solution)/shard_map/ppermute | solution.py:697
  219.5 18.2 %collective-permute-start.26 = (bf16[128,2560]{1,0:T(8,128)(2,1)S(1)}, bf16[128,2560]{1,0:T(8,128)(2,1)S(1)}, u32[]{:S(2)}, u32[]{:S(2)}) collective-permute-start(bf16[128,2560]{1,0:T(8,128)(2,1)S(1)} %get-tuple-element.419), channel_id=1, source_target_pairs={{0,16},{4,20},{8,24},{12,28},{16,0},{20,4},{24,8},{28,12},{1,17},{... | collective-permute-start | bytes 1966088 | tf_op jit(solution)/shard_map/ppermute | solution.py:697
  245.3 24.8 %collective-permute-start.28 = (bf16[1024,2048]{1,0:T(8,128)(2,1)}, bf16[1024,2048]{1,0:T(8,128)(2,1)S(1)}, u32[]{:S(2)}, u32[]{:S(2)}) collective-permute-start(bf16[1024,2048]{1,0:T(8,128)(2,1)} %up_away.1), channel_id=1, source_target_pairs={{0,4},{4,0},{8,12},{12,8},{16,20},{20,16},{24,28},{28,24},{1,5},{5... | collective-permute-start | bytes 12582920 | tf_op jit(solution)/shard_map/ppermute | solution.py:697
  245.3 34.8 %collective-permute-start.32 = (bf16[1024,1536]{1,0:T(8,128)(2,1)}, bf16[1024,1536]{1,0:T(8,128)(2,1)S(1)}, u32[]{:S(2)}, u32[]{:S(2)}) collective-permute-start(bf16[1024,1536]{1,0:T(8,128)(2,1)} %qkv_away.1), channel_id=1, source_target_pairs={{0,4},{4,0},{8,12},{12,8},{16,20},{20,16},{24,28},{28,24},{1,5},{5... | collective-permute-start | bytes 9437192 | tf_op jit(solution)/shard_map/ppermute | solution.py:697
  245.8 31.0 %collective-permute-start.29 = (bf16[256,2560]{1,0:T(8,128)(2,1)}, bf16[256,2560]{1,0:T(8,128)(2,1)}, u32[]{:S(2)}, u32[]{:S(2)}) collective-permute-start(bf16[256,2560]{1,0:T(8,128)(2,1)} %get-tuple-element.472), channel_id=1, source_target_pairs={{0,8},{4,12},{8,0},{12,4},{16,24},{20,28},{24,16},{28,20},{1,9},{5... | collective-permute-start | bytes 3932168 | tf_op jit(solution)/shard_map/ppermute | solution.py:697
  247.0 30.7 %collective-permute-start.30 = (bf16[256,2560]{1,0:T(8,128)(2,1)}, bf16[256,2560]{1,0:T(8,128)(2,1)}, u32[]{:S(2)}, u32[]{:S(2)}) collective-permute-start(bf16[256,2560]{1,0:T(8,128)(2,1)} %get-tuple-element.473), channel_id=1, source_target_pairs={{0,16},{4,20},{8,24},{12,28},{16,0},{20,4},{24,8},{28,12},{1,17},{... | collective-permute-start | bytes 3932168 | tf_op jit(solution)/shard_map/ppermute | solution.py:697
  249.3 27.1 %collective-permute-start.27 = (bf16[256,2048]{1,0:T(8,128)(2,1)}, bf16[256,2048]{1,0:T(8,128)(2,1)}, u32[]{:S(2)}, u32[]{:S(2)}) collective-permute-start(bf16[256,2048]{1,0:T(8,128)(2,1)} %add_convert_fusion.2), channel_id=1, source_target_pairs={{0,1},{1,2},{2,3},{3,0},{4,5},{5,6},{6,7},{7,4},{8,9},{9,10},{10,1... | collective-permute-start | bytes 3145736 | tf_op jit(solution)/shard_map/ppermute | solution.py:827
  277.8 25.9 %collective-permute-start.31 = (bf16[256,2048]{1,0:T(8,128)(2,1)S(1)}, bf16[256,2048]{1,0:T(8,128)(2,1)S(1)}, u32[]{:S(2)}, u32[]{:S(2)}) collective-permute-start(bf16[256,2048]{1,0:T(8,128)(2,1)S(1)} %slice.76), channel_id=1, source_target_pairs={{0,1},{1,2},{2,3},{3,0},{4,5},{5,6},{6,7},{7,4},{8,9},{9,10},{10,1... | collective-permute-start | bytes 3145736 | tf_op jit(solution)/shard_map/ppermute | solution.py:827
  280.1 21.1 %collective-permute-start.33 = (bf16[128,2048]{1,0:T(8,128)(2,1)S(1)}, bf16[128,2048]{1,0:T(8,128)(2,1)S(1)}, u32[]{:S(2)}, u32[]{:S(2)}) collective-permute-start(bf16[128,2048]{1,0:T(8,128)(2,1)S(1)} %get-tuple-element.498), channel_id=1, source_target_pairs={{0,8},{4,12},{8,0},{12,4},{16,24},{20,28},{24,16},{28,20},{1,9},{5... | collective-permute-start | bytes 1572872 | tf_op jit(solution)/shard_map/ppermute | solution.py:697
  280.7 20.6 %collective-permute-start.34 = (bf16[128,2048]{1,0:T(8,128)(2,1)S(1)}, bf16[128,2048]{1,0:T(8,128)(2,1)S(1)}, u32[]{:S(2)}, u32[]{:S(2)}) collective-permute-start(bf16[128,2048]{1,0:T(8,128)(2,1)S(1)} %get-tuple-element.499), channel_id=1, source_target_pairs={{0,16},{4,20},{8,24},{12,28},{16,0},{20,4},{24,8},{28,12},{1,17},{... | collective-permute-start | bytes 1572872 | tf_op jit(solution)/shard_map/ppermute | solution.py:697
  287.5 13.5 %collective-permute-start.35 = (bf16[128,1536]{1,0:T(8,128)(2,1)S(1)}, bf16[128,1536]{1,0:T(8,128)(2,1)S(1)}, u32[]{:S(2)}, u32[]{:S(2)}) collective-permute-start(bf16[128,1536]{1,0:T(8,128)(2,1)S(1)} %get-tuple-element.502), channel_id=1, source_target_pairs={{0,8},{4,12},{8,0},{12,4},{16,24},{20,28},{24,16},{28,20},{1,9},{5... | collective-permute-start | bytes 1179656 | tf_op jit(solution)/shard_map/ppermute | solution.py:697
  288.8 12.5 %collective-permute-start.36 = (bf16[128,1536]{1,0:T(8,128)(2,1)S(1)}, bf16[128,1536]{1,0:T(8,128)(2,1)S(1)}, u32[]{:S(2)}, u32[]{:S(2)}) collective-permute-start(bf16[128,1536]{1,0:T(8,128)(2,1)S(1)} %get-tuple-element.503), channel_id=1, source_target_pairs={{0,16},{4,20},{8,24},{12,28},{16,0},{20,4},{24,8},{28,12},{1,17},{... | collective-permute-start | bytes 1179656 | tf_op jit(solution)/shard_map/ppermute | solution.py:697
  304.0 23.0 %collective-permute-start.38 = (bf16[256,2048]{1,0:T(8,128)(2,1)S(1)}, bf16[256,2048]{1,0:T(8,128)(2,1)S(1)}, u32[]{:S(2)}, u32[]{:S(2)}) collective-permute-start(bf16[256,2048]{1,0:T(8,128)(2,1)S(1)} %get-tuple-element.517), channel_id=1, source_target_pairs={{0,8},{4,12},{8,0},{12,4},{16,24},{20,28},{24,16},{28,20},{1,9},{5... | collective-permute-start | bytes 3145736 | tf_op jit(solution)/shard_map/ppermute | solution.py:697
  305.0 22.7 %collective-permute-start.39 = (bf16[256,2048]{1,0:T(8,128)(2,1)S(1)}, bf16[256,2048]{1,0:T(8,128)(2,1)S(1)}, u32[]{:S(2)}, u32[]{:S(2)}) collective-permute-start(bf16[256,2048]{1,0:T(8,128)(2,1)S(1)} %get-tuple-element.518), channel_id=1, source_target_pairs={{0,16},{4,20},{8,24},{12,28},{16,0},{20,4},{24,8},{28,12},{1,17},{... | collective-permute-start | bytes 3145736 | tf_op jit(solution)/shard_map/ppermute | solution.py:697
  306.9 24.3 %collective-permute-start.37 = (bf16[256,2048]{1,0:T(8,128)(2,1)S(1)}, bf16[256,2048]{1,0:T(8,128)(2,1)S(1)}, u32[]{:S(2)}, u32[]{:S(2)}) collective-permute-start(bf16[256,2048]{1,0:T(8,128)(2,1)S(1)} %add_convert_fusion.1), channel_id=1, source_target_pairs={{0,1},{1,2},{2,3},{3,0},{4,5},{5,6},{6,7},{7,4},{8,9},{9,10},{10,1... | collective-permute-start | bytes 3145736 | tf_op jit(solution)/shard_map/ppermute | solution.py:827
  331.5 23.3 %collective-permute-start.40 = (bf16[256,2048]{1,0:T(8,128)(2,1)S(1)}, bf16[256,2048]{1,0:T(8,128)(2,1)S(1)}, u32[]{:S(2)}, u32[]{:S(2)}) collective-permute-start(bf16[256,2048]{1,0:T(8,128)(2,1)S(1)} %add_convert_fusion), channel_id=1, source_target_pairs={{0,1},{1,2},{2,3},{3,0},{4,5},{5,6},{6,7},{7,4},{8,9},{9,10},{10,1... | collective-permute-start | bytes 3145736 | tf_op jit(solution)/shard_map/ppermute | solution.py:827
  331.8 15.9 %collective-permute-start.41 = (bf16[256,1536]{1,0:T(8,128)(2,1)S(1)}, bf16[256,1536]{1,0:T(8,128)(2,1)S(1)}, u32[]{:S(2)}, u32[]{:S(2)}) collective-permute-start(bf16[256,1536]{1,0:T(8,128)(2,1)S(1)} %get-tuple-element.526), channel_id=1, source_target_pairs={{0,8},{4,12},{8,0},{12,4},{16,24},{20,28},{24,16},{28,20},{1,9},{5... | collective-permute-start | bytes 2359304 | tf_op jit(solution)/shard_map/ppermute | solution.py:697
  332.6 15.7 %collective-permute-start.42 = (bf16[256,1536]{1,0:T(8,128)(2,1)S(1)}, bf16[256,1536]{1,0:T(8,128)(2,1)S(1)}, u32[]{:S(2)}, u32[]{:S(2)}) collective-permute-start(bf16[256,1536]{1,0:T(8,128)(2,1)S(1)} %get-tuple-element.527), channel_id=1, source_target_pairs={{0,16},{4,20},{8,24},{12,28},{16,0},{20,4},{24,8},{28,12},{1,17},{... | collective-permute-start | bytes 2359304 | tf_op jit(solution)/shard_map/ppermute | solution.py:697
  356.0 7.1 %collective-permute-start.43 = (f32[2,2048]{1,0:T(2,128)S(1)}, f32[2,2048]{1,0:T(2,128)S(1)}, u32[]{:S(2)}, u32[]{:S(2)}) collective-permute-start(f32[2,2048]{1,0:T(2,128)S(1)} %norm_sums.1), channel_id=1, source_target_pairs={{0,1},{1,2},{2,3},{3,0},{4,5},{5,6},{6,7},{7,4},{8,9},{9,10},{10,1... | collective-permute-start | bytes 49160 | tf_op jit(solution)/shard_map/ppermute | solution.py:827
  356.1 7.0 %collective-permute-start.44 = (f32[2,2048]{1,0:T(2,128)S(1)}, f32[2,2048]{1,0:T(2,128)S(1)}, u32[]{:S(2)}, u32[]{:S(2)}) collective-permute-start(f32[2,2048]{1,0:T(2,128)S(1)} %norm_sums.1), channel_id=1, source_target_pairs={{0,2},{1,3},{2,0},{3,1},{4,6},{5,7},{6,4},{7,5},{8,10},{9,11},{10,... | collective-permute-start | bytes 49160 | tf_op jit(solution)/shard_map/ppermute | solution.py:827
  357.4 5.7 %collective-permute-start.45 = (f32[2,2048]{1,0:T(2,128)S(1)}, f32[2,2048]{1,0:T(2,128)S(1)}, u32[]{:S(2)}, u32[]{:S(2)}) collective-permute-start(f32[2,2048]{1,0:T(2,128)S(1)} %norm_sums.1), channel_id=1, source_target_pairs={{0,3},{1,0},{2,1},{3,2},{4,7},{5,4},{6,5},{7,6},{8,11},{9,8},{10,9... | collective-permute-start | bytes 49160 | tf_op jit(solution)/shard_map/ppermute | solution.py:827
  364.4 3.6 collective-permute-start.47
  366.1 4.5 %collective-permute-start.49 = (f32[2,256]{1,0:T(2,128)S(1)}, f32[2,256]{1,0:T(2,128)S(1)}, u32[]{:S(2)}, u32[]{:S(2)}) collective-permute-start(f32[2,256]{1,0:T(2,128)S(1)} %get-tuple-element.545), channel_id=1, source_target_pairs={{0,24},{4,28},{8,16},{12,20},{16,8},{20,12},{24,0},{28,4},{1,25},{... | collective-permute-start | bytes 6152 | tf_op jit(solution)/shard_map/ppermute | solution.py:697
  (64 other events, 929.2 us)

commit v3 on v2

--- a/solution.py
+++ b/solution.py
@@ -69,7 +69,7 @@
     return list(range(0, count, 2)) + list(range(1, count, 2))
 
 
-def enter_kernel(count, me_ref, x_ref, cot_ref, gain_ref, bias_ref, normed_ref, cot_out_ref, row_ref):
+def enter_kernel(count, me_ref, x_ref, gain_ref, bias_ref, normed_ref, row_ref):
     x = x_ref[...].astype(F32)
     centered = x - jnp.mean(x, axis=-1, keepdims=True)
     inverse = lax.rsqrt(jnp.mean(centered * centered, axis=-1, keepdims=True) + 1e-05)
@@ -79,10 +79,9 @@
         at = pl.ds(pl.multiple_of((me_ref[0] ^ r) * size, size), size)
         to = slice(place * size, (place + 1) * size)
         normed_ref[:, to] = row_ref[:, at]
-        cot_out_ref[:, to] = cot_ref[:, at]
-
-
-def enter(x, cot, gain, bias, me, count):
+
+
+def enter(x, gain, bias, me, count):
     shape = jax.ShapeDtypeStruct(x.shape, BF)
     whole = pl.BlockSpec(x.shape, lambda j, me: (0, 0))
     line = pl.BlockSpec((1, x.shape[1]), lambda j, me: (0, 0))
@@ -91,15 +90,35 @@
         grid_spec=pltpu.PrefetchScalarGridSpec(
             num_scalar_prefetch=1,
             grid=(1,),
-            in_specs=[whole, whole, line, line],
-            out_specs=[whole, whole],
+            in_specs=[whole, line, line],
+            out_specs=whole,
             scratch_shapes=[pltpu.VMEM(x.shape, BF)],
         ),
-        out_shape=[shape, shape],
+        out_shape=shape,
         compiler_params=params(),
-        cost_estimate=cost(12 * x.size, [x, cot], [shape, shape]),
+        cost_estimate=cost(12 * x.size, [x], [shape]),
         name="enter",
-    )(me, x, cot, gain[None], bias[None])
+    )(me, x, gain[None], bias[None])
+
+
+def reorder_kernel(count, me_ref, x_ref, out_ref):
+    size = x_ref.shape[1] // count
+    for place, r in enumerate(place_order(count)):
+        at = pl.ds(pl.multiple_of((me_ref[0] ^ r) * size, size), size)
+        out_ref[:, place * size : (place + 1) * size] = x_ref[:, at]
+
+
+def reorder(x, me, count):
+    whole = pl.BlockSpec(x.shape, lambda j, me: (0, 0))
+    shape = jax.ShapeDtypeStruct(x.shape, x.dtype)
+    return pl.pallas_call(
+        functools.partial(reorder_kernel, count),
+        grid_spec=pltpu.PrefetchScalarGridSpec(num_scalar_prefetch=1, grid=(1,), in_specs=[whole], out_specs=whole),
+        out_shape=shape,
+        compiler_params=params(),
+        cost_estimate=cost(x.size, [x], [shape]),
+        name="reorder",
+    )(me, x)
 
 
 def leave_output_kernel(count, me_ref, x_ref, own_ref, in_ref, out_ref):
@@ -867,7 +886,8 @@
     more = n - 1
 
     near_up = gather_near(w_up)
-    normed_own, cot_own = enter(x, g, gain, bias, own_f, count)
+    normed_own = enter(x, gain, bias, own_f, count)
+    cot_own = reorder(after(g, normed_own), own_f, count)
     normed = [normed_own]
     if more >= 1:
         normed.append(step(normed[-1], 1))

time: 378 us -> 379 us (level)
  waiting for transfers between devices: 132 us -> 126 us
  local copies, waits for them, and re-layouts: 27 us -> 32.6 us
  starting transfers between devices: 43 us -> 47.8 us
    ppermute x16, waiting for transfers between devices: 54.1 us -> 46 us  [step(): return lax.ppermute(array, 'tp', [(i, (i + by) % n) for i in range(n)])]
    unnamed x136 -> x110, local copies, waits for them, and re-layouts: 20.6 us -> 26.3 us
    ppermute x16, starting transfers between devices: 11.1 us -> 15.8 us  [step(): return lax.ppermute(array, 'tp', [(i, (i + by) % n) for i in range(n)])]
  transfers between devices with their start and end apart: 50 -> 50, of which waited for: 26 -> 24; matrix products, arithmetic and copies ran while one was open for 6% -> 6% of each run, Pallas kernels for 43% -> 42%
where the time goes in v3:
time: 379 us; the launch traced here: 373 us
  Pallas kernels  159 us (42%)
  waiting for transfers between devices  126 us (33%)
  starting transfers between devices  47.8 us (13%)
  local copies, waits for them, and re-layouts  32.6 us (9%)
  other arithmetic  5.93 us (2%)
    pallas_call x13, Pallas kernels, product(): pl.pallas_call(body, grid=(steps,), in_specs=specs, out_specs=out_specs,...  115 us
    ppermute x34, waiting for transfers between devices, flip(): return lax.ppermute(array, 'fsdp', [(s, s ^ bit) for s in range(count)])  80.1 us
    ppermute x16, waiting for transfers between devices, step(): return lax.ppermute(array, 'tp', [(i, (i + by) % n) for i in range(n)])  46 us
    ppermute x34, starting transfers between devices, flip(): return lax.ppermute(array, 'fsdp', [(s, s ^ bit) for s in range(count)])  31.9 us
    unnamed x110, local copies, waits for them, and re-layouts  26.3 us
    pallas_call x1, Pallas kernels, attend_backward(): pl.pallas_call(functools.partial(attend_backward_kernel, block, count), g...  16.8 us
    ppermute x16, starting transfers between devices, step(): return lax.ppermute(array, 'tp', [(i, (i + by) % n) for i in range(n)])  15.8 us
    pallas_call x1, Pallas kernels, attend_forward(): pl.pallas_call(functools.partial(attend_forward_kernel, block, count), gr...  11.4 us
  transfers between devices with their start and end apart: 50, of which 24 were waited for; matrix products, arithmetic and copies ran while one was open for 6% of the time, Pallas kernels for 42%

profile of v3, /device:TPU:0, one launch (start us, length us, event | category | flops | bytes accessed | tf_op | source)
XLA Modules:
  0.0 373.4 jit_solution(9610749448477003793)
XLA Ops:
  0.6 3.0 collective-permute-start.3
  11.8 3.2 fusion.2
  16.1 18.8 %collective-permute-done.refs_1_ = bf16[256,2048]{1,0:T(8,128)(2,1)S(1)} collective-permute-done((bf16[256,2048]{1,0:T(8,128)(2,1)S(1)}, bf16[256,2048]{1,0:T(8,128)(2,1)S(1)}, u32[]{:S(2)}, u32[]{:S(2)}) %collective-permute-start) | collective-permute-done | bytes 1048608 | tf_op jit(solution)/shard_map/ppermute | solution.py:846
  43.0 21.2 %collective-permute-done.5 = bf16[128,2048]{1,0:T(8,128)(2,1)S(1)} collective-permute-done((bf16[128,2048]{1,0:T(8,128)(2,1)S(1)}, bf16[128,2048]{1,0:T(8,128)(2,1)S(1)}, u32[]{:S(2)}, u32[]{:S(2)}) %collective-permute-start.5) | collective-permute-done | bytes 524320 | tf_op jit(solution)/shard_map/ppermute | solution.py:716
  69.6 6.5 %collective-permute-done.11 = bf16[3,128,512]{2,1,0:T(8,128)(2,1)S(1)} collective-permute-done((bf16[3,128,512]{2,1,0:T(8,128)(2,1)S(1)}, bf16[3,128,512]{2,1,0:T(8,128)(2,1)S(1)}, u32[]{:S(2)}, u32[]{:S(2)}) %collective-permute-start.11) | collective-permute-done | bytes 393248 | tf_op jit(solution)/shard_map/ppermute | solution.py:716
  78.3 13.6 %collective-permute-done.2.refs_3_ = bf16[256,2048]{1,0:T(8,128)(2,1)S(1)} collective-permute-done((bf16[256,2048]{1,0:T(8,128)(2,1)S(1)}, bf16[256,2048]{1,0:T(8,128)(2,1)S(1)}, u32[]{:S(2)}, u32[]{:S(2)}) %collective-permute-start.2) | collective-permute-done | bytes 1048608 | tf_op jit(solution)/shard_map/ppermute | solution.py:846
  92.0 1.6 collective-permute-start.15
  94.1 14.5 %up.1 = (bf16[1024,2048]{1,0:T(8,128)(2,1)S(1)}, bf16[1024,2048]{1,0:T(8,128)(2,1)S(1)}) custom-call(bf16[256,2048]{1,0:T(8,128)(2,1)S(1)} %enter.1.refs_0_, bf16[256,2048]{1,0:T(8,128)(2,1)S(1)} %collective-permute-done.refs_1_, bf16[256,2048]{1,0:T(8,128)(2,1)S(1)} %collective-permute-done.1.refs_2_, bf16[256,2048]{1,0:T(8,128)(2,1)S(1)} %collective-permute-done.2.refs_3_, ...), custom_call_target="tpu_custom_call" | custom-call | flops 1073741824 | bytes 2621440 | tf_op jit(solution)/shard_map/up/pallas_call | solution.py:448
  108.7 2.0 copy-done
  110.7 1.9 copy-done.14
  112.7 6.7 %collective-permute-done.9.refs_1_ = bf16[256,2048]{1,0:T(8,128)(2,1)} collective-permute-done((bf16[256,2048]{1,0:T(8,128)(2,1)S(1)}, bf16[256,2048]{1,0:T(8,128)(2,1)}, u32[]{:S(2)}, u32[]{:S(2)}) %collective-permute-start.9) | collective-permute-done | bytes 1048608 | tf_op jit(solution)/shard_map/ppermute | solution.py:846
  120.8 9.3 %qkv.1.q_in.k_in.v_in = f32[1024,1536]{1,0:T(8,128)S(1)} custom-call(bf16[256,2048]{1,0:T(8,128)(2,1)S(1)} %enter.1.refs_0_, bf16[256,2048]{1,0:T(8,128)(2,1)S(1)} %collective-permute-done.refs_1_, bf16[256,2048]{1,0:T(8,128)(2,1)S(1)} %collective-permute-done.1.refs_2_, bf16[256,2048]{1,0:T(8,128)(2,1)S(1)} %copy-done.5, ...), custom_call_target="tpu_custom_call" | custom-call | flops 805306368 | bytes 2097152 | tf_op jit(solution)/shard_map/qkv/pallas_call | solution.py:448
  134.6 11.4 %attend_forward.1 = (bf16[1024,512]{1,0:T(8,128)(2,1)S(1)}, bf16[1024,512]{1,0:T(8,128)(2,1)S(1)}, bf16[1024,512]{1,0:T(8,128)(2,1)S(1)}, bf16[1024,512]{1,0:T(8,128)(2,1)S(1)}, f32[4,8,1024]{2,1,0:T(8,128)S(1)}) custom-call(s32[1]{0:T(128)} %bitcast.6.me_ref, f32[1024,1536]{1,0:T(8,128)S(1)} %qkv.1.q_in.k_in.v_in, f32[1024,1536]{1,0:T(8,128)S(1)} %qkv.1.q_in.k_in.v_in, ...), custom_call_target="tpu_custom_call" | custom-call | flops 1073741824 | bytes 1523712 | tf_op jit(solution)/shard_map/attend_forward/pallas_call | solution.py:320
  146.0 2.5 constant_dynamic-update-slice_fusion.14
  150.0 1.6 constant_dynamic-update-slice_fusion.12
  152.6 6.2 %branch.2.rest_0_ = bf16[1024,2048]{1,0:T(8,128)(2,1)S(1)} custom-call(bf16[1024,2048]{1,0:T(8,128)(2,1)S(1)} %copy-done.1, bf16[1024,512]{1,0:T(8,128)(2,1)S(1)} %get-tuple-element.346.att_ref.refs_5_, bf16[2560,1024]{1,0:T(8,128)(2,1)S(1)} %constant_dynamic-update-slice_fusion.10.w_ref.refs_3_), custom_call_target="tpu_custom_call" | custom-call | flops 671088640 | bytes 1835008 | tf_op jit(solution)/shard_map/branch/pallas_call | solution.py:448
  158.9 2.0 collective-permute-done.20.w_ref.refs_4_
  160.9 6.2 %branch.3.own_ref = bf16[1024,2048]{1,0:T(8,128)(2,1)S(1)} custom-call(bf16[1024,2048]{1,0:T(8,128)(2,1)S(1)} %copy-done.1, bf16[1024,512]{1,0:T(8,128)(2,1)S(1)} %get-tuple-element.346.att_ref.refs_5_, bf16[2560,1024]{1,0:T(8,128)(2,1)S(1)} %collective-permute-done.20.w_ref.refs_4_, ...), custom_call_target="tpu_custom_call", output_to_operand_aliasing={{}: (3, {})} | custom-call | flops 671088640 | bytes 2359296 | tf_op jit(solution)/shard_map/branch/pallas_call | solution.py:448
  167.1 2.3 copy-done.2
  169.5 2.5 copy-done.3
  171.9 8.6 %d_branch.2.refs_5_ = bf16[1024,2560]{1,0:T(8,128)(2,1)S(1)} custom-call(bf16[256,2048]{1,0:T(8,128)(2,1)S(1)} %copy-done.10, bf16[256,2048]{1,0:T(8,128)(2,1)} %collective-permute-done.9.refs_1_, bf16[1024,2048]{1,0:T(8,128)(2,1)S(1)} %copy-done.15, bf16[2560,1024]{1,0:T(8,128)(2,1)S(1)} %constant_dynamic-update-slice_fusion.10.w_ref.refs_3_, ...), custom_call_target="tpu_custom_call" | custom-call | flops 671088640 | bytes 2752512 | tf_op jit(solution)/shard_map/d_branch/pallas_call | solution.py:448
  181.0 9.0 %down_away.1 = bf16[1024,2560]{1,0:T(8,128)(2,1)} custom-call(bf16[256,2048]{1,0:T(8,128)(2,1)S(1)} %copy-done.10, bf16[256,2048]{1,0:T(8,128)(2,1)} %collective-permute-done.9.refs_1_, bf16[256,2048]{1,0:T(8,128)(2,1)} %collective-permute-done.13.refs_2_.refs_0_, bf16[256,2048]{1,0:T(8,128)(2,1)S(1)} %collective-permute-done.17.refs_3_.refs_1_, ...), custom_call_target="tpu_custom_call" | custom-call | flops 671088640 | bytes 1835008 | tf_op jit(solution)/shard_map/down_away/pallas_call | solution.py:448
  190.0 8.7 %d_branch.3.refs_4_.g_in.du_ref = bf16[1024,2560]{1,0:T(8,128)(2,1)S(1)} custom-call(bf16[256,2048]{1,0:T(8,128)(2,1)} %collective-permute-done.13.refs_2_.refs_0_, bf16[256,2048]{1,0:T(8,128)(2,1)S(1)} %collective-permute-done.17.refs_3_.refs_1_, bf16[1024,2048]{1,0:T(8,128)(2,1)S(1)} %copy-done.16, ...), custom_call_target="tpu_custom_call", output_to_operand_aliasing={{}: (5, {})} | custom-call | flops 671088640 | bytes 3407872 | tf_op jit(solution)/shard_map/d_branch/pallas_call | solution.py:448
  199.0 1.9 collective-permute-start.22
  200.9 6.8 %up_away.1 = bf16[1024,2048]{1,0:T(8,128)(2,1)} custom-call(bf16[256,2048]{1,0:T(8,128)(2,1)S(1)} %enter.1.refs_0_, bf16[256,2048]{1,0:T(8,128)(2,1)S(1)} %collective-permute-done.refs_1_, bf16[256,2048]{1,0:T(8,128)(2,1)S(1)} %collective-permute-done.1.refs_2_, bf16[256,2048]{1,0:T(8,128)(2,1)S(1)} %copy-done.6, ...), custom_call_target="tpu_custom_call" | custom-call | flops 536870912 | bytes 1703936 | tf_op jit(solution)/shard_map/up_away/pallas_call | solution.py:448
  207.7 8.7 %down_mine.1 = (bf16[256,2560]{1,0:T(8,128)(2,1)S(1)}, bf16[256,2560]{1,0:T(8,128)(2,1)S(1)}, bf16[256,2560]{1,0:T(8,128)(2,1)S(1)}, bf16[128,2560]{1,0:T(8,128)(2,1)S(1)}, bf16[128,2560]{1,0:T(8,128)(2,1)S(1)}) custom-call(bf16[256,2048]{1,0:T(8,128)(2,1)S(1)} %copy-done.11, bf16[256,2048]{1,0:T(8,128)(2,1)} %collective-permute-done.9.refs_1_, ...), custom_call_target="tpu_custom_call" | custom-call | flops 671088640 | bytes 2490368 | tf_op jit(solution)/shard_map/down_mine/pallas_call | solution.py:448
  216.8 3.1 collective-permute-start.24
  222.0 16.8 %attend_backward.1 = (bf16[1024,512]{1,0:T(8,128)(2,1)S(1)}, bf16[1024,512]{1,0:T(8,128)(2,1)S(1)}, bf16[1024,512]{1,0:T(8,128)(2,1)S(1)}) custom-call(s32[1]{0:T(128)} %bitcast.6.me_ref, bf16[1024,512]{1,0:T(8,128)(2,1)S(1)} %copy-done.33, bf16[1024,512]{1,0:T(8,128)(2,1)S(1)} %copy-done.35, bf16[1024,512]{1,0:T(8,128)(2,1)S(1)} %copy-done.37, ...), custom_call_target="tpu_custom_call" | custom-call | flops 2684354560 | bytes 1114112 | tf_op jit(solution)/shard_map/attend_backward/pallas_call | solution.py:416
  238.9 1.9 merge.3
  240.7 5.3 %qkv_away.1 = bf16[1024,1536]{1,0:T(8,128)(2,1)} custom-call(bf16[256,2048]{1,0:T(8,128)(2,1)S(1)} %enter.1.refs_0_, bf16[256,2048]{1,0:T(8,128)(2,1)S(1)} %collective-permute-done.refs_1_, bf16[256,2048]{1,0:T(8,128)(2,1)S(1)} %collective-permute-done.1.refs_2_, bf16[256,2048]{1,0:T(8,128)(2,1)S(1)} %copy-done.6, ...), custom_call_target="tpu_custom_call" | custom-call | flops 402653184 | bytes 1310720 | tf_op jit(solution)/shard_map/qkv_away/pallas_call | solution.py:448
  248.9 2.0 collective-permute-start.27
  250.9 19.0 %d_normed.1.own_ref = bf16[1024,2048]{1,0:T(8,128)(2,1)S(1)} custom-call(bf16[1024,2560]{1,0:T(8,128)(2,1)S(1)} %d_branch.3.refs_4_.g_in.du_ref, bf16[1024,512]{1,0:T(8,128)(2,1)S(1)} %get-tuple-element.486.refs_4_.dq_ref, bf16[1024,512]{1,0:T(8,128)(2,1)S(1)} %get-tuple-element.487.refs_5_.dk_ref, bf16[1024,512]{1,0:T(8,128)(2,1)S(1)} %get-tuple-element.488.refs_6_.dv_ref, ...), custom_call_target="tpu_custom_call" | custom-call | flops 1879048192 | bytes 3407872 | tf_op jit(solution)/shard_map/d_normed/pallas_call | solution.py:448
  270.0 6.3 %up_mine.1 = (bf16[256,2048]{1,0:T(8,128)(2,1)S(1)}, bf16[256,2048]{1,0:T(8,128)(2,1)S(1)}, bf16[256,2048]{1,0:T(8,128)(2,1)S(1)}, bf16[128,2048]{1,0:T(8,128)(2,1)S(1)}, bf16[128,2048]{1,0:T(8,128)(2,1)S(1)}) custom-call(bf16[256,2048]{1,0:T(8,128)(2,1)S(1)} %enter.1.refs_0_, bf16[256,2048]{1,0:T(8,128)(2,1)S(1)} %collective-permute-done.refs_1_, ...), custom_call_target="tpu_custom_call" | custom-call | flops 536870912 | bytes 2228224 | tf_op jit(solution)/shard_map/up_mine/pallas_call | solution.py:448
  278.9 2.5 collective-permute-start.31
  283.0 6.0 %qkv_mine.1 = (bf16[256,1536]{1,0:T(8,128)(2,1)S(1)}, bf16[256,1536]{1,0:T(8,128)(2,1)S(1)}, bf16[256,1536]{1,0:T(8,128)(2,1)S(1)}, bf16[128,1536]{1,0:T(8,128)(2,1)S(1)}, bf16[128,1536]{1,0:T(8,128)(2,1)S(1)}) custom-call(bf16[256,2048]{1,0:T(8,128)(2,1)S(1)} %enter.1.refs_0_, bf16[256,2048]{1,0:T(8,128)(2,1)S(1)} %collective-permute-done.refs_1_, ...), custom_call_target="tpu_custom_call" | custom-call | flops 402653184 | bytes 1703936 | tf_op jit(solution)/shard_map/qkv_mine/pallas_call | solution.py:448
  292.9 9.4 %collective-permute-done.35.via_x_ref = bf16[128,1536]{1,0:T(8,128)(2,1)S(1)} collective-permute-done((bf16[128,1536]{1,0:T(8,128)(2,1)S(1)}, bf16[128,1536]{1,0:T(8,128)(2,1)S(1)}, u32[]{:S(2)}, u32[]{:S(2)}) %collective-permute-start.35) | collective-permute-done | bytes 393248 | tf_op jit(solution)/shard_map/ppermute | solution.py:716
  303.5 1.7 collective-permute-done.31
  305.5 1.6 collective-permute-start.38
  308.2 3.5 finish_down.1
  311.6 17.2 %collective-permute-done.38.refs_1_ = bf16[256,2048]{1,0:T(8,128)(2,1)S(1)} collective-permute-done((bf16[256,2048]{1,0:T(8,128)(2,1)S(1)}, bf16[256,2048]{1,0:T(8,128)(2,1)S(1)}, u32[]{:S(2)}, u32[]{:S(2)}) %collective-permute-start.38) | collective-permute-done | bytes 1048608 | tf_op jit(solution)/shard_map/ppermute | solution.py:716
  330.2 2.4 collective-permute-done.37
  335.3 14.4 %collective-permute-done.41.refs_1_ = bf16[256,1536]{1,0:T(8,128)(2,1)S(1)} collective-permute-done((bf16[256,1536]{1,0:T(8,128)(2,1)S(1)}, bf16[256,1536]{1,0:T(8,128)(2,1)S(1)}, u32[]{:S(2)}, u32[]{:S(2)}) %collective-permute-start.41) | collective-permute-done | bytes 786464 | tf_op jit(solution)/shard_map/ppermute | solution.py:716
  351.6 1.7 finish_up.1
  354.1 2.7 collective-permute-done.40.in_ref
  359.4 2.4 collective-permute-start.45
  361.8 3.2 leave_grad.1
  368.2 1.7 collective-permute-start.49
  370.8 1.9 collective-permute-done.49
  (217 shorter events, 64.3 us)
Async XLA Ops:
  0.6 34.3 %collective-permute-start.3 = (bf16[256,2048]{1,0:T(8,128)(2,1)}, bf16[256,2048]{1,0:T(8,128)(2,1)S(1)}, u32[]{:S(2)}, u32[]{:S(2)}) collective-permute-start(bf16[256,2048]{1,0:T(8,128)(2,1)} %param.13), channel_id=1, source_target_pairs={{0,8},{4,12},{8,0},{12,4},{16,24},{20,28},{24,16},{28,20},{1,9},{5... | collective-permute-start | bytes 3145736 | tf_op jit(solution)/shard_map/ppermute | solution.py:716
  3.6 31.3 %collective-permute-start.4 = (bf16[256,2048]{1,0:T(8,128)(2,1)}, bf16[256,2048]{1,0:T(8,128)(2,1)}, u32[]{:S(2)}, u32[]{:S(2)}) collective-permute-start(bf16[256,2048]{1,0:T(8,128)(2,1)} %param.13), channel_id=1, source_target_pairs={{0,16},{4,20},{8,24},{12,28},{16,0},{20,4},{24,8},{28,12},{1,17},{... | collective-permute-start | bytes 3145736 | tf_op jit(solution)/shard_map/ppermute | solution.py:716
  8.7 26.3 %collective-permute-start = (bf16[256,2048]{1,0:T(8,128)(2,1)S(1)}, bf16[256,2048]{1,0:T(8,128)(2,1)S(1)}, u32[]{:S(2)}, u32[]{:S(2)}) collective-permute-start(bf16[256,2048]{1,0:T(8,128)(2,1)S(1)} %enter.1.refs_0_), channel_id=1, source_target_pairs={{0,1},{1,2},{2,3},{3,0},{4,5},{5,6},{6,7},{7,4},{8,9},{9,10},{10,1... | collective-permute-start | bytes 3145736 | tf_op jit(solution)/shard_map/ppermute | solution.py:846
  35.0 29.4 %collective-permute-start.7 = (bf16[3,256,512]{2,1,0:T(8,128)(2,1)S(1)}, bf16[3,256,512]{2,1,0:T(8,128)(2,1)S(1)}, u32[]{:S(2)}, u32[]{:S(2)}) collective-permute-start(bf16[3,256,512]{2,1,0:T(8,128)(2,1)S(1)} %bitcast.26), channel_id=1, source_target_pairs={{0,8},{4,12},{8,0},{12,4},{16,24},{20,28},{24,16},{28,20},{1,9},{5... | collective-permute-start | bytes 2359304 | tf_op jit(solution)/shard_map/ppermute | solution.py:716
  35.6 28.9 %collective-permute-start.8 = (bf16[3,256,512]{2,1,0:T(8,128)(2,1)S(1)}, bf16[3,256,512]{2,1,0:T(8,128)(2,1)S(1)}, u32[]{:S(2)}, u32[]{:S(2)}) collective-permute-start(bf16[3,256,512]{2,1,0:T(8,128)(2,1)S(1)} %bitcast.27), channel_id=1, source_target_pairs={{0,16},{4,20},{8,24},{12,28},{16,0},{20,4},{24,8},{28,12},{1,17},{... | collective-permute-start | bytes 2359304 | tf_op jit(solution)/shard_map/ppermute | solution.py:716
  37.2 27.0 %collective-permute-start.5 = (bf16[128,2048]{1,0:T(8,128)(2,1)S(1)}, bf16[128,2048]{1,0:T(8,128)(2,1)S(1)}, u32[]{:S(2)}, u32[]{:S(2)}) collective-permute-start(bf16[128,2048]{1,0:T(8,128)(2,1)S(1)} %slice.66), channel_id=1, source_target_pairs={{0,8},{4,12},{8,0},{12,4},{16,24},{20,28},{24,16},{28,20},{1,9},{5... | collective-permute-start | bytes 1572872 | tf_op jit(solution)/shard_map/ppermute | solution.py:716
  38.7 25.7 %collective-permute-start.1 = (bf16[256,2048]{1,0:T(8,128)(2,1)S(1)}, bf16[256,2048]{1,0:T(8,128)(2,1)S(1)}, u32[]{:S(2)}, u32[]{:S(2)}) collective-permute-start(bf16[256,2048]{1,0:T(8,128)(2,1)S(1)} %collective-permute-done.refs_1_), channel_id=1, source_target_pairs={{0,1},{1,2},{2,3},{3,0},{4,5},{5,6},{6,7},{7,4},{8,9},{9,10},{10,1... | collective-permute-start | bytes 3145736 | tf_op jit(solution)/shard_map/ppermute | solution.py:846
  39.9 24.4 %collective-permute-start.6 = (bf16[128,2048]{1,0:T(8,128)(2,1)S(1)}, bf16[128,2048]{1,0:T(8,128)(2,1)S(1)}, u32[]{:S(2)}, u32[]{:S(2)}) collective-permute-start(bf16[128,2048]{1,0:T(8,128)(2,1)S(1)} %slice.67), channel_id=1, source_target_pairs={{0,16},{4,20},{8,24},{12,28},{16,0},{20,4},{24,8},{28,12},{1,17},{... | collective-permute-start | bytes 1572872 | tf_op jit(solution)/shard_map/ppermute | solution.py:716
  64.4 27.4 %collective-permute-start.10 = (bf16[1024,2048]{1,0:T(8,128)(2,1)S(1)}, bf16[1024,2048]{1,0:T(8,128)(2,1)S(1)}, u32[]{:S(2)}, u32[]{:S(2)}) collective-permute-start(bf16[1024,2048]{1,0:T(8,128)(2,1)S(1)} %constant_dynamic-update-slice_fusion.refs_4_.um_ref), channel_id=1, source_target_pairs={{0,4},{4,0},{8,12},{12,8},{16,20},{20,16},{24,28},{28,24},{1,5},{5... | collective-permute-start | bytes 12582920 | tf_op jit(solution)/shard_map/ppermute | solution.py:716
  64.5 27.4 %collective-permute-start.2 = (bf16[256,2048]{1,0:T(8,128)(2,1)S(1)}, bf16[256,2048]{1,0:T(8,128)(2,1)S(1)}, u32[]{:S(2)}, u32[]{:S(2)}) collective-permute-start(bf16[256,2048]{1,0:T(8,128)(2,1)S(1)} %collective-permute-done.1.refs_2_), channel_id=1, source_target_pairs={{0,1},{1,2},{2,3},{3,0},{4,5},{5,6},{6,7},{7,4},{8,9},{9,10},{10,1... | collective-permute-start | bytes 3145736 | tf_op jit(solution)/shard_map/ppermute | solution.py:846
  64.6 11.5 %collective-permute-start.11 = (bf16[3,128,512]{2,1,0:T(8,128)(2,1)S(1)}, bf16[3,128,512]{2,1,0:T(8,128)(2,1)S(1)}, u32[]{:S(2)}, u32[]{:S(2)}) collective-permute-start(bf16[3,128,512]{2,1,0:T(8,128)(2,1)S(1)} %slice.68), channel_id=1, source_target_pairs={{0,8},{4,12},{8,0},{12,4},{16,24},{20,28},{24,16},{28,20},{1,9},{5... | collective-permute-start | bytes 1179656 | tf_op jit(solution)/shard_map/ppermute | solution.py:716
  66.3 11.2 %collective-permute-start.12 = (bf16[3,128,512]{2,1,0:T(8,128)(2,1)S(1)}, bf16[3,128,512]{2,1,0:T(8,128)(2,1)S(1)}, u32[]{:S(2)}, u32[]{:S(2)}) collective-permute-start(bf16[3,128,512]{2,1,0:T(8,128)(2,1)S(1)} %slice.69), channel_id=1, source_target_pairs={{0,16},{4,20},{8,24},{12,28},{16,0},{20,4},{24,8},{28,12},{1,17},{... | collective-permute-start | bytes 1179656 | tf_op jit(solution)/shard_map/ppermute | solution.py:716
  91.9 27.7 %collective-permute-start.14 = (bf16[3,1024,512]{2,1,0:T(8,128)(2,1)}, bf16[3,1024,512]{2,1,0:T(8,128)(2,1)}, u32[]{:S(2)}, u32[]{:S(2)}) collective-permute-start(bf16[3,1024,512]{2,1,0:T(8,128)(2,1)} %constant_dynamic-update-slice_fusion.5.refs_4_.qm_ref), channel_id=1, source_target_pairs={{0,4},{4,0},{8,12},{12,8},{16,20},{20,16},{24,28},{28,24},{1,5},{5... | collective-permute-start | bytes 9437192 | tf_op jit(solution)/shard_map/ppermute | solution.py:716
  92.0 27.5 %collective-permute-start.9 = (bf16[256,2048]{1,0:T(8,128)(2,1)S(1)}, bf16[256,2048]{1,0:T(8,128)(2,1)}, u32[]{:S(2)}, u32[]{:S(2)}) collective-permute-start(bf16[256,2048]{1,0:T(8,128)(2,1)S(1)} %reorder.1.refs_0_), channel_id=1, source_target_pairs={{0,1},{1,2},{2,3},{3,0},{4,5},{5,6},{6,7},{7,4},{8,9},{9,10},{10,1... | collective-permute-start | bytes 3145736 | tf_op jit(solution)/shard_map/ppermute | solution.py:846
  92.0 38.1 %collective-permute-start.15 = (bf16[2560,256]{1,0:T(8,128)(2,1)}, bf16[2560,256]{1,0:T(8,128)(2,1)}, u32[]{:S(2)}, u32[]{:S(2)}) collective-permute-start(bf16[2560,256]{1,0:T(8,128)(2,1)} %pad_maximum_fusion), channel_id=1, source_target_pairs={{0,8},{4,12},{8,0},{12,4},{16,24},{20,28},{24,16},{28,20},{1,9},{5... | collective-permute-start | bytes 3932168 | tf_op jit(solution)/shard_map/ppermute | solution.py:716
  93.7 36.5 %collective-permute-start.16 = (bf16[2560,256]{1,0:T(8,128)(2,1)}, bf16[2560,256]{1,0:T(8,128)(2,1)}, u32[]{:S(2)}, u32[]{:S(2)}) collective-permute-start(bf16[2560,256]{1,0:T(8,128)(2,1)} %pad_maximum_fusion), channel_id=1, source_target_pairs={{0,16},{4,20},{8,24},{12,28},{16,0},{20,4},{24,8},{28,12},{1,17},{... | collective-permute-start | bytes 3932168 | tf_op jit(solution)/shard_map/ppermute | solution.py:716
  119.4 29.1 %collective-permute-start.13 = (bf16[256,2048]{1,0:T(8,128)(2,1)}, bf16[256,2048]{1,0:T(8,128)(2,1)}, u32[]{:S(2)}, u32[]{:S(2)}) collective-permute-start(bf16[256,2048]{1,0:T(8,128)(2,1)} %collective-permute-done.9.refs_1_), channel_id=1, source_target_pairs={{0,1},{1,2},{2,3},{3,0},{4,5},{5,6},{6,7},{7,4},{8,9},{9,10},{10,1... | collective-permute-start | bytes 3145736 | tf_op jit(solution)/shard_map/ppermute | solution.py:846
  131.3 20.4 %collective-permute-start.18 = (bf16[2560,128]{1,0:T(8,128)(2,1)S(1)}, bf16[2560,128]{1,0:T(8,128)(2,1)S(1)}, u32[]{:S(2)}, u32[]{:S(2)}) collective-permute-start(bf16[2560,128]{1,0:T(8,128)(2,1)S(1)} %slice.70), channel_id=1, source_target_pairs={{0,8},{4,12},{8,0},{12,4},{16,24},{20,28},{24,16},{28,20},{1,9},{5... | collective-permute-start | bytes 1966088 | tf_op jit(solution)/shard_map/ppermute | solution.py:716
  134.1 17.9 %collective-permute-start.19 = (bf16[2560,128]{1,0:T(8,128)(2,1)S(1)}, bf16[2560,128]{1,0:T(8,128)(2,1)S(1)}, u32[]{:S(2)}, u32[]{:S(2)}) collective-permute-start(bf16[2560,128]{1,0:T(8,128)(2,1)S(1)} %slice.71), channel_id=1, source_target_pairs={{0,16},{4,20},{8,24},{12,28},{16,0},{20,4},{24,8},{28,12},{1,17},{... | collective-permute-start | bytes 1966088 | tf_op jit(solution)/shard_map/ppermute | solution.py:716
  152.2 8.7 %collective-permute-start.20 = (bf16[2560,1024]{1,0:T(8,128)(2,1)S(1)}, bf16[2560,1024]{1,0:T(8,128)(2,1)S(1)}, u32[]{:S(2)}, u32[]{:S(2)}) collective-permute-start(bf16[2560,1024]{1,0:T(8,128)(2,1)S(1)} %constant_dynamic-update-slice_fusion.10.w_ref.refs_3_), channel_id=1, source_target_pairs={{0,4},{4,0},{8,12},{12,8},{16,20},{20,16},{24,28},{28,24},{1,5},{5... | collective-permute-start | bytes 15728648 | tf_op jit(solution)/shard_map/ppermute | solution.py:716
  152.2 28.3 %collective-permute-start.17 = (bf16[256,2048]{1,0:T(8,128)(2,1)}, bf16[256,2048]{1,0:T(8,128)(2,1)S(1)}, u32[]{:S(2)}, u32[]{:S(2)}) collective-permute-start(bf16[256,2048]{1,0:T(8,128)(2,1)} %collective-permute-done.13.refs_2_.refs_0_), channel_id=1, source_target_pairs={{0,1},{1,2},{2,3},{3,0},{4,5},{5,6},{6,7},{7,4},{8,9},{9,10},{10,1... | collective-permute-start | bytes 3145736 | tf_op jit(solution)/shard_map/ppermute | solution.py:846
  180.7 18.0 %collective-permute-start.21 = (bf16[256,1024]{1,0:T(8,128)(2,1)S(1)}, bf16[256,1024]{1,0:T(8,128)(2,1)S(1)}, u32[]{:S(2)}, u32[]{:S(2)}) collective-permute-start(bf16[256,1024]{1,0:T(8,128)(2,1)S(1)} %get-tuple-element.541), channel_id=1, source_target_pairs={{0,1},{1,2},{2,3},{3,0},{4,5},{5,6},{6,7},{7,4},{8,9},{9,10},{10,1... | collective-permute-start | bytes 1572872 | tf_op jit(solution)/shard_map/ppermute | solution.py:846
  198.8 8.9 %collective-permute-start.23 = (bf16[1024,2560]{1,0:T(8,128)(2,1)}, bf16[1024,2560]{1,0:T(8,128)(2,1)S(1)}, u32[]{:S(2)}, u32[]{:S(2)}) collective-permute-start(bf16[1024,2560]{1,0:T(8,128)(2,1)} %down_away.1), channel_id=1, source_target_pairs={{0,4},{4,0},{8,12},{12,8},{16,20},{20,16},{24,28},{28,24},{1,5},{5... | collective-permute-start | bytes 15728648 | tf_op jit(solution)/shard_map/ppermute | solution.py:716
  199.0 17.5 %collective-permute-start.22 = (bf16[256,1024]{1,0:T(8,128)(2,1)S(1)}, bf16[256,1024]{1,0:T(8,128)(2,1)S(1)}, u32[]{:S(2)}, u32[]{:S(2)}) collective-permute-start(bf16[256,1024]{1,0:T(8,128)(2,1)S(1)} %get-tuple-element.362), channel_id=1, source_target_pairs={{0,1},{1,2},{2,3},{3,0},{4,5},{5,6},{6,7},{7,4},{8,9},{9,10},{10,1... | collective-permute-start | bytes 1572872 | tf_op jit(solution)/shard_map/ppermute | solution.py:846
  216.8 29.2 %collective-permute-start.24 = (bf16[256,2048]{1,0:T(8,128)(2,1)S(1)}, bf16[256,2048]{1,0:T(8,128)(2,1)S(1)}, u32[]{:S(2)}, u32[]{:S(2)}) collective-permute-start(bf16[256,2048]{1,0:T(8,128)(2,1)S(1)} %add_convert_fusion.3), channel_id=1, source_target_pairs={{0,1},{1,2},{2,3},{3,0},{4,5},{5,6},{6,7},{7,4},{8,9},{9,10},{10,1... | collective-permute-start | bytes 3145736 | tf_op jit(solution)/shard_map/ppermute | solution.py:846
  219.9 18.9 %collective-permute-start.25 = (bf16[128,2560]{1,0:T(8,128)(2,1)S(1)}, bf16[128,2560]{1,0:T(8,128)(2,1)S(1)}, u32[]{:S(2)}, u32[]{:S(2)}) collective-permute-start(bf16[128,2560]{1,0:T(8,128)(2,1)S(1)} %get-tuple-element.416), channel_id=1, source_target_pairs={{0,8},{4,12},{8,0},{12,4},{16,24},{20,28},{24,16},{28,20},{1,9},{5... | collective-permute-start | bytes 1966088 | tf_op jit(solution)/shard_map/ppermute | solution.py:716
  220.7 18.1 %collective-permute-start.26 = (bf16[128,2560]{1,0:T(8,128)(2,1)S(1)}, bf16[128,2560]{1,0:T(8,128)(2,1)S(1)}, u32[]{:S(2)}, u32[]{:S(2)}) collective-permute-start(bf16[128,2560]{1,0:T(8,128)(2,1)S(1)} %get-tuple-element.417), channel_id=1, source_target_pairs={{0,16},{4,20},{8,24},{12,28},{16,0},{20,4},{24,8},{28,12},{1,17},{... | collective-permute-start | bytes 1966088 | tf_op jit(solution)/shard_map/ppermute | solution.py:716
  246.0 24.0 %collective-permute-start.28 = (bf16[1024,2048]{1,0:T(8,128)(2,1)}, bf16[1024,2048]{1,0:T(8,128)(2,1)S(1)}, u32[]{:S(2)}, u32[]{:S(2)}) collective-permute-start(bf16[1024,2048]{1,0:T(8,128)(2,1)} %up_away.1), channel_id=1, source_target_pairs={{0,4},{4,0},{8,12},{12,8},{16,20},{20,16},{24,28},{28,24},{1,5},{5... | collective-permute-start | bytes 12582920 | tf_op jit(solution)/shard_map/ppermute | solution.py:716
  246.0 35.3 %collective-permute-start.32 = (bf16[1024,1536]{1,0:T(8,128)(2,1)}, bf16[1024,1536]{1,0:T(8,128)(2,1)S(1)}, u32[]{:S(2)}, u32[]{:S(2)}) collective-permute-start(bf16[1024,1536]{1,0:T(8,128)(2,1)} %qkv_away.1), channel_id=1, source_target_pairs={{0,4},{4,0},{8,12},{12,8},{16,20},{20,16},{24,28},{28,24},{1,5},{5... | collective-permute-start | bytes 9437192 | tf_op jit(solution)/shard_map/ppermute | solution.py:716
  246.5 30.9 %collective-permute-start.29 = (bf16[256,2560]{1,0:T(8,128)(2,1)}, bf16[256,2560]{1,0:T(8,128)(2,1)S(1)}, u32[]{:S(2)}, u32[]{:S(2)}) collective-permute-start(bf16[256,2560]{1,0:T(8,128)(2,1)} %get-tuple-element.470), channel_id=1, source_target_pairs={{0,8},{4,12},{8,0},{12,4},{16,24},{20,28},{24,16},{28,20},{1,9},{5... | collective-permute-start | bytes 3932168 | tf_op jit(solution)/shard_map/ppermute | solution.py:716
  248.1 30.7 %collective-permute-start.30 = (bf16[256,2560]{1,0:T(8,128)(2,1)}, bf16[256,2560]{1,0:T(8,128)(2,1)}, u32[]{:S(2)}, u32[]{:S(2)}) collective-permute-start(bf16[256,2560]{1,0:T(8,128)(2,1)} %get-tuple-element.471), channel_id=1, source_target_pairs={{0,16},{4,20},{8,24},{12,28},{16,0},{20,4},{24,8},{28,12},{1,17},{... | collective-permute-start | bytes 3932168 | tf_op jit(solution)/shard_map/ppermute | solution.py:716
  248.9 27.3 %collective-permute-start.27 = (bf16[256,2048]{1,0:T(8,128)(2,1)S(1)}, bf16[256,2048]{1,0:T(8,128)(2,1)S(1)}, u32[]{:S(2)}, u32[]{:S(2)}) collective-permute-start(bf16[256,2048]{1,0:T(8,128)(2,1)S(1)} %add_convert_fusion.2), channel_id=1, source_target_pairs={{0,1},{1,2},{2,3},{3,0},{4,5},{5,6},{6,7},{7,4},{8,9},{9,10},{10,1... | collective-permute-start | bytes 3145736 | tf_op jit(solution)/shard_map/ppermute | solution.py:846
  278.9 26.3 %collective-permute-start.31 = (bf16[256,2048]{1,0:T(8,128)(2,1)S(1)}, bf16[256,2048]{1,0:T(8,128)(2,1)S(1)}, u32[]{:S(2)}, u32[]{:S(2)}) collective-permute-start(bf16[256,2048]{1,0:T(8,128)(2,1)S(1)} %slice.76), channel_id=1, source_target_pairs={{0,1},{1,2},{2,3},{3,0},{4,5},{5,6},{6,7},{7,4},{8,9},{9,10},{10,1... | collective-permute-start | bytes 3145736 | tf_op jit(solution)/shard_map/ppermute | solution.py:846
  281.3 22.2 %collective-permute-start.33 = (bf16[128,2048]{1,0:T(8,128)(2,1)S(1)}, bf16[128,2048]{1,0:T(8,128)(2,1)S(1)}, u32[]{:S(2)}, u32[]{:S(2)}) collective-permute-start(bf16[128,2048]{1,0:T(8,128)(2,1)S(1)} %get-tuple-element.496), channel_id=1, source_target_pairs={{0,8},{4,12},{8,0},{12,4},{16,24},{20,28},{24,16},{28,20},{1,9},{5... | collective-permute-start | bytes 1572872 | tf_op jit(solution)/shard_map/ppermute | solution.py:716
  282.6 21.0 %collective-permute-start.34 = (bf16[128,2048]{1,0:T(8,128)(2,1)S(1)}, bf16[128,2048]{1,0:T(8,128)(2,1)S(1)}, u32[]{:S(2)}, u32[]{:S(2)}) collective-permute-start(bf16[128,2048]{1,0:T(8,128)(2,1)S(1)} %get-tuple-element.497), channel_id=1, source_target_pairs={{0,16},{4,20},{8,24},{12,28},{16,0},{20,4},{24,8},{28,12},{1,17},{... | collective-permute-start | bytes 1572872 | tf_op jit(solution)/shard_map/ppermute | solution.py:716
  289.1 13.2 %collective-permute-start.35 = (bf16[128,1536]{1,0:T(8,128)(2,1)S(1)}, bf16[128,1536]{1,0:T(8,128)(2,1)S(1)}, u32[]{:S(2)}, u32[]{:S(2)}) collective-permute-start(bf16[128,1536]{1,0:T(8,128)(2,1)S(1)} %get-tuple-element.500), channel_id=1, source_target_pairs={{0,8},{4,12},{8,0},{12,4},{16,24},{20,28},{24,16},{28,20},{1,9},{5... | collective-permute-start | bytes 1179656 | tf_op jit(solution)/shard_map/ppermute | solution.py:716
  290.0 13.6 %collective-permute-start.36 = (bf16[128,1536]{1,0:T(8,128)(2,1)S(1)}, bf16[128,1536]{1,0:T(8,128)(2,1)S(1)}, u32[]{:S(2)}, u32[]{:S(2)}) collective-permute-start(bf16[128,1536]{1,0:T(8,128)(2,1)S(1)} %get-tuple-element.501), channel_id=1, source_target_pairs={{0,16},{4,20},{8,24},{12,28},{16,0},{20,4},{24,8},{28,12},{1,17},{... | collective-permute-start | bytes 1179656 | tf_op jit(solution)/shard_map/ppermute | solution.py:716
  305.5 23.3 %collective-permute-start.38 = (bf16[256,2048]{1,0:T(8,128)(2,1)S(1)}, bf16[256,2048]{1,0:T(8,128)(2,1)S(1)}, u32[]{:S(2)}, u32[]{:S(2)}) collective-permute-start(bf16[256,2048]{1,0:T(8,128)(2,1)S(1)} %get-tuple-element.515), channel_id=1, source_target_pairs={{0,8},{4,12},{8,0},{12,4},{16,24},{20,28},{24,16},{28,20},{1,9},{5... | collective-permute-start | bytes 3145736 | tf_op jit(solution)/shard_map/ppermute | solution.py:716
  307.1 23.1 %collective-permute-start.39 = (bf16[256,2048]{1,0:T(8,128)(2,1)S(1)}, bf16[256,2048]{1,0:T(8,128)(2,1)S(1)}, u32[]{:S(2)}, u32[]{:S(2)}) collective-permute-start(bf16[256,2048]{1,0:T(8,128)(2,1)S(1)} %get-tuple-element.516), channel_id=1, source_target_pairs={{0,16},{4,20},{8,24},{12,28},{16,0},{20,4},{24,8},{28,12},{1,17},{... | collective-permute-start | bytes 3145736 | tf_op jit(solution)/shard_map/ppermute | solution.py:716
  307.9 24.7 %collective-permute-start.37 = (bf16[256,2048]{1,0:T(8,128)(2,1)S(1)}, bf16[256,2048]{1,0:T(8,128)(2,1)S(1)}, u32[]{:S(2)}, u32[]{:S(2)}) collective-permute-start(bf16[256,2048]{1,0:T(8,128)(2,1)S(1)} %add_convert_fusion.1), channel_id=1, source_target_pairs={{0,1},{1,2},{2,3},{3,0},{4,5},{5,6},{6,7},{7,4},{8,9},{9,10},{10,1... | collective-permute-start | bytes 3145736 | tf_op jit(solution)/shard_map/ppermute | solution.py:846
  333.0 23.8 %collective-permute-start.40 = (bf16[256,2048]{1,0:T(8,128)(2,1)S(1)}, bf16[256,2048]{1,0:T(8,128)(2,1)S(1)}, u32[]{:S(2)}, u32[]{:S(2)}) collective-permute-start(bf16[256,2048]{1,0:T(8,128)(2,1)S(1)} %add_convert_fusion), channel_id=1, source_target_pairs={{0,1},{1,2},{2,3},{3,0},{4,5},{5,6},{6,7},{7,4},{8,9},{9,10},{10,1... | collective-permute-start | bytes 3145736 | tf_op jit(solution)/shard_map/ppermute | solution.py:846
  333.3 16.4 %collective-permute-start.41 = (bf16[256,1536]{1,0:T(8,128)(2,1)S(1)}, bf16[256,1536]{1,0:T(8,128)(2,1)S(1)}, u32[]{:S(2)}, u32[]{:S(2)}) collective-permute-start(bf16[256,1536]{1,0:T(8,128)(2,1)S(1)} %get-tuple-element.524), channel_id=1, source_target_pairs={{0,8},{4,12},{8,0},{12,4},{16,24},{20,28},{24,16},{28,20},{1,9},{5... | collective-permute-start | bytes 2359304 | tf_op jit(solution)/shard_map/ppermute | solution.py:716
  334.2 16.0 %collective-permute-start.42 = (bf16[256,1536]{1,0:T(8,128)(2,1)S(1)}, bf16[256,1536]{1,0:T(8,128)(2,1)S(1)}, u32[]{:S(2)}, u32[]{:S(2)}) collective-permute-start(bf16[256,1536]{1,0:T(8,128)(2,1)S(1)} %get-tuple-element.525), channel_id=1, source_target_pairs={{0,16},{4,20},{8,24},{12,28},{16,0},{20,4},{24,8},{28,12},{1,17},{... | collective-permute-start | bytes 2359304 | tf_op jit(solution)/shard_map/ppermute | solution.py:716
  357.9 7.1 %collective-permute-start.43 = (f32[2,2048]{1,0:T(2,128)S(1)}, f32[2,2048]{1,0:T(2,128)S(1)}, u32[]{:S(2)}, u32[]{:S(2)}) collective-permute-start(f32[2,2048]{1,0:T(2,128)S(1)} %norm_sums.1), channel_id=1, source_target_pairs={{0,1},{1,2},{2,3},{3,0},{4,5},{5,6},{6,7},{7,4},{8,9},{9,10},{10,1... | collective-permute-start | bytes 49160 | tf_op jit(solution)/shard_map/ppermute | solution.py:846
  358.0 7.0 %collective-permute-start.44 = (f32[2,2048]{1,0:T(2,128)S(1)}, f32[2,2048]{1,0:T(2,128)S(1)}, u32[]{:S(2)}, u32[]{:S(2)}) collective-permute-start(f32[2,2048]{1,0:T(2,128)S(1)} %norm_sums.1), channel_id=1, source_target_pairs={{0,2},{1,3},{2,0},{3,1},{4,6},{5,7},{6,4},{7,5},{8,10},{9,11},{10,... | collective-permute-start | bytes 49160 | tf_op jit(solution)/shard_map/ppermute | solution.py:846
  359.4 5.7 %collective-permute-start.45 = (f32[2,2048]{1,0:T(2,128)S(1)}, f32[2,2048]{1,0:T(2,128)S(1)}, u32[]{:S(2)}, u32[]{:S(2)}) collective-permute-start(f32[2,2048]{1,0:T(2,128)S(1)} %norm_sums.1), channel_id=1, source_target_pairs={{0,3},{1,0},{2,1},{3,2},{4,7},{5,4},{6,5},{7,6},{8,11},{9,8},{10,9... | collective-permute-start | bytes 49160 | tf_op jit(solution)/shard_map/ppermute | solution.py:846
  366.3 3.6 collective-permute-start.47
  368.2 4.5 %collective-permute-start.49 = (f32[2,256]{1,0:T(2,128)S(1)}, f32[2,256]{1,0:T(2,128)S(1)}, u32[]{:S(2)}, u32[]{:S(2)}) collective-permute-start(f32[2,256]{1,0:T(2,128)S(1)} %get-tuple-element.543), channel_id=1, source_target_pairs={{0,24},{4,28},{8,16},{12,20},{16,8},{20,12},{24,0},{28,4},{1,25},{... | collective-permute-start | bytes 6152 | tf_op jit(solution)/shard_map/ppermute | solution.py:716
  (51 other events, 495.2 us)
